TPU v7x, 32 devices: a whole 2x2x4 slice. The times are simulated.
32 devices in a mesh: fsdp: 8 (over y, x, core), ctx: 4 (over z).
Axes of the slice: x: 2, y: 2, z: 4, core: 2. Of those that a mesh axis runs over, the one named last changes fastest.
Arguments:
- tokens: bfloat16 [8, 512, 2048], P('fsdp', 'ctx'), may hold values from -6 to 6
- doc_starts: int32 [8, 4], P('fsdp'), may hold values from 0 to 511, as said below
- expert_ids: int32 [8, 512, 8], P('fsdp', 'ctx'), may hold values from 0 to 63, all different within a row; in each aligned block of 128 rows (0 to 127, 128 to 255, ..., all dimensions but the last counted through in order) at most 24 rows name the same one
- w_query: bfloat16 [2048, 2048], P(('fsdp', 'ctx')), may hold values from -0.125 to 0.125
- w_key: bfloat16 [2048, 2048], P(('fsdp', 'ctx')), may hold values from -0.125 to 0.125
- w_value: bfloat16 [2048, 2048], P(('fsdp', 'ctx')), may hold values from -0.125 to 0.125
- w_attn_out: bfloat16 [2048, 2048], P(('fsdp', 'ctx')), may hold values from -1 to 1
- w_router: bfloat16 [2048, 64], P(('fsdp', 'ctx')), may hold values from -0.0625 to 0.0625
- g_attn: bfloat16 [2048], P(('fsdp', 'ctx')), may hold values from 0.099609375 to 1.8984375
- g_query: bfloat16 [2048], P(('fsdp', 'ctx')), may hold values from 0.099609375 to 1.8984375
- g_key: bfloat16 [2048], P(('fsdp', 'ctx')), may hold values from 0.099609375 to 1.8984375
- g_ffn: bfloat16 [2048], P(('fsdp', 'ctx')), may hold values from 0.099609375 to 1.8984375
- w_in: bfloat16 [128, 2048, 1024], P(('fsdp', 'ctx')), may hold values from -0.125 to 0.125
- w_out: bfloat16 [128, 512, 2048], P(('fsdp', 'ctx')), may hold values from -6 to 6
- cotangent: bfloat16 [8, 512, 2048], P('fsdp', 'ctx'), may hold values from -6 to 6
Outputs:
- output: bfloat16 [8, 512, 2048], P('fsdp', 'ctx')
- input_grad: float32 [8, 512, 2048], P('fsdp', 'ctx')
- grad_query: float32 [2048, 2048], P(('fsdp', 'ctx'))
- grad_key: float32 [2048, 2048], P(('fsdp', 'ctx'))
- grad_value: float32 [2048, 2048], P(('fsdp', 'ctx'))
- grad_attn_out: float32 [2048, 2048], P(('fsdp', 'ctx'))
- grad_router: float32 [2048, 64], P(('fsdp', 'ctx'))
- grad_g_attn: float32 [2048], P(('fsdp', 'ctx'))
- grad_g_query: float32 [2048], P(('fsdp', 'ctx'))
- grad_g_key: float32 [2048], P(('fsdp', 'ctx'))
- grad_g_ffn: float32 [2048], P(('fsdp', 'ctx'))
- grad_w_in: float32 [128, 2048, 1024], P(('fsdp', 'ctx'))
- grad_w_out: float32 [128, 512, 2048], P(('fsdp', 'ctx'))
Inputs may be any that keep to these rules, and one draw needn't show every extreme that they name: `doc_starts`: each row rises strictly from 0. `expert_ids`: each row names 8 different experts; within the rows of one device (aligned blocks of 128 positions) no expert is named more than 24 times.
All inputs are finite; a program needn't handle non-finite values.
Results may differ from a plain program's by a relative error of at most 0.03.
Values may be sent and summed in bfloat16 or wider, within the bound.
No kernel may reach another device: no remote copies, remote signals or barrier semaphores. Data moves between devices by JAX's collectives and lax.ppermute only.
A program may use at most 384 MiB of HBM per device.

v0:
```python
import math

import jax
import jax.numpy as jnp
from jax import lax
from jax.sharding import PartitionSpec as P

H = 16
HD = 128
E = 64
TOP = 8
FH = 512
CAP = 24


epsilon = 1e-05
masked_score = -1e30
rope_base = 10000.0
highest_prec = lax.Precision.HIGHEST


def rms_scale(values, gain_vec):
    inv_rms = lax.rsqrt(jnp.mean(values * values, axis=-1, keepdims=True) + epsilon)
    return values * inv_rms * gain_vec


def rotary_tables(positions, head_dim):
    half_dim = head_dim // 2
    frequency = rope_base ** (-(jnp.arange(half_dim, dtype=jnp.float32) * 2.0 / head_dim))
    angles = positions.astype(jnp.float32)[:, None] * frequency[None, :]
    return (jnp.cos(angles), jnp.sin(angles))


def rotate(values, cosine, sine_tab, head_count):
    row_count = values.shape[0]
    shaped = values.reshape(row_count, head_count, -1)
    half_dim = shaped.shape[-1] // 2
    first_half = shaped[..., :half_dim]
    second_half = shaped[..., half_dim:]
    cos_heads = cosine[:, None, :]
    sin_heads = sine_tab[:, None, :]
    turned = jnp.concatenate(
        [
            first_half * cos_heads - second_half * sin_heads,
            second_half * cos_heads + first_half * sin_heads,
        ],
        axis=-1,
    )
    return turned.reshape(row_count, -1)


def doc_index(positions, starts):
    return jnp.sum((starts[None, :] <= positions[:, None]).astype(jnp.int32), axis=1) - 1


def gated(gate_part, up_part):
    return jax.nn.silu(gate_part) * up_part


def shards(
    tokens,
    doc_starts,
    expert_ids,
    w_query,
    w_key,
    w_value,
    w_attn_out,
    w_router,
    g_attn,
    g_query,
    g_key,
    g_ffn,
    w_in,
    w_out,
    cotangent,
):
    x_rows = tokens[0]
    tok_count = x_rows.shape[0]
    model_dim = x_rows.shape[1]
    seq_len = tok_count * lax.axis_size("ctx")
    positions = lax.axis_index("ctx") * tok_count + jnp.arange(tok_count, dtype=jnp.int32)
    starts_row = doc_starts[0]
    stream_ids = expert_ids[0]
    dense_fwd = (
        lax.all_gather(w_query, ("fsdp", "ctx"), axis=0, tiled=True),
        lax.all_gather(w_key, ("fsdp", "ctx"), axis=0, tiled=True),
        lax.all_gather(w_value, ("fsdp", "ctx"), axis=0, tiled=True),
        lax.all_gather(w_attn_out, ("fsdp", "ctx"), axis=0, tiled=True),
        lax.all_gather(w_router, ("fsdp", "ctx"), axis=0, tiled=True),
        lax.all_gather(g_attn, ("fsdp", "ctx"), axis=0, tiled=True),
        lax.all_gather(g_query, ("fsdp", "ctx"), axis=0, tiled=True),
        lax.all_gather(g_key, ("fsdp", "ctx"), axis=0, tiled=True),
        lax.all_gather(g_ffn, ("fsdp", "ctx"), axis=0, tiled=True),
    )
    query_all, key_all, value_all, attn_out_all, router_all = dense_fwd[:5]
    gain_attn = dense_fwd[5].astype(jnp.float32)
    gain_query = dense_fwd[6].astype(jnp.float32)
    gain_key = dense_fwd[7].astype(jnp.float32)
    gain_ffn = dense_fwd[8].astype(jnp.float32)
    x_float = x_rows.astype(jnp.float32)
    normed_float, attn_norm_pull = jax.vjp(rms_scale, x_float, gain_attn)
    normed = normed_float.astype(jnp.bfloat16)
    query_raw = jnp.dot(normed, query_all, preferred_element_type=jnp.float32)
    key_raw = jnp.dot(normed, key_all, preferred_element_type=jnp.float32)
    value_rows = jnp.dot(normed, value_all, preferred_element_type=jnp.float32).astype(jnp.bfloat16)
    cosine, sine_tab = rotary_tables(positions, HD)

    def head_path(raw_rows, gain_vec):
        return rotate(rms_scale(raw_rows, gain_vec), cosine, sine_tab, H)

    queries_float, query_pull = jax.vjp(head_path, query_raw, gain_query)
    keys_float, key_pull = jax.vjp(head_path, key_raw, gain_key)
    queries = queries_float.astype(jnp.bfloat16)
    keys_local = keys_float.astype(jnp.bfloat16)
    keys_seen, values_seen = (
        lax.all_gather(keys_local, "ctx", axis=0, tiled=True),
        lax.all_gather(value_rows, "ctx", axis=0, tiled=True),
    )
    scale_factor = 1.0 / math.sqrt(HD)
    query_heads = queries.reshape(tok_count, H, HD)
    query_docs = doc_index(positions, starts_row)
    key_block = min(seq_len, 512)
    block_total = seq_len // key_block
    block_positions = jnp.arange(seq_len, dtype=jnp.int32).reshape(block_total, key_block)

    def split_blocks(rows_in):
        return rows_in.reshape(block_total, key_block, H, HD)

    def block_scores(key_blk, block_pos):
        raw_scores = (
            jnp.einsum("qhd,khd->hqk", query_heads, key_blk, preferred_element_type=jnp.float32)
            * scale_factor
        )
        allowed = (block_pos[None, :] <= positions[:, None]) & (
            doc_index(block_pos, starts_row)[None, :] == query_docs[:, None]
        )
        return jnp.where(allowed[None], raw_scores, masked_score)

    def stat_step(stats, block_in):
        row_max, row_sum = stats
        key_blk, block_pos = block_in
        scores = block_scores(key_blk, block_pos)
        new_max = jnp.maximum(row_max, jnp.max(scores, axis=-1))
        new_sum = row_sum * jnp.exp(row_max - new_max) + jnp.sum(
            jnp.exp(scores - new_max[..., None]), axis=-1
        )
        return ((new_max, new_sum), None)

    start_stats = (
        jnp.full((H, tok_count), masked_score, jnp.float32),
        jnp.zeros((H, tok_count), jnp.float32),
    )
    (row_max, row_sum), unused = lax.scan(
        stat_step, start_stats, (split_blocks(keys_seen), block_positions)
    )

    def block_probs(key_blk, block_pos):
        return jnp.exp(block_scores(key_blk, block_pos) - row_max[..., None]) / row_sum[..., None]

    def mix_step(running, block_in):
        key_blk, value_blk, block_pos = block_in
        weights = block_probs(key_blk, block_pos).astype(jnp.bfloat16)
        return (
            running
            + jnp.einsum("hqk,khd->qhd", weights, value_blk, preferred_element_type=jnp.float32),
            None,
        )

    mixed_float, unused = lax.scan(
        mix_step,
        jnp.zeros((tok_count, H, HD), jnp.float32),
        (split_blocks(keys_seen), split_blocks(values_seen), block_positions),
    )
    mixed_low = mixed_float.reshape(tok_count, model_dim).astype(jnp.bfloat16)
    hidden = x_float + jnp.dot(mixed_low, attn_out_all, preferred_element_type=jnp.float32)
    moe_float, moe_norm_pull = jax.vjp(rms_scale, hidden, gain_ffn)
    moe_in = moe_float.astype(jnp.bfloat16)
    logits = jnp.dot(moe_in, router_all, preferred_element_type=jnp.float32)
    router_probs = jax.nn.softmax(logits, axis=-1)
    choose = (stream_ids[..., None] == jnp.arange(E, dtype=jnp.int32)[None, None, :]).astype(
        jnp.float32
    )
    gate_values = jnp.einsum("tke,te->tk", choose, router_probs, precision=highest_prec)
    flat_ids = stream_ids.reshape(-1)
    onehot = (flat_ids[:, None] == jnp.arange(E, dtype=jnp.int32)[None, :]).astype(jnp.int32)
    slot_rank = jnp.sum(jnp.cumsum(onehot, axis=0) * onehot, axis=1) - 1
    slot_tokens = jnp.arange(tok_count * TOP, dtype=jnp.int32) // TOP
    slot_table = jnp.zeros((E, CAP), jnp.int32).at[flat_ids, slot_rank].set(slot_tokens)
    send_rows = jnp.take(moe_in, slot_table.reshape(-1), axis=0).reshape(E, 1, CAP, model_dim)
    outgoing = jnp.broadcast_to(send_rows, (E, 2, CAP, model_dim)).reshape(2 * E, CAP, model_dim)
    arrived = lax.all_to_all(outgoing, ("fsdp", "ctx"), split_axis=0, concat_axis=1, tiled=True)
    projected = jnp.einsum("prd,pdf->prf", arrived, w_in, preferred_element_type=jnp.float32)
    inner_act = gated(projected[..., :FH], projected[..., FH:]).astype(jnp.bfloat16)
    piece_out = jnp.einsum(
        "prf,pfd->prd", inner_act, w_out, preferred_element_type=jnp.float32
    ).astype(jnp.bfloat16)
    returned = lax.all_to_all(piece_out, ("fsdp", "ctx"), split_axis=1, concat_axis=0, tiled=True)
    combined = jnp.sum(returned.reshape(E, 2, CAP, model_dim).astype(jnp.float32), axis=1)
    slot_values = combined[flat_ids, slot_rank].reshape(tok_count, TOP, model_dim)
    output = (hidden + jnp.sum(gate_values[..., None] * slot_values, axis=1)).astype(jnp.bfloat16)
    upstream = cotangent[0].astype(jnp.float32)
    dgates = jnp.einsum("tkd,td->tk", slot_values, upstream, precision=highest_prec)
    dpiece_slots = (
        (gate_values[..., None] * upstream[:, None, :])
        .astype(jnp.bfloat16)
        .reshape(tok_count * TOP, model_dim)
    )
    dpiece_table = (
        jnp.zeros((E, CAP, model_dim), jnp.bfloat16).at[flat_ids, slot_rank].set(dpiece_slots)
    )
    dpiece_send = jnp.broadcast_to(dpiece_table[:, None], (E, 2, CAP, model_dim)).reshape(
        2 * E, CAP, model_dim
    )
    dpiece_in = lax.all_to_all(
        dpiece_send, ("fsdp", "ctx"), split_axis=0, concat_axis=1, tiled=True
    )
    dinner = jnp.einsum("prd,pfd->prf", dpiece_in, w_out, preferred_element_type=jnp.float32)
    grad_w_out = jnp.einsum(
        "prf,prd->pfd", inner_act, dpiece_in, preferred_element_type=jnp.float32
    )
    unused, gate_pull = jax.vjp(gated, projected[..., :FH], projected[..., FH:])
    dgate_part, dup_part = gate_pull(dinner)
    dprojected = jnp.concatenate([dgate_part, dup_part], axis=-1).astype(jnp.bfloat16)
    grad_w_in = jnp.einsum("prd,prf->pdf", arrived, dprojected, preferred_element_type=jnp.float32)
    dslot_in = jnp.einsum(
        "prf,pdf->prd", dprojected, w_in, preferred_element_type=jnp.float32
    ).astype(jnp.bfloat16)
    dslot_back = lax.all_to_all(dslot_in, ("fsdp", "ctx"), split_axis=1, concat_axis=0, tiled=True)
    dslot_sum = jnp.sum(dslot_back.reshape(E, 2, CAP, model_dim).astype(jnp.float32), axis=1)
    dmoe_in = jnp.sum(dslot_sum[flat_ids, slot_rank].reshape(tok_count, TOP, model_dim), axis=1)
    dprob_router = jnp.einsum("tke,tk->te", choose, dgates, precision=highest_prec)
    dlogits = router_probs * (
        dprob_router - jnp.sum(router_probs * dprob_router, axis=-1, keepdims=True)
    )
    grad_router = jnp.einsum(
        "td,te->de", moe_in.astype(jnp.float32), dlogits, precision=highest_prec
    )
    dmoe_in = dmoe_in + jnp.einsum(
        "te,de->td", dlogits, router_all.astype(jnp.float32), precision=highest_prec
    )
    dhidden_norm, grad_ffn_gain = moe_norm_pull(dmoe_in)
    dhidden = upstream + dhidden_norm
    dhidden_low = dhidden.astype(jnp.bfloat16)
    query_back, key_back, value_back, attn_out_back = (
        lax.all_gather(w_query, ("fsdp", "ctx"), axis=0, tiled=True),
        lax.all_gather(w_key, ("fsdp", "ctx"), axis=0, tiled=True),
        lax.all_gather(w_value, ("fsdp", "ctx"), axis=0, tiled=True),
        lax.all_gather(w_attn_out, ("fsdp", "ctx"), axis=0, tiled=True),
    )
    grad_attn_out = jnp.einsum(
        "td,te->de", mixed_low, dhidden_low, preferred_element_type=jnp.float32
    )
    dmixed = jnp.einsum(
        "te,de->td", dhidden_low, attn_out_back, preferred_element_type=jnp.float32
    ).astype(jnp.bfloat16)
    dmixed_heads = dmixed.reshape(tok_count, H, HD)
    keys_back, values_back = (
        lax.all_gather(keys_local, "ctx", axis=0, tiled=True),
        lax.all_gather(value_rows, "ctx", axis=0, tiled=True),
    )
    back_blocks = (split_blocks(keys_back), split_blocks(values_back), block_positions)

    def block_grads(key_blk, value_blk, block_pos):
        prob_block = block_probs(key_blk, block_pos)
        dprobs = jnp.einsum(
            "qhd,khd->hqk", dmixed_heads, value_blk, preferred_element_type=jnp.float32
        )
        return (prob_block, dprobs)

    def delta_step(running, block_in):
        key_blk, value_blk, block_pos = block_in
        prob_block, dprobs = block_grads(key_blk, value_blk, block_pos)
        return (running + jnp.sum(prob_block * dprobs, axis=-1), None)

    row_delta, unused = lax.scan(delta_step, jnp.zeros((H, tok_count), jnp.float32), back_blocks)

    def grad_step(dquery_total, block_in):
        key_blk, value_blk, block_pos = block_in
        prob_block, dprobs = block_grads(key_blk, value_blk, block_pos)
        dscores = (prob_block * (dprobs - row_delta[..., None])).astype(jnp.bfloat16)
        dquery_total = dquery_total + jnp.einsum(
            "hqk,khd->qhd", dscores, key_blk, preferred_element_type=jnp.float32
        )
        dkey_blk = (
            jnp.einsum("hqk,qhd->khd", dscores, query_heads, preferred_element_type=jnp.float32)
            * scale_factor
        )
        dvalue_blk = jnp.einsum(
            "hqk,qhd->khd",
            prob_block.astype(jnp.bfloat16),
            dmixed_heads,
            preferred_element_type=jnp.float32,
        )
        return (dquery_total, (dkey_blk, dvalue_blk))

    dquery_heads, (dkey_blocks, dvalue_blocks) = lax.scan(
        grad_step, jnp.zeros((tok_count, H, HD), jnp.float32), back_blocks
    )
    dkey_term = dkey_blocks.reshape(seq_len, model_dim)
    dvalue_term = dvalue_blocks.reshape(seq_len, model_dim)
    dkey_local, dvalue = (
        lax.psum_scatter(
            dkey_term.astype(jnp.bfloat16), "ctx", scatter_dimension=0, tiled=True
        ).astype(jnp.float32),
        lax.psum_scatter(
            dvalue_term.astype(jnp.bfloat16), "ctx", scatter_dimension=0, tiled=True
        ).astype(jnp.float32),
    )
    dquery_raw, grad_query_gain = query_pull(
        dquery_heads.reshape(tok_count, model_dim) * scale_factor
    )
    dkey_raw, grad_key_gain = key_pull(dkey_local)
    dquery_low = dquery_raw.astype(jnp.bfloat16)
    dkey_low = dkey_raw.astype(jnp.bfloat16)
    dvalue_low = dvalue.astype(jnp.bfloat16)
    grad_query = jnp.einsum("td,te->de", normed, dquery_low, preferred_element_type=jnp.float32)
    grad_key = jnp.einsum("td,te->de", normed, dkey_low, preferred_element_type=jnp.float32)
    grad_value = jnp.einsum("td,te->de", normed, dvalue_low, preferred_element_type=jnp.float32)
    dnormed = jnp.einsum("te,de->td", dquery_low, query_back, preferred_element_type=jnp.float32)
    dnormed = dnormed + jnp.einsum(
        "te,de->td", dkey_low, key_back, preferred_element_type=jnp.float32
    )
    dnormed = dnormed + jnp.einsum(
        "te,de->td", dvalue_low, value_back, preferred_element_type=jnp.float32
    )
    dx_norm, grad_attn_gain = attn_norm_pull(dnormed)
    input_grad = (dhidden + dx_norm)[None]
    dense_grads = (
        lax.psum_scatter(grad_query, ("fsdp", "ctx"), scatter_dimension=0, tiled=True),
        lax.psum_scatter(grad_key, ("fsdp", "ctx"), scatter_dimension=0, tiled=True),
        lax.psum_scatter(grad_value, ("fsdp", "ctx"), scatter_dimension=0, tiled=True),
        lax.psum_scatter(grad_attn_out, ("fsdp", "ctx"), scatter_dimension=0, tiled=True),
        lax.psum_scatter(grad_router, ("fsdp", "ctx"), scatter_dimension=0, tiled=True),
        lax.psum_scatter(grad_attn_gain, ("fsdp", "ctx"), scatter_dimension=0, tiled=True),
        lax.psum_scatter(grad_query_gain, ("fsdp", "ctx"), scatter_dimension=0, tiled=True),
        lax.psum_scatter(grad_key_gain, ("fsdp", "ctx"), scatter_dimension=0, tiled=True),
        lax.psum_scatter(grad_ffn_gain, ("fsdp", "ctx"), scatter_dimension=0, tiled=True),
    )
    return (
        output[None],
        input_grad,
        dense_grads[0],
        dense_grads[1],
        dense_grads[2],
        dense_grads[3],
        dense_grads[4],
        dense_grads[5],
        dense_grads[6],
        dense_grads[7],
        dense_grads[8],
        grad_w_in,
        grad_w_out,
    )


def solution(mesh):
    return jax.shard_map(
        shards,
        mesh=mesh,
        in_specs=(
            P("fsdp", "ctx", None),
            P("fsdp", None),
            P("fsdp", "ctx", None),
            P(("fsdp", "ctx"), None),
            P(("fsdp", "ctx"), None),
            P(("fsdp", "ctx"), None),
            P(("fsdp", "ctx"), None),
            P(("fsdp", "ctx"), None),
            P(("fsdp", "ctx")),
            P(("fsdp", "ctx")),
            P(("fsdp", "ctx")),
            P(("fsdp", "ctx")),
            P(("fsdp", "ctx"), None, None),
            P(("fsdp", "ctx"), None, None),
            P("fsdp", "ctx", None),
        ),
        out_specs=(
            P("fsdp", "ctx", None),
            P("fsdp", "ctx", None),
            P(("fsdp", "ctx"), None),
            P(("fsdp", "ctx"), None),
            P(("fsdp", "ctx"), None),
            P(("fsdp", "ctx"), None),
            P(("fsdp", "ctx"), None),
            P(("fsdp", "ctx")),
            P(("fsdp", "ctx")),
            P(("fsdp", "ctx")),
            P(("fsdp", "ctx")),
            P(("fsdp", "ctx"), None, None),
            P(("fsdp", "ctx"), None, None),
        ),
        check_vma=False,
    )
```

profile of v0, /device:TPU:0, one launch (start us, length us, event | category | flops | bytes accessed | tf_op | source)
XLA Modules:
  0.0 3548.3 jit_solution(734649239627095168)
XLA Ops:
  12.9 42.6 %all-reduce.13 = (bf16[2048]{0:T(1024)(128)(2,1)S(1)}, bf16[2048]{0:T(1024)(128)(2,1)S(1)}, bf16[2048]{0:T(1024)(128)(2,1)S(1)}, bf16[2048]{0:T(1024)(128)(2,1)S(1)}) all-reduce(bf16[2048]{0:T(1024)(128)(2,1)S(1)} %dynamic-update-slice, bf16[2048]{0:T(1024)(128)(2,1)S(1)} %dynamic-update-slice.2, ...), channel_id=1, replica_groups=mesh['fsdp'=8,'ctx'=4] {'fsdp','ctx'}, use_global_device_ids=true, to_apply=%add.4 | all-reduce | flops 8192 | bytes 32768
  57.7 33.8 all-gather.11.cloned.1.call-done
  97.9 72.6 %all-gather.13.cloned.1.call-done = bf16[2048,2048]{1,0:T(8,128)(2,1)} async-done(((bf16[64,2048]{1,0:T(8,128)(2,1)}), bf16[2048,2048]{1,0:T(8,128)(2,1)}) %all-gather.13.cloned.1.call-update) | async-done | bytes 8388624 | tf_op jit(solution)/shard_map/all_gather | solution.py:86
  180.2 69.3 %all-gather.7.cloned.1.call-done = bf16[2048,2048]{1,0:T(8,128)(2,1)} async-done(((bf16[64,2048]{1,0:T(8,128)(2,1)}), bf16[2048,2048]{1,0:T(8,128)(2,1)}) %all-gather.7.cloned.1.call-update) | async-done | bytes 8388624 | tf_op jit(solution)/shard_map/all_gather | solution.py:87
  256.0 18.0 reduce-window.6
  280.7 15.6 all-gather.15.cloned.1.call-done
  302.3 40.2 %all-gather.9.cloned.1.call-done = bf16[512,2048]{1,0:T(8,128)(2,1)} async-done(((bf16[128,2048]{1,0:T(8,128)(2,1)}), bf16[512,2048]{1,0:T(8,128)(2,1)}) %all-gather.9.cloned.1.call-update) | async-done | bytes 2097168 | tf_op jit(solution)/shard_map/all_gather | solution.py:117
  347.1 74.2 %all-gather.17.cloned.1.call-done = bf16[2048,2048]{1,0:T(8,128)(2,1)} async-done(((bf16[64,2048]{1,0:T(8,128)(2,1)}), bf16[2048,2048]{1,0:T(8,128)(2,1)}) %all-gather.17.cloned.1.call-update) | async-done | bytes 8388624 | tf_op jit(solution)/shard_map/all_gather | solution.py:88
  447.1 341.4 %all_gather.49 = bf16[2048,64]{1,0:T(8,128)(2,1)S(1)} all-gather(bf16[64,64]{1,0:T(8,128)(2,1)S(1)} %copy-done.62), channel_id=1, replica_groups=mesh['fsdp'=8,'ctx'=4] {'fsdp','ctx'}, dimensions={0}, use_global_device_ids=true | all-gather | bytes 270336 | tf_op jit(solution)/shard_map/all_gather | solution.py:89
  790.7 10.7 scatter_custom_fusion.1
  801.4 8.5 broadcast_in_dim.193
  813.9 10.7 copy.161
  824.7 260.2 %all-to-all-done.2 = bf16[128,24,2048]{2,1,0:T(8,128)(2,1)} async-done(((bf16[128,24,2048]{2,1,0:T(8,128)(2,1)}), bf16[128,24,2048]{2,1,0:T(8,128)(2,1)}, u32[]{:S(2)}, u32[]{:S(2)}) %all-to-all-start.2) | async-done | bytes 12582944 | tf_op jit(solution)/shard_map/all_to_all | solution.py:214
  1084.8 11.4 copy.165
  1097.8 19.5 fusion.101
  1117.2 16.5 fusion.6
  1133.8 20.7 convolution_convert_fusion
  1154.5 17.3 copy.168
  1171.8 11.4 all-to-all-start.3
  1183.2 10.3 convolution_convert_fusion.1
  1193.4 30.3 copy.162
  1223.7 230.3 %all-to-all-done.3 = bf16[4,768,2048]{2,0,1:T(4,128)(2,1)} async-done(((bf16[4,768,2048]{2,0,1:T(4,128)(2,1)}), bf16[4,768,2048]{2,0,1:T(4,128)(2,1)}, u32[]{:S(2)}, u32[]{:S(2)}) %all-to-all-start.3) | async-done | bytes 12582944 | tf_op jit(solution)/shard_map/all_to_all | solution.py:228
  1454.1 11.3 all-to-all-start.1
  1465.5 12.1 copy.169
  1481.0 8.7 copy.170
  1489.8 15.2 reduce_sum.237
  1504.9 25.6 gather_fusion.2
  1535.9 200.5 %all-to-all-done.1 = bf16[4,768,2048]{2,0,1:T(4,128)(2,1)} async-done(((bf16[4,768,2048]{2,0,1:T(4,128)(2,1)}), bf16[4,768,2048]{2,0,1:T(4,128)(2,1)}, u32[]{:S(2)}, u32[]{:S(2)}) %all-to-all-start.1) | async-done | bytes 12582944 | tf_op jit(solution)/shard_map/all_to_all | solution.py:197
  1736.3 14.5 copy.163
  1758.2 8.7 copy.164
  1766.9 15.2 reduce_sum.232
  1782.1 25.7 gather_fusion.1
  1807.8 7.6 fusion.3
  1815.5 8.4 fusion.29
  1859.8 9.3 fusion.51
  1872.9 26.5 reduce-scatter.22.cloned.1.call-done
  1910.2 8.2 fusion.88
  1924.2 8.2 fusion.86
  1932.6 12.4 reduce-scatter.24.cloned.1.call-done
  1945.0 9.2 fusion.84
  1954.3 15.5 fusion.103
  1969.8 24.4 fusion.12
  2010.4 40.1 %all-reduce.12 = (f32[2048]{0:T(1024)S(1)}, f32[2048]{0:T(1024)S(1)}, f32[2048]{0:T(1024)S(1)}, f32[2048]{0:T(1024)S(1)}) all-reduce(f32[2048]{0:T(1024)S(1)} %get-tuple-element.130, f32[2048]{0:T(1024)S(1)} %get-tuple-element.128, f32[2048]{0:T(1024)S(1)} %get-tuple-element.114, ...), channel_id=9, replica_groups=mesh['fsdp'=8,'ctx'=4] {'fsdp','ctx'}, use_global_device_ids=true, to_apply=%region_33.34.clone | all-reduce | flops 8192 | bytes 65536
  2054.2 28.5 reduce-scatter.20.cloned.1.call-done
  2082.7 363.5 %reduce-scatter.18.cloned.1.call-done = f32[64,2048]{1,0:T(8,128)} async-done(((f32[2048,2048]{1,0:T(8,128)}), f32[64,2048]{1,0:T(8,128)}) %reduce-scatter.18.cloned.1.call-update) | async-done | bytes 524304 | tf_op jit(solution)/shard_map/reduce_scatter | solution.py:332
  2446.2 365.2 %reduce-scatter.12.cloned.1.call-done = f32[64,2048]{1,0:T(8,128)} async-done(((f32[2048,2048]{1,0:T(8,128)}), f32[64,2048]{1,0:T(8,128)}) %reduce-scatter.12.cloned.1.call-update) | async-done | bytes 524304 | tf_op jit(solution)/shard_map/reduce_scatter | solution.py:329
  2811.3 365.0 %reduce-scatter.14.cloned.1.call-done = f32[64,2048]{1,0:T(8,128)} async-done(((f32[2048,2048]{1,0:T(8,128)}), f32[64,2048]{1,0:T(8,128)}) %reduce-scatter.14.cloned.1.call-update) | async-done | bytes 524304 | tf_op jit(solution)/shard_map/reduce_scatter | solution.py:330
  3176.4 365.2 %reduce-scatter.16.cloned.1.call-done = f32[64,2048]{1,0:T(8,128)} async-done(((f32[2048,2048]{1,0:T(8,128)}), f32[64,2048]{1,0:T(8,128)}) %reduce-scatter.16.cloned.1.call-update) | async-done | bytes 524304 | tf_op jit(solution)/shard_map/reduce_scatter | solution.py:331
  (327 shorter events, 172.5 us)
Async XLA Ops:
  7.2 84.4 %all-gather.11.cloned.1.call-start = ((), (), s32[]{:S(2)}) async-start(), calls=%async_computation.13 | async-start | bytes 8650752 | tf_op jit(solution)/shard_map/all_gather | solution.py:85
  7.9 162.6 %all-gather.13.cloned.1.call-start = ((), (), s32[]{:S(2)}) async-start(), calls=%async_computation.14 | async-start | bytes 8650752 | tf_op jit(solution)/shard_map/all_gather | solution.py:86
  8.7 240.8 %all-gather.7.cloned.1.call-start = ((), (), s32[]{:S(2)}) async-start(), calls=%async_computation.11 | async-start | bytes 8650752 | tf_op jit(solution)/shard_map/all_gather | solution.py:87
  9.4 286.9 %all-gather.15.cloned.1.call-start = ((), (), s32[]{:S(2)}) async-start(), calls=%async_computation.15 | async-start | bytes 2621440 | tf_op jit(solution)/shard_map/all_gather | solution.py:116
  55.5 193.9 %copy-start.31 = (f32[2048]{0:T(1024)}, f32[2048]{0:T(1024)S(1)}, u32[]{:S(2)}) copy-start(f32[2048]{0:T(1024)S(1)} %convert_element_type.163) | copy-start | bytes 24580
  55.5 41.0 %copy-start.48 = (f32[2048]{0:T(1024)}, f32[2048]{0:T(1024)S(1)}, u32[]{:S(2)}) copy-start(f32[2048]{0:T(1024)S(1)} %convert_element_type.168) | copy-start | bytes 24580
  55.5 119.8 %copy-start.46 = (f32[2048]{0:T(1024)}, f32[2048]{0:T(1024)S(1)}, u32[]{:S(2)}) copy-start(f32[2048]{0:T(1024)S(1)} %convert_element_type.170) | copy-start | bytes 24580
  57.4 192.1 %copy-start.52 = (f32[128]{0:T(128)}, f32[128]{0:T(128)S(1)}, u32[]{:S(2)}) copy-start(f32[128]{0:T(128)S(1)} %fusion.72) | copy-start | bytes 1540
  57.7 119.6 %copy-start.38 = (f32[128,64]{1,0:T(8,128)}, f32[128,64]{1,0:T(8,128)S(1)}, u32[]{:S(2)}) copy-start(f32[128,64]{1,0:T(8,128)S(1)} %get-tuple-element.202) | copy-start | bytes 98308
  57.7 119.6 %copy-start.40 = (f32[128,64]{1,0:T(8,128)}, f32[128,64]{1,0:T(8,128)S(1)}, u32[]{:S(2)}) copy-start(f32[128,64]{1,0:T(8,128)S(1)} %get-tuple-element.203) | copy-start | bytes 98308
  57.7 112.8 %copy-start.3 = (bf16[1,128,2048]{2,1,0:T(8,128)(2,1)S(1)}, bf16[1,128,2048]{2,1,0:T(8,128)(2,1)}, u32[]{:S(2)}) copy-start(bf16[1,128,2048]{2,1,0:T(8,128)(2,1)} %param.15) | copy-start | bytes 1572868
  96.5 78.7 %copy-start.68 = (f32[128]{0:T(128)}, f32[128]{0:T(128)S(1)}, u32[]{:S(2)}) copy-start(f32[128]{0:T(128)S(1)} %fusion.73) | copy-start | bytes 1540
  178.7 117.6 %copy-start.21 = (bf16[128,16,64]{2,0,1:T(8,128)(2,1)}, bf16[128,16,64]{2,0,1:T(8,128)(2,1)S(1)}, u32[]{:S(2)}) copy-start(bf16[128,16,64]{2,0,1:T(8,128)(2,1)S(1)} %get-tuple-element.164) | copy-start | bytes 786436
  178.7 117.6 %copy-start.23 = (bf16[128,16,64]{2,0,1:T(8,128)(2,1)}, bf16[128,16,64]{2,0,1:T(8,128)(2,1)S(1)}, u32[]{:S(2)}) copy-start(bf16[128,16,64]{2,0,1:T(8,128)(2,1)S(1)} %get-tuple-element.165) | copy-start | bytes 786436
  180.1 75.5 %copy-start.63 = (s32[1,128,8]{1,2,0:T(8,128)S(1)}, s32[1,128,8]{1,2,0:T(8,128)}, u32[]{:S(2)}) copy-start(s32[1,128,8]{1,2,0:T(8,128)} %param.17) | copy-start | bytes 12292
  180.1 95.1 %copy-start.83 = (s32[2]{0:T(128)S(1)}, s32[2]{0:T(128)}, u32[]{:S(2)}) copy-start(s32[2]{0:T(128)} %constant.175) | copy-start | bytes 28
  180.1 95.2 %copy-start.81 = (s32[2]{0:T(128)S(1)}, s32[2]{0:T(128)}, u32[]{:S(2)}) copy-start(s32[2]{0:T(128)} %constant.178) | copy-start | bytes 28
  180.1 95.2 %copy-start.82 = (s32[2]{0:T(128)S(1)}, s32[2]{0:T(128)}, u32[]{:S(2)}) copy-start(s32[2]{0:T(128)} %constant.172) | copy-start | bytes 28
  180.1 100.3 %copy-start.80 = (s32[1,4]{1,0:T(1,128)S(1)}, s32[1,4]{1,0:T(1,128)}, u32[]{:S(2)}) copy-start(s32[1,4]{1,0:T(1,128)} %param.16) | copy-start | bytes 52
  180.1 162.4 %all-gather.9.cloned.1.call-start = ((), (), s32[]{:S(2)}) async-start(), calls=%async_computation.12 | async-start | bytes 2621440 | tf_op jit(solution)/shard_map/all_gather | solution.py:117
  254.9 166.4 %all-gather.17.cloned.1.call-start = ((), (), s32[]{:S(2)}) async-start(), calls=%async_computation.16 | async-start | bytes 8650752 | tf_op jit(solution)/shard_map/all_gather | solution.py:88
  255.9 170.2 %copy-start.50 = (f32[2048]{0:T(1024)}, f32[2048]{0:T(1024)S(1)}, u32[]{:S(2)}) copy-start(f32[2048]{0:T(1024)S(1)} %convert_element_type.176) | copy-start | bytes 24580
  280.7 66.3 %copy-start.36 = (pred[128,512]{1,0:T(8,128)(4,1)}, pred[128,512]{1,0:T(8,128)(4,1)S(1)}, u32[]{:S(2)}) copy-start(pred[128,512]{1,0:T(8,128)(4,1)S(1)} %fusion.56) | copy-start | bytes 196612
  299.0 48.1 %copy-start.54 = (f32[16,128]{1,0:T(8,128)}, f32[16,128]{1,0:T(8,128)S(1)}, u32[]{:S(2)}) copy-start(f32[16,128]{1,0:T(8,128)S(1)} %broadcast_maximum_fusion) | copy-start | bytes 24580
  302.3 44.8 %copy-start.58 = (f32[16,128]{1,0:T(8,128)}, f32[16,128]{1,0:T(8,128)S(1)}, u32[]{:S(2)}) copy-start(f32[16,128]{1,0:T(8,128)S(1)} %multiply_add_fusion.4) | copy-start | bytes 24580
  347.1 79.0 %copy-start.29 = (bf16[16,128,128]{2,1,0:T(8,128)(2,1)}, bf16[16,128,128]{2,1,0:T(8,128)(2,1)S(1)}, u32[]{:S(2)}) copy-start(bf16[16,128,128]{2,1,0:T(8,128)(2,1)S(1)} %fusion.24) | copy-start | bytes 1572868
  427.2 361.4 %copy-start = (bf16[128,2048]{1,0:T(8,128)(2,1)}, bf16[128,2048]{1,0:T(8,128)(2,1)S(1)}, u32[]{:S(2)}) copy-start(bf16[128,2048]{1,0:T(8,128)(2,1)S(1)} %multiply_convert_fusion.4) | copy-start | bytes 1572868
  443.1 345.4 %copy-start.19 = (bf16[1,128,2048]{2,1,0:T(8,128)(2,1)S(1)}, bf16[1,128,2048]{2,1,0:T(8,128)(2,1)}, u32[]{:S(2)}) copy-start(bf16[1,128,2048]{2,1,0:T(8,128)(2,1)} %param.29) | copy-start | bytes 1572868
  443.1 358.3 %all-to-all-start = ((bf16[128,24,2048]{2,1,0:T(8,128)(2,1)}), bf16[128,24,2048]{2,1,0:T(8,128)(2,1)}, u32[]{:S(2)}, u32[]{:S(2)}) async-start(bf16[128,24,2048]{2,1,0:T(8,128)(2,1)} %bitcast.216), calls=%async_computation | async-start | bytes 25165824 | tf_op jit(solution)/shard_map/all_to_all | solution.py:191
  447.1 362.8 %copy-start.56 = (s32[128,8]{1,0:T(8,128)}, s32[128,8]{1,0:T(8,128)S(1)}, u32[]{:S(2)}) copy-start(s32[128,8]{1,0:T(8,128)S(1)} %copy.153) | copy-start | bytes 12292
  789.3 20.6 copy-start.34
  809.9 274.9 %all-to-all-start.2 = ((bf16[128,24,2048]{2,1,0:T(8,128)(2,1)}), bf16[128,24,2048]{2,1,0:T(8,128)(2,1)}, u32[]{:S(2)}, u32[]{:S(2)}) async-start(bf16[128,24,2048]{2,1,0:T(8,128)(2,1)} %bitcast.217), calls=%async_computation.2 | async-start | bytes 25165824 | tf_op jit(solution)/shard_map/all_to_all | solution.py:214
  1133.8 49.4 %copy-start.84 = (bf16[4,768,512]{2,1,0:T(8,128)(2,1)}, bf16[4,768,512]{2,1,0:T(8,128)(2,1)S(1)}, u32[]{:S(2)}) copy-start(bf16[4,768,512]{2,1,0:T(8,128)(2,1)S(1)} %get-tuple-element.161) | copy-start | bytes 9437188
  1171.8 282.3 %all-to-all-start.3 = ((bf16[4,768,2048]{2,0,1:T(4,128)(2,1)}), bf16[4,768,2048]{2,0,1:T(4,128)(2,1)}, u32[]{:S(2)}, u32[]{:S(2)}) async-start(bf16[4,768,2048]{2,0,1:T(4,128)(2,1)} %copy.168), calls=%async_computation.3 | async-start | bytes 25165824 | tf_op jit(solution)/shard_map/all_to_all | solution.py:228
  1454.1 282.3 %all-to-all-start.1 = ((bf16[4,768,2048]{2,0,1:T(4,128)(2,1)}), bf16[4,768,2048]{2,0,1:T(4,128)(2,1)}, u32[]{:S(2)}, u32[]{:S(2)}) async-start(bf16[4,768,2048]{2,0,1:T(4,128)(2,1)} %copy.162), calls=%async_computation.1 | async-start | bytes 25165824 | tf_op jit(solution)/shard_map/all_to_all | solution.py:197
  1465.4 434.0 %reduce-scatter.22.cloned.1.call-start = ((), (), s32[]{:S(2)}) async-start(), calls=%async_computation.22 | async-start | bytes 2621440
  1782.1 25.8 copy-start.45
  1848.8 96.2 %reduce-scatter.24.cloned.1.call-start = ((), (), s32[]{:S(2)}) async-start(), calls=%async_computation.23 | async-start | bytes 2621440
  1858.0 224.7 %reduce-scatter.20.cloned.1.call-start = ((), (), s32[]{:S(2)}) async-start(), calls=%async_computation.21 | async-start | bytes 1081344 | tf_op jit(solution)/shard_map/reduce_scatter | solution.py:333
  1859.7 586.4 %reduce-scatter.18.cloned.1.call-start = ((), (), s32[]{:S(2)}) async-start(), calls=%async_computation.20 | async-start | bytes 17301504 | tf_op jit(solution)/shard_map/reduce_scatter | solution.py:332
  1869.2 36.3 %copy-start.39 = (f32[128,64]{1,0:T(8,128)S(1)}, f32[128,64]{1,0:T(8,128)}, u32[]{:S(2)}) copy-start(f32[128,64]{1,0:T(8,128)} %copy-done.38) | copy-start | bytes 98308
  1869.2 36.3 %copy-start.41 = (f32[128,64]{1,0:T(8,128)S(1)}, f32[128,64]{1,0:T(8,128)}, u32[]{:S(2)}) copy-start(f32[128,64]{1,0:T(8,128)} %copy-done.40) | copy-start | bytes 98308
  1869.2 942.2 %reduce-scatter.12.cloned.1.call-start = ((), (), s32[]{:S(2)}) async-start(), calls=%async_computation.17 | async-start | bytes 17301504 | tf_op jit(solution)/shard_map/reduce_scatter | solution.py:329
  1872.9 32.5 copy-start.17
  1918.4 1257.9 %reduce-scatter.14.cloned.1.call-start = ((), (), s32[]{:S(2)}) async-start(), calls=%async_computation.18 | async-start | bytes 17301504 | tf_op jit(solution)/shard_map/reduce_scatter | solution.py:330
  1932.4 1609.1 %reduce-scatter.16.cloned.1.call-start = ((), (), s32[]{:S(2)}) async-start(), calls=%async_computation.19 | async-start | bytes 17301504 | tf_op jit(solution)/shard_map/reduce_scatter | solution.py:331
  2007.3 45.6 %copy-start.75 = (f32[128]{0:T(128)S(1)}, f32[128]{0:T(128)}, u32[]{:S(2)}) copy-start(f32[128]{0:T(128)} %copy-done.74) | copy-start | bytes 1540
  2007.3 45.6 %copy-start.11 = (f32[128,2048]{1,0:T(8,128)S(1)}, f32[128,2048]{1,0:T(8,128)}, u32[]{:S(2)}) copy-start(f32[128,2048]{1,0:T(8,128)} %copy-done.10) | copy-start | bytes 3145732
  (58 other events, 348.7 us)
Sparse Core Ops, SparseCore 0:
  10.9 80.5 all-gather.10
  94.5 75.9 all-gather.12
  173.4 75.9 all-gather.6
  251.4 44.8 all-gather.14
  298.3 44.1 all-gather.8
  345.3 76.0 all-gather.16
  1848.9 50.4 reduce-scatter.21
  1901.8 43.1 reduce-scatter.23
  1947.8 134.7 reduce-scatter.19
  2085.5 360.6 reduce-scatter.17
  2449.1 362.1 reduce-scatter.11
  2814.2 362.1 reduce-scatter.13
  3179.3 362.1 reduce-scatter.15
where the time goes:
time: 3560 us; the launch traced here: 3550 us
  waiting for transfers between devices  2530 us (71%)
  blocking collectives  424 us (12%)
  local copies, waits for them, and re-layouts  225 us (6%)
  matrix products  220 us (6%)
  other arithmetic  106 us (3%)
    reduce_scatter x1, waiting for transfers between devices, shards(): lax.psum_scatter(grad_value, ('fsdp', 'ctx'), scatter_dimension=0, tiled=...  365 us
    reduce_scatter x1, waiting for transfers between devices, shards(): lax.psum_scatter(grad_query, ('fsdp', 'ctx'), scatter_dimension=0, tiled=...  365 us
    reduce_scatter x1, waiting for transfers between devices, shards(): lax.psum_scatter(grad_key, ('fsdp', 'ctx'), scatter_dimension=0, tiled=True)  365 us
    reduce_scatter x1, waiting for transfers between devices, shards(): lax.psum_scatter(grad_attn_out, ('fsdp', 'ctx'), scatter_dimension=0, til...  363 us
    all_gather x1, blocking collectives, shards(): lax.all_gather(w_router, ('fsdp', 'ctx'), axis=0, tiled=True)  341 us
    all_to_all x1, waiting for transfers between devices, shards(): lax.all_to_all(dpiece_send, ('fsdp', 'ctx'), split_axis=0, concat_axis=1,...  260 us
    all_to_all x1, waiting for transfers between devices, shards(): lax.all_to_all(dslot_in, ('fsdp', 'ctx'), split_axis=1, concat_axis=0, ti...  230 us
    all_to_all x1, waiting for transfers between devices, shards(): lax.all_to_all(piece_out, ('fsdp', 'ctx'), split_axis=1, concat_axis=0, t...  200 us
  transfers between devices with their start and end apart: 17, of which 16 were waited for; matrix products, arithmetic and copies ran while one was open for 9% of the time, Pallas kernels for 0%

commit v1 on v0

v1 whole, which is shorter than its diff:
```python
import math

import jax
import jax.numpy as jnp
from jax import lax
from jax.sharding import PartitionSpec as P

H = 16
HD = 128
E = 64
TOP = 8
FH = 512
CAP = 24

EPS = 1e-05
MASKED = -1e30
ROPE_BASE = 10000.0
HIGHEST = lax.Precision.HIGHEST
F32 = jnp.float32
BF = jnp.bfloat16
ALL = ("fsdp", "ctx")


def pick(stacked, index):
    return lax.dynamic_index_in_dim(stacked, index, 0, keepdims=False)


def add_low(a, b):
    return (a.astype(F32) + b.astype(F32)).astype(BF)


class Links:
    def __init__(self, fsdp_size, ctx_size):
        self.nf = fsdp_size
        self.nc = ctx_size
        self.native = fsdp_size == 8 and ctx_size == 4
        self.f = lax.axis_index("fsdp")
        self.c = lax.axis_index("ctx")

    def swap(self, value, mask):
        return lax.ppermute(value, "fsdp", [(i, i ^ mask) for i in range(self.nf)])

    def shift(self, value, step):
        n = self.nc
        return lax.ppermute(value, "ctx", [(i, (i + step) % n) for i in range(n)])

    def block_of(self, m):
        return self.f ^ m if self.native else jnp.int32(m)

    def gather_ctx(self, value):
        if not self.native:
            return lax.all_gather(value, "ctx", axis=0)
        up = down = value
        below, above = [], []
        last = self.nc - 1
        for k in range(last):
            up = lax.ppermute(up, "ctx", [(i, i + 1) for i in range(k, last)])
            down = lax.ppermute(down, "ctx", [(i + 1, i) for i in range(0, last - k)])
            below.append(up)
            above.append(down)
        line = jnp.stack(below[::-1] + [value] + above)
        return lax.dynamic_slice_in_dim(line, last - self.c, self.nc, 0)

    def sum_ctx(self, value):
        if not self.native:
            return lax.psum(value, "ctx")
        total = value
        for k in range(1, self.nc):
            total = total + self.shift(value, k)
        return total

    def scatter_ctx(self, value):
        if not self.native:
            return lax.psum_scatter(value, "ctx", scatter_dimension=0, tiled=False).astype(F32)
        total = pick(value, self.c).astype(F32)
        for k in range(1, self.nc):
            total = total + self.shift(pick(value, (self.c + k) % self.nc), k).astype(F32)
        return total

    def exchange_ctx(self, value):
        return lax.all_to_all(value, "ctx", split_axis=0, concat_axis=0, tiled=True)

    def gather_fsdp(self, value):
        if not self.native:
            whole = lax.all_gather(value, "fsdp", axis=0)
            return [[whole[m]] for m in range(self.nf)]
        half = value.shape[0] // 2
        from_x = self.swap(value, 2)
        from_y = self.swap(value, 4)
        other = self.swap(value, 1)
        diag_a = self.swap(from_y[:half], 2)
        diag_b = self.swap(from_x[half:], 4)
        other_x = self.swap(from_x, 1)
        other_y = self.swap(from_y, 1)
        other_a = self.swap(diag_a, 1)
        other_b = self.swap(diag_b, 1)

        def cut(rows):
            return [rows[:half], rows[half:]]

        return [
            cut(value),
            cut(other),
            cut(from_x),
            cut(other_x),
            cut(from_y),
            cut(other_y),
            [diag_a, diag_b],
            [other_a, other_b],
        ]

    def gather_fsdp_sorted(self, value):
        blocks = self.gather_fsdp(value)
        if not self.native:
            return jnp.concatenate([b[0] for b in blocks])
        stacked = jnp.concatenate([p for b in blocks for p in b]).reshape((self.nf,) + value.shape)
        return jnp.concatenate([pick(stacked, self.f ^ j) for j in range(self.nf)])

    def scatter_fsdp(self, parts):
        if not self.native:
            whole = jnp.stack(parts)
            return lax.psum_scatter(whole, "fsdp", scatter_dimension=0, tiled=False).astype(F32)
        near = [add_low(parts[m], self.swap(parts[m + 1], 1)) for m in (2, 4, 6)]
        own = parts[0].astype(F32) + self.swap(parts[1], 1).astype(F32)
        to_x, to_y, to_d = near
        half = own.shape[0] // 2
        xa = self.swap(to_x[:half], 2)
        xd = self.swap(to_d[:half], 2)
        yb = self.swap(to_y[half:], 4)
        yd = self.swap(to_d[half:], 4)
        ya = self.swap(add_low(to_y[:half], xd), 4)
        xb = self.swap(add_low(to_x[half:], yd), 2)
        top = own[:half] + xa.astype(F32) + ya.astype(F32)
        bottom = own[half:] + yb.astype(F32) + xb.astype(F32)
        return jnp.concatenate([top, bottom])


def rms_parts(values):
    return lax.rsqrt(jnp.mean(values * values, axis=-1, keepdims=True) + EPS)


def rms_back(values, inv, gain, grad):
    u = grad * gain
    mean = jnp.mean(u * values, axis=-1, keepdims=True)
    return inv * u - values * (inv * inv * inv) * mean, jnp.sum(grad * values * inv, axis=0)


def rotary_tables(positions):
    half = HD // 2
    frequency = ROPE_BASE ** (-(jnp.arange(half, dtype=F32) * 2.0 / HD))
    angles = positions.astype(F32)[:, None] * frequency[None, :]
    return jnp.cos(angles), jnp.sin(angles)


def rotate(values, cosine, sine):
    rows = values.shape[0]
    shaped = values.reshape(rows, -1, HD)
    a, b = shaped[..., : HD // 2], shaped[..., HD // 2 :]
    cos, sin = cosine[:, None, :], sine[:, None, :]
    return jnp.concatenate([a * cos - b * sin, b * cos + a * sin], axis=-1).reshape(rows, -1)


def doc_index(positions, starts):
    return jnp.sum((starts[None, :] <= positions[:, None]).astype(jnp.int32), axis=1) - 1


def dot(a, b):
    return jnp.dot(a, b, preferred_element_type=F32)


def dot_t(a, b):
    return jnp.einsum("td,ed->te", a, b, preferred_element_type=F32)


def t_dot(a, b):
    return jnp.einsum("td,te->de", a, b, preferred_element_type=F32)


def shards(
    tokens,
    doc_starts,
    expert_ids,
    w_query,
    w_key,
    w_value,
    w_attn_out,
    w_router,
    g_attn,
    g_query,
    g_key,
    g_ffn,
    w_in,
    w_out,
    cotangent,
):
    nf, nc = lax.axis_size("fsdp"), lax.axis_size("ctx")
    ndev = nf * nc
    links = Links(nf, nc)
    x_own = tokens[0]
    g_own = cotangent[0]
    tok, dim = x_own.shape
    seq = tok * nc
    width = dim // nc
    heads = H // nc
    own_rows = w_query.shape[0]
    fsdp_rows = own_rows * nc
    starts = doc_starts[0]

    small = jnp.concatenate(
        [
            w_router.reshape(-1),
            g_attn,
            g_query,
            g_key,
            g_ffn,
            expert_ids[0].T.reshape(-1).astype(BF),
        ]
    )
    small_len = small.shape[0]
    small_rows = -(-small_len // (16 * 128)) * 16
    small = jnp.pad(small, (0, small_rows * 128 - small_len)).reshape(1, small_rows, 128)
    small_all = lax.all_to_all(
        jnp.broadcast_to(small, (ndev, small_rows, 128)),
        ALL,
        split_axis=0,
        concat_axis=0,
        tiled=True,
    ).reshape(ndev, -1)
    router_len = own_rows * E
    router = small_all[:, :router_len].reshape(dim, E)
    gains = small_all[:, router_len : router_len + 4 * own_rows].reshape(ndev, 4, own_rows)
    gains = gains.transpose(1, 0, 2).reshape(4, dim).astype(F32)
    gain_attn, gain_query, gain_key, gain_ffn = gains
    ids_all = small_all[:, router_len + 4 * own_rows : small_len].astype(jnp.int32)
    ids_all = ids_all.reshape(nf, nc, TOP, tok)

    qkv_own = jnp.stack([w.reshape(own_rows, nc, width) for w in (w_query, w_key, w_value)], axis=2)
    qkv_own = qkv_own.transpose(1, 0, 2, 3).reshape(nc, own_rows, 3 * width)
    qkv_rows = links.exchange_ctx(qkv_own).reshape(fsdp_rows, 3 * width)
    w_qkv = links.gather_fsdp_sorted(qkv_rows)
    x_all = links.gather_ctx(x_own).reshape(seq, dim)
    w_o = links.gather_fsdp_sorted(links.gather_ctx(w_attn_out).reshape(fsdp_rows, dim))
    g_stream = links.gather_ctx(g_own).reshape(seq, dim)
    g_blocks = links.gather_fsdp(g_stream)

    x_float = x_all.astype(F32)
    normed = (x_float * rms_parts(x_float) * gain_attn).astype(BF)
    raw = dot(normed, w_qkv)
    query_raw, key_raw = raw[:, :width], raw[:, width : 2 * width]
    value = raw[:, 2 * width :].astype(BF)
    sums = jnp.stack([jnp.sum(query_raw * query_raw, -1), jnp.sum(key_raw * key_raw, -1)])
    sums = links.sum_ctx(sums)
    inv_query = lax.rsqrt(sums[0] / dim + EPS)[:, None]
    inv_key = lax.rsqrt(sums[1] / dim + EPS)[:, None]
    positions = jnp.arange(seq, dtype=jnp.int32)
    cosine, sine = rotary_tables(positions)
    gq = pick(gain_query.reshape(nc, width), links.c)
    gk = pick(gain_key.reshape(nc, width), links.c)
    queries = rotate(query_raw * inv_query * gq, cosine, sine).astype(BF).reshape(seq, heads, HD)
    keys = rotate(key_raw * inv_key * gk, cosine, sine).astype(BF).reshape(seq, heads, HD)
    values = value.reshape(seq, heads, HD)
    scale = 1.0 / math.sqrt(HD)
    docs = doc_index(positions, starts)
    allowed = (positions[None, :] <= positions[:, None]) & (docs[None, :] == docs[:, None])
    scores = jnp.einsum("qhd,khd->hqk", queries, keys, preferred_element_type=F32) * scale
    probs = jax.nn.softmax(jnp.where(allowed[None], scores, MASKED), axis=-1)
    probs_low = probs.astype(BF)
    mixed = jnp.einsum("hqk,khd->qhd", probs_low, values, preferred_element_type=F32)
    mixed = mixed.reshape(seq, width).astype(BF)
    mixed_all = links.gather_ctx(mixed).transpose(1, 0, 2).reshape(seq, dim)
    hidden = x_float + dot(mixed_all, w_o)
    inv_ffn = rms_parts(hidden)
    moe_in = (hidden * inv_ffn * gain_ffn).astype(BF)

    x_blocks = links.gather_fsdp(moe_in)
    pieces = w_in.shape[0]
    halves = min(2, pieces)
    experts = pieces // halves
    device = links.f * nc + links.c
    first_expert = device * pieces // 2
    mine = first_expert + jnp.arange(experts, dtype=jnp.int32)
    ids_rel = jnp.stack([pick(ids_all, links.block_of(m)) for m in range(nf)])
    named = jnp.any(ids_rel[:, :, None] == mine[:, None, None], axis=3)
    before = (jnp.arange(tok)[:, None] < jnp.arange(tok)[None, :]).astype(BF)
    rank = jnp.einsum("mcjt,ts->mcjs", named.astype(BF), before, preferred_element_type=F32)
    slots = (
        named[:, :, :, None] & (rank[:, :, :, None] == jnp.arange(CAP, dtype=F32)[:, None])
    ).astype(BF)

    def take_rows(blocks):
        taken = []
        for m in range(nf):
            at = 0
            for piece in blocks[m]:
                n = piece.shape[0] // tok
                taken.append(
                    jnp.einsum(
                        "cjrt,ctd->jcrd",
                        slots[m, at : at + n],
                        piece.reshape(n, tok, dim),
                        preferred_element_type=BF,
                    )
                )
                at += n
        return jnp.concatenate(taken, axis=1).reshape(experts, ndev * CAP, dim)

    def put_rows(rows):
        shaped = rows.reshape(experts, nf, nc, CAP, dim)
        return [
            jnp.einsum("cjrt,jcrd->ctd", slots[m], shaped[:, m], preferred_element_type=BF).reshape(
                seq, dim
            )
            for m in range(nf)
        ]

    g_rows = take_rows(g_blocks)
    w_out_e = w_out.reshape(experts, halves * FH, dim)
    dinner_raw = jnp.einsum("jrd,jfd->jrf", g_rows, w_out_e, preferred_element_type=F32)
    x_rows = take_rows(x_blocks)
    route = jnp.einsum("jrd,de->jre", x_rows, router, preferred_element_type=F32)
    route = jax.nn.softmax(route, axis=-1)
    chosen = mine[:, None, None] == jnp.arange(E, dtype=jnp.int32)
    gate = jnp.sum(jnp.where(chosen, route, 0.0), axis=-1)[..., None]
    nrow = x_rows.shape[1]
    x_pieces = jnp.broadcast_to(x_rows[:, None], (experts, halves, nrow, dim))
    x_pieces = x_pieces.reshape(pieces, nrow, dim)
    projected = jnp.einsum("prd,pdf->prf", x_pieces, w_in, preferred_element_type=F32)
    gate_part, up_part = projected[..., :FH], projected[..., FH:]
    sig = jax.nn.sigmoid(gate_part)
    inner_float = gate_part * sig * up_part
    inner = inner_float.astype(BF)
    dinner_p = dinner_raw.reshape(experts, nrow, halves, FH).transpose(0, 2, 1, 3)
    dinner_p = dinner_p.reshape(pieces, nrow, FH)
    dgate_rows = jnp.sum(
        jnp.sum(inner.astype(F32) * dinner_p, axis=-1).reshape(experts, halves, nrow), axis=1
    )
    gate_p = jnp.broadcast_to(gate[:, None], (experts, halves, nrow, 1)).reshape(pieces, nrow, 1)
    dinner = gate_p * dinner_p
    dprojected = jnp.concatenate(
        [
            dinner * up_part * sig * (1.0 + gate_part * (1.0 - sig)),
            dinner * gate_part * sig,
        ],
        axis=-1,
    ).astype(BF)
    dslot_p = jnp.einsum("prf,pdf->prd", dprojected, w_in, preferred_element_type=F32)
    dslot = jnp.sum(dslot_p.reshape(experts, halves, nrow, dim), axis=1).astype(BF)
    dmoe_stream = links.scatter_fsdp(put_rows(dslot)).astype(BF)
    dmoe = links.scatter_ctx(dmoe_stream.reshape(nc, tok, dim))

    dgate_blocks = dgate_rows.reshape(experts, nf, nc, CAP)
    dgate_tok = jnp.einsum(
        "mcjrt,jmcr->mcjt", slots.astype(F32), dgate_blocks, precision=HIGHEST
    )
    dgate_sorted = jnp.stack([pick(dgate_tok, links.block_of(j)) for j in range(nf)])
    dgate_back = lax.all_to_all(
        dgate_sorted.reshape(ndev, experts, tok), ALL, split_axis=0, concat_axis=0, tiled=True
    )
    dprob = jnp.sum(dgate_back.reshape(E, ndev * experts // E, tok), axis=1).T

    inner_e = inner.reshape(experts, halves, nrow, FH)
    inner_e = inner_e.transpose(0, 2, 1, 3).reshape(experts, nrow, halves * FH)
    combined = jnp.einsum("jrf,jfd->jrd", inner_e, w_out_e, preferred_element_type=F32)
    out_stream = links.scatter_fsdp(put_rows((gate * combined).astype(BF))).astype(BF)
    out_rows = links.scatter_ctx(out_stream.reshape(nc, tok, dim))
    hidden_own = pick(hidden.reshape(nc, tok, dim), links.c)
    output = (hidden_own + out_rows).astype(BF)

    gated_inner = (gate * inner_e.astype(F32)).astype(BF)
    grad_w_out = jnp.einsum("jrf,jrd->jfd", gated_inner, g_rows, preferred_element_type=F32)
    grad_w_out = grad_w_out.reshape(w_out.shape)
    grad_w_in = jnp.einsum("prd,prf->pdf", x_pieces, dprojected, preferred_element_type=F32)

    moe_own = pick(moe_in.reshape(nc, tok, dim), links.c)
    router_probs = jax.nn.softmax(dot(moe_own, router), axis=-1)
    dlogits = router_probs * (dprob - jnp.sum(router_probs * dprob, axis=-1, keepdims=True))
    grad_router = jnp.einsum("td,te->de", moe_own.astype(F32), dlogits, precision=HIGHEST)
    dmoe = dmoe + jnp.einsum("te,de->td", dlogits, router.astype(F32), precision=HIGHEST)
    inv_own = pick(inv_ffn.reshape(nc, tok, 1), links.c)
    dhidden, grad_gain_ffn = rms_back(hidden_own, inv_own, gain_ffn, dmoe)
    dhidden = g_own.astype(F32) + dhidden

    dhidden_all = links.gather_ctx(dhidden.astype(BF)).reshape(seq, dim)
    w_o_own = pick(w_o.reshape(nc, width, dim), links.c)
    dmixed = dot_t(dhidden_all, w_o_own).astype(BF).reshape(seq, heads, HD)
    dprobs = jnp.einsum("qhd,khd->hqk", dmixed, values, preferred_element_type=F32)
    delta = jnp.sum(probs * dprobs, axis=-1, keepdims=True)
    dscores = (probs * (dprobs - delta)).astype(BF)
    dqueries = jnp.einsum("hqk,khd->qhd", dscores, keys, preferred_element_type=F32) * scale
    dkeys = jnp.einsum("hqk,qhd->khd", dscores, queries, preferred_element_type=F32) * scale
    dvalue = jnp.einsum("hqk,qhd->khd", probs_low, dmixed, preferred_element_type=F32)
    dvalue_low = dvalue.reshape(seq, width).astype(BF)
    turned_query = rotate(dqueries.reshape(seq, width), cosine, -sine)
    turned_key = rotate(dkeys.reshape(seq, width), cosine, -sine)
    uq, uk = turned_query * gq, turned_key * gk
    back = jnp.stack([jnp.sum(uq * query_raw, -1), jnp.sum(uk * key_raw, -1)])
    back = links.sum_ctx(back) / dim
    dquery_low = (inv_query * uq - query_raw * inv_query**3 * back[0][:, None]).astype(BF)
    dkey_low = (inv_key * uk - key_raw * inv_key**3 * back[1][:, None]).astype(BF)
    grad_gain_query = jnp.sum(turned_query * query_raw * inv_query, axis=0)
    grad_gain_key = jnp.sum(turned_key * key_raw * inv_key, axis=0)
    dqkv = jnp.concatenate([dquery_low, dkey_low, dvalue_low], axis=1)
    dnormed = links.scatter_ctx(dot_t(dqkv, w_qkv).astype(BF).reshape(nc, tok, dim))
    x_own_float = x_own.astype(F32)
    dx, grad_gain_attn = rms_back(x_own_float, rms_parts(x_own_float), gain_attn, dnormed)
    input_grad = (dhidden + dx)[None]

    dhidden_cols = pick(dhidden_all.reshape(seq, nc, width).transpose(1, 0, 2), links.c)

    def reduce_columns(grad):
        blocks = grad.astype(BF).reshape(nf, fsdp_rows, grad.shape[1])
        summed = links.scatter_fsdp([pick(blocks, links.block_of(m)) for m in range(nf)])
        return links.exchange_ctx(summed.reshape(nc, own_rows, grad.shape[1]))

    grad_o = reduce_columns(t_dot(mixed_all, dhidden_cols))
    grad_attn_out = grad_o.transpose(1, 0, 2).reshape(own_rows, dim)
    grad_qkv = reduce_columns(t_dot(normed, dqkv))
    grad_qkv = grad_qkv.reshape(nc, own_rows, 3, width).transpose(2, 1, 0, 3)
    grad_qkv = grad_qkv.reshape(3, own_rows, dim)

    def placed(vector):
        return lax.dynamic_update_slice(
            jnp.zeros((dim,), F32), vector, (links.c * width,)
        )

    router_terms = jnp.concatenate(
        [grad_router.reshape(ndev, -1), grad_gain_ffn.reshape(ndev, -1)], axis=1
    )
    gain_terms = jnp.stack([grad_gain_attn, placed(grad_gain_query), placed(grad_gain_key)])
    gain_terms = gain_terms.reshape(3, ndev, own_rows).transpose(1, 0, 2).reshape(ndev, -1)

    def reduce_small(terms):
        count = terms.shape[1]
        rows = -(-count // 1024) * 8
        padded = jnp.pad(terms, ((0, 0), (0, rows * 128 - count))).reshape(ndev, rows, 128)
        moved = lax.all_to_all(padded, ALL, split_axis=0, concat_axis=0, tiled=True)
        return jnp.sum(moved, axis=0).reshape(-1)[:count]

    router_sum = reduce_small(router_terms)
    gain_sum = reduce_small(gain_terms).reshape(3, own_rows)
    return (
        output[None],
        input_grad,
        grad_qkv[0],
        grad_qkv[1],
        grad_qkv[2],
        grad_attn_out,
        router_sum[: own_rows * E].reshape(own_rows, E),
        gain_sum[0],
        gain_sum[1],
        gain_sum[2],
        router_sum[own_rows * E :],
        grad_w_in,
        grad_w_out,
    )


def solution(mesh):
    rows = P(ALL, None)
    vec = P(ALL)
    cube = P(ALL, None, None)
    stream = P("fsdp", "ctx", None)
    return jax.shard_map(
        shards,
        mesh=mesh,
        in_specs=(
            stream,
            P("fsdp", None),
            stream,
            rows,
            rows,
            rows,
            rows,
            rows,
            vec,
            vec,
            vec,
            vec,
            cube,
            cube,
            stream,
        ),
        out_specs=(
            stream,
            stream,
            rows,
            rows,
            rows,
            rows,
            rows,
            vec,
            vec,
            vec,
            vec,
            cube,
            cube,
        ),
        check_vma=False,
    )
```

time: 3560 us -> 1050 us (0.29)
  waiting for transfers between devices: 2530 us -> 418 us
  blocking collectives: 424 us -> 0 us
  starting transfers between devices: 31.7 us -> 189 us
  local copies, waits for them, and re-layouts: 225 us -> 160 us
    reduce_scatter x5 -> x0, waiting for transfers between devices: 1490 us -> none  [the longest x1 365 us: shards(): lax.psum_scatter(grad_value, ('fsdp', 'ctx'), scatter_dimension=0, tiled=...]
    all_to_all x4 -> x7, waiting for transfers between devices: 691 us -> 22.3 us  [the longest x3 12.2 us: exchange_ctx(): return lax.all_to_all(value, 'ctx', split_axis=0, concat_axis=0, tiled=True)]
    ppermute x0 -> x121, waiting for transfers between devices: none -> 396 us  [the longest x76 234 us: swap(): return lax.ppermute(value, 'fsdp', [(i, i ^ mask) for i in range(self.nf)])]
    all_gather x1 -> x0, blocking collectives: 341 us -> none  [shards(): lax.all_gather(w_router, ('fsdp', 'ctx'), axis=0, tiled=True)]
    all_gather x6 -> x0, waiting for transfers between devices: 306 us -> none  [the longest x1 74.2 us: shards(): lax.all_gather(w_attn_out, ('fsdp', 'ctx'), axis=0, tiled=True)]
    ppermute x0 -> x121, starting transfers between devices: none -> 143 us  [the longest x76 56.7 us: swap(): return lax.ppermute(value, 'fsdp', [(i, i ^ mask) for i in range(self.nf)])]
    unnamed x2 -> x0, blocking collectives: 82.8 us -> none
    convert_element_type x4 -> x2, local copies, waits for them, and re-layouts: 65.1 us -> 2.14 us  [the longest x1 2.05 us: shards(): dvalue_low = dvalue.reshape(seq, width).astype(BF)]
  transfers between devices with their start and end apart: 17 -> 128, of which waited for: 16 -> 43; matrix products, arithmetic and copies ran while one was open for 9% -> 33% of each run, Pallas kernels for 0% -> 0%
where the time goes in v1:
time: 1050 us; the launch traced here: 1040 us
  waiting for transfers between devices  418 us (40%)
  matrix products  192 us (18%)
  starting transfers between devices  189 us (18%)
  local copies, waits for them, and re-layouts  160 us (15%)
  other arithmetic  76.7 us (7%)
    ppermute x76, waiting for transfers between devices, swap(): return lax.ppermute(value, 'fsdp', [(i, i ^ mask) for i in range(self.nf)])  234 us
    ppermute x15, waiting for transfers between devices, shift(): return lax.ppermute(value, 'ctx', [(i, (i + step) % n) for i in range(n)])  79.8 us
    ppermute x15, waiting for transfers between devices, gather_ctx(): down = lax.ppermute(down, 'ctx', [(i + 1, i) for i in range(0, last - k)])  71.9 us
    unnamed x252, local copies, waits for them, and re-layouts  59.6 us
    ppermute x76, starting transfers between devices, swap(): return lax.ppermute(value, 'fsdp', [(i, i ^ mask) for i in range(self.nf)])  56.7 us
    ppermute x15, starting transfers between devices, gather_ctx(): up = lax.ppermute(up, 'ctx', [(i, i + 1) for i in range(k, last)])  34 us
    ppermute x15, starting transfers between devices, shift(): return lax.ppermute(value, 'ctx', [(i, (i + step) % n) for i in range(n)])  32.4 us
    dot_general x16, matrix products, put_rows(): jnp.einsum('cjrt,jcrd->ctd', slots[m], shaped[:, m], preferred_element_ty...  32.4 us
  transfers between devices with their start and end apart: 128, of which 43 were waited for; matrix products, arithmetic and copies ran while one was open for 33% of the time, Pallas kernels for 0%

profile of v1, /device:TPU:0, one launch (start us, length us, event | category | flops | bytes accessed | tf_op | source)
XLA Modules:
  0.0 1039.2 jit_solution(10158326104133675637)
XLA Ops:
  0.6 5.6 collective-permute-start.24
  8.9 6.0 collective-permute-start
  19.9 4.6 all-to-all-start
  43.4 7.5 all-to-all-start.1
  61.4 17.3 %collective-permute-done.64 = bf16[128,2048]{1,0:T(8,128)(2,1)} collective-permute-done((bf16[128,2048]{1,0:T(8,128)(2,1)S(1)}, bf16[128,2048]{1,0:T(8,128)(2,1)}, u32[]{:S(2)}, u32[]{:S(2)}) %collective-permute-start.64) | collective-permute-done | bytes 524320 | tf_op jit(solution)/shard_map/ppermute | solution.py:58
  96.8 9.9 collective-permute-done.65
  122.7 5.3 collective-permute-done.66
  143.5 26.8 %collective-permute-done.11 = bf16[128,1536]{1,0:T(8,128)(2,1)S(1)} collective-permute-done((bf16[128,1536]{1,0:T(8,128)(2,1)S(1)}, bf16[128,1536]{1,0:T(8,128)(2,1)S(1)}, u32[]{:S(2)}, u32[]{:S(2)}) %collective-permute-start.11) | collective-permute-done | bytes 393248 | tf_op jit(solution)/shard_map/ppermute | solution.py:41
  171.8 24.1 %collective-permute-done.12 = bf16[128,1536]{1,0:T(8,128)(2,1)S(1)} collective-permute-done((bf16[128,1536]{1,0:T(8,128)(2,1)S(1)}, bf16[128,1536]{1,0:T(8,128)(2,1)S(1)}, u32[]{:S(2)}, u32[]{:S(2)}) %collective-permute-start.12) | collective-permute-done | bytes 393248 | tf_op jit(solution)/shard_map/ppermute | solution.py:41
  202.4 9.9 collective-permute-start.16
  232.8 5.6 fusion.207
  277.7 12.1 %collective-permute-done.68 = bf16[512,2048]{1,0:T(8,128)(2,1)S(1)} collective-permute-done((bf16[512,2048]{1,0:T(8,128)(2,1)}, bf16[512,2048]{1,0:T(8,128)(2,1)S(1)}, u32[]{:S(2)}, u32[]{:S(2)}) %collective-permute-start.68) | collective-permute-done | bytes 2097184 | tf_op jit(solution)/shard_map/ppermute | solution.py:41
  295.1 14.0 %collective-permute-done.23 = bf16[512,512]{0,1:T(8,128)(2,1)S(1)} collective-permute-done((bf16[512,512]{0,1:T(8,128)(2,1)S(1)}, bf16[512,512]{0,1:T(8,128)(2,1)S(1)}, u32[]{:S(2)}, u32[]{:S(2)}) %collective-permute-start.23) | collective-permute-done | bytes 524320 | tf_op jit(solution)/shard_map/ppermute | solution.py:58
  309.3 8.0 multiply_reduce_fusion.2
  334.0 10.3 fusion.216
  348.4 16.3 %collective-permute-done.42 = bf16[512,2048]{1,0:T(8,128)(2,1)} collective-permute-done((bf16[512,2048]{1,0:T(8,128)(2,1)S(1)}, bf16[512,2048]{1,0:T(8,128)(2,1)}, u32[]{:S(2)}, u32[]{:S(2)}) %collective-permute-start.42) | collective-permute-done | bytes 2097184 | tf_op jit(solution)/shard_map/ppermute | solution.py:41
  375.4 15.2 %collective-permute-done.44 = bf16[256,2048]{1,0:T(8,128)(2,1)S(1)} collective-permute-done((bf16[256,2048]{1,0:T(8,128)(2,1)S(1)}, bf16[256,2048]{1,0:T(8,128)(2,1)S(1)}, u32[]{:S(2)}, u32[]{:S(2)}) %collective-permute-start.44) | collective-permute-done | bytes 1048608 | tf_op jit(solution)/shard_map/ppermute | solution.py:41
  390.6 5.8 collective-permute-done.45
  403.1 8.6 copy.274
  411.7 4.9 fusion.208
  416.7 9.1 broadcast_in_dim.40
  425.8 23.3 %fusion.215 = f32[4,768,1024]{2,1,0:T(8,128)} fusion(bf16[4,768,2048]{1,2,0:T(8,128)(2,1)} %bitcast.966, bf16[4,2048,1024]{2,1,0:T(8,128)(2,1)} %param.27), kind=kOutput, calls=%fused_computation.554 | convolution fusion | flops 12884901888 | bytes 41943040 | tf_op jit(solution)/shard_map/prd,pdf->prf/dot_general | solution.py:327
  449.0 10.5 %multiply_convert_fusion.3 = (bf16[4,768,512]{2,1,0:T(8,128)(2,1)}, bf16[4,768,512]{2,1,0:T(8,128)(2,1)}, f32[4,768]{1,0:T(4,128)S(1)}, bf16[4,768,512]{2,1,0:T(8,128)(2,1)S(1)}) fusion(f32[4,768,1024]{2,1,0:T(8,128)} %fusion.215, f32[4,768,512]{2,1,0:T(8,128)S(1)} %bitcast.960, f32[4,768]{1,0:T(4,128)S(1)} %broadcast_in_dim.43), kind=kLoop, calls=%fused_computation.11 | loop fusion | flops 31454208 | bytes 28336128 | tf_op jit(solution)/shard_map/convert.25
  470.9 10.9 %multiply_convert_fusion = bf16[2,768,2048]{2,1,0:T(8,128)(2,1)S(1)} fusion(f32[2,768]{1,0:T(2,128)S(1)} %fusion.208, bf16[2,768,1024]{1,2,0:T(8,128)(2,1)} %bitcast.1016, bf16[2,1024,2048]{2,1,0:T(8,128)(2,1)} %bitcast.1112), kind=kOutput, calls=%fused_computation.4 | convolution fusion | flops 6448742400 | bytes 17831936 | tf_op jit(solution)/shard_map/jrf,jfd->jrd/dot_general | solution.py:363
  499.2 21.6 %bitcast_reduce_fusion = bf16[2,768,2048]{2,1,0:T(8,128)(2,1)} fusion(bf16[4,2048,1024]{2,1,0:T(8,128)(2,1)} %param.27, bf16[4,768,512]{2,1,0:T(8,128)(2,1)} %get-tuple-element.38, bf16[4,768,512]{2,1,0:T(8,128)(2,1)} %get-tuple-element.37), kind=kOutput, calls=%fused_computation.3 | convolution fusion | flops 12900630528 | bytes 29360128 | tf_op jit(solution)/shard_map/prf,pdf->prd/dot_general | solution.py:346
  565.6 37.2 %collective-permute-done.84 = bf16[256,2048]{1,0:T(8,128)(2,1)S(1)} collective-permute-done((bf16[256,2048]{1,0:T(8,128)(2,1)S(1)}, bf16[256,2048]{1,0:T(8,128)(2,1)S(1)}, u32[]{:S(2)}, u32[]{:S(2)}) %collective-permute-start.84) | collective-permute-done | bytes 1048608 | tf_op jit(solution)/shard_map/ppermute | solution.py:41
  608.7 13.3 %collective-permute-done.78 = bf16[256,2048]{1,0:T(8,128)(2,1)S(1)} collective-permute-done((bf16[256,2048]{1,0:T(8,128)(2,1)S(1)}, bf16[256,2048]{1,0:T(8,128)(2,1)S(1)}, u32[]{:S(2)}, u32[]{:S(2)}) %collective-permute-start.78) | collective-permute-done | bytes 1048608 | tf_op jit(solution)/shard_map/ppermute | solution.py:41
  624.0 4.9 collective-permute-done.83
  629.5 15.0 %collective-permute-done.85 = bf16[256,2048]{1,0:T(8,128)(2,1)S(1)} collective-permute-done((bf16[256,2048]{1,0:T(8,128)(2,1)S(1)}, bf16[256,2048]{1,0:T(8,128)(2,1)S(1)}, u32[]{:S(2)}, u32[]{:S(2)}) %collective-permute-start.85) | collective-permute-done | bytes 1048608 | tf_op jit(solution)/shard_map/ppermute | solution.py:41
  646.4 4.9 collective-permute-done.82
  654.5 12.4 %collective-permute-done.50 = bf16[256,2048]{1,0:T(8,128)(2,1)S(1)} collective-permute-done((bf16[256,2048]{1,0:T(8,128)(2,1)S(1)}, bf16[256,2048]{1,0:T(8,128)(2,1)S(1)}, u32[]{:S(2)}, u32[]{:S(2)}) %collective-permute-start.50) | collective-permute-done | bytes 1048608 | tf_op jit(solution)/shard_map/ppermute | solution.py:41
  676.2 12.7 %collective-permute-done.57 = bf16[256,2048]{1,0:T(8,128)(2,1)S(1)} collective-permute-done((bf16[256,2048]{1,0:T(8,128)(2,1)S(1)}, bf16[256,2048]{1,0:T(8,128)(2,1)S(1)}, u32[]{:S(2)}, u32[]{:S(2)}) %collective-permute-start.57) | collective-permute-done | bytes 1048608 | tf_op jit(solution)/shard_map/ppermute | solution.py:41
  688.9 5.3 collective-permute-done.54
  700.3 16.7 %collective-permute-done.87 = bf16[128,2048]{1,0:T(8,128)(2,1)S(1)} collective-permute-done((bf16[128,2048]{1,0:T(8,128)(2,1)S(1)}, bf16[128,2048]{1,0:T(8,128)(2,1)S(1)}, u32[]{:S(2)}, u32[]{:S(2)}) %collective-permute-start.87) | collective-permute-done | bytes 524320 | tf_op jit(solution)/shard_map/ppermute | solution.py:45
  718.2 7.3 collective-permute-done.60
  725.5 22.5 %collective-permute-done.59 = bf16[128,2048]{1,0:T(8,128)(2,1)S(1)} collective-permute-done((bf16[128,2048]{1,0:T(8,128)(2,1)S(1)}, bf16[128,2048]{1,0:T(8,128)(2,1)S(1)}, u32[]{:S(2)}, u32[]{:S(2)}) %collective-permute-start.59) | collective-permute-done | bytes 524320 | tf_op jit(solution)/shard_map/ppermute | solution.py:45
  754.5 10.0 collective-permute-done.89
  774.6 19.0 %all-to-all-start.5 = ((f32[32,40,128]{2,1,0:T(8,128)}), f32[32,40,128]{2,1,0:T(8,128)}, u32[]{:S(2)}, u32[]{:S(2)}) async-start(f32[32,40,128]{2,1,0:T(8,128)} %bitcast.505), calls=%async_computation.5 | async-start | bytes 1310720 | tf_op jit(solution)/shard_map/all_to_all | solution.py:436
  798.5 19.6 %collective-permute-done.94 = bf16[128,2048]{1,0:T(8,128)(2,1)S(1)} collective-permute-done((bf16[128,2048]{1,0:T(8,128)(2,1)}, bf16[128,2048]{1,0:T(8,128)(2,1)S(1)}, u32[]{:S(2)}, u32[]{:S(2)}) %collective-permute-start.94) | collective-permute-done | bytes 524320 | tf_op jit(solution)/shard_map/ppermute | solution.py:58
  849.1 6.7 convolution_convert_fusion.2
  885.4 5.3 collective-permute-done.98
  892.1 7.0 collective-permute-done.100
  900.6 21.0 %collective-permute-done.99 = bf16[128,2048]{1,0:T(8,128)(2,1)S(1)} collective-permute-done((bf16[128,2048]{1,0:T(8,128)(2,1)S(1)}, bf16[128,2048]{1,0:T(8,128)(2,1)S(1)}, u32[]{:S(2)}, u32[]{:S(2)}) %collective-permute-start.99) | collective-permute-done | bytes 524320 | tf_op jit(solution)/shard_map/ppermute | solution.py:45
  936.3 6.8 collective-permute-done.109
  955.4 10.1 all-to-all-done.6
  972.8 12.1 %all-to-all-done.4 = f32[4,64,512]{2,1,0:T(8,128)} async-done(((f32[4,64,512]{2,1,0:T(8,128)}), f32[4,64,512]{2,1,0:T(8,128)}, u32[]{:S(2)}, u32[]{:S(2)}) %all-to-all-start.4) | async-done | bytes 524320 | tf_op jit(solution)/shard_map/all_to_all | solution.py:81
  989.3 22.9 %fusion.12 = f32[4,2048,1024]{2,1,0:T(8,128)} fusion(bf16[4,768,2048]{1,2,0:T(8,128)(2,1)} %bitcast.967, bf16[4,768,512]{2,1,0:T(8,128)(2,1)} %get-tuple-element.38, bf16[4,768,512]{2,1,0:T(8,128)(2,1)} %get-tuple-element.37), kind=kOutput, calls=%fused_computation.40 | convolution fusion | flops 12897484800 | bytes 52428800 | tf_op jit(solution)/shard_map/prd,prf->pdf/dot_general | solution.py:372
  1012.2 12.6 %fusion.15 = f32[2,1024,2048]{2,1,0:T(8,128)} fusion(bf16[2,768,2048]{2,1,0:T(8,128)(2,1)} %bitcast.989, bf16[2,768,1024]{1,2,0:T(8,128)(2,1)S(1)} %bitcast.1017, f32[2,768]{1,0:T(2,128)S(1)} %copy-done.71), kind=kOutput, calls=%fused_computation.43 | convolution fusion | flops 6447169536 | bytes 26220544 | tf_op jit(solution)/shard_map/jrf,jrd->jfd/dot_general | solution.py:370
  (723 shorter events, 437.1 us)
Async XLA Ops:
  0.6 40.8 %collective-permute-start.24 = (bf16[64,2048]{1,0:T(8,128)(2,1)}, bf16[64,2048]{1,0:T(8,128)(2,1)}, u32[]{:S(2)}, u32[]{:S(2)}) collective-permute-start(bf16[64,2048]{1,0:T(8,128)(2,1)} %param.21), channel_id=1, source_target_pairs={{0,1},{1,2},{2,3},{4,5},{5,6},{6,7},{8,9},{9,10},{10,11},{12,13},{... | collective-permute-start | bytes 786440 | tf_op jit(solution)/shard_map/ppermute | solution.py:57
  6.3 35.8 %collective-permute-start.27 = (bf16[64,2048]{1,0:T(8,128)(2,1)}, bf16[64,2048]{1,0:T(8,128)(2,1)S(1)}, u32[]{:S(2)}, u32[]{:S(2)}) collective-permute-start(bf16[64,2048]{1,0:T(8,128)(2,1)} %param.21), channel_id=1, source_target_pairs={{1,0},{2,1},{3,2},{5,4},{6,5},{7,6},{9,8},{10,9},{11,10},{13,12},{... | collective-permute-start | bytes 786440 | tf_op jit(solution)/shard_map/ppermute | solution.py:58
  7.6 49.7 %collective-permute-start.3 = (bf16[128,2048]{1,0:T(8,128)(2,1)}, bf16[128,2048]{1,0:T(8,128)(2,1)}, u32[]{:S(2)}, u32[]{:S(2)}) collective-permute-start(bf16[128,2048]{1,0:T(8,128)(2,1)} %bitcast.975), channel_id=1, source_target_pairs={{1,0},{2,1},{3,2},{5,4},{6,5},{7,6},{9,8},{10,9},{11,10},{13,12},{... | collective-permute-start | bytes 1572872 | tf_op jit(solution)/shard_map/ppermute | solution.py:58
  8.9 49.7 %collective-permute-start = (bf16[128,2048]{1,0:T(8,128)(2,1)}, bf16[128,2048]{1,0:T(8,128)(2,1)}, u32[]{:S(2)}, u32[]{:S(2)}) collective-permute-start(bf16[128,2048]{1,0:T(8,128)(2,1)} %bitcast.976), channel_id=1, source_target_pairs={{0,1},{1,2},{2,3},{4,5},{5,6},{6,7},{8,9},{9,10},{10,11},{12,13},{... | collective-permute-start | bytes 1572872 | tf_op jit(solution)/shard_map/ppermute | solution.py:57
  24.5 35.4 %collective-permute-start.61 = (bf16[128,2048]{1,0:T(8,128)(2,1)}, bf16[128,2048]{1,0:T(8,128)(2,1)}, u32[]{:S(2)}, u32[]{:S(2)}) collective-permute-start(bf16[128,2048]{1,0:T(8,128)(2,1)} %bitcast.1023), channel_id=1, source_target_pairs={{0,1},{1,2},{2,3},{4,5},{5,6},{6,7},{8,9},{9,10},{10,11},{12,13},{... | collective-permute-start | bytes 1572872 | tf_op jit(solution)/shard_map/ppermute | solution.py:57
  43.4 49.7 %all-to-all-start.1 = ((bf16[4,64,1536]{2,1,0:T(8,128)(2,1)}), bf16[4,64,1536]{2,1,0:T(8,128)(2,1)S(1)}, u32[]{:S(2)}, u32[]{:S(2)}) async-start(bf16[4,64,1536]{2,1,0:T(8,128)(2,1)} %reshape.727), calls=%async_computation.1 | async-start | bytes 1572864 | tf_op jit(solution)/shard_map/all_to_all | solution.py:81
  58.6 36.9 %collective-permute-start.4 = (bf16[128,2048]{1,0:T(8,128)(2,1)}, bf16[128,2048]{1,0:T(8,128)(2,1)}, u32[]{:S(2)}, u32[]{:S(2)}) collective-permute-start(bf16[128,2048]{1,0:T(8,128)(2,1)} %collective-permute-done.3), channel_id=1, source_target_pairs={{1,0},{2,1},{5,4},{6,5},{9,8},{10,9},{13,12},{14,13},{17,16},{18,1... | collective-permute-start | bytes 1572872 | tf_op jit(solution)/shard_map/ppermute | solution.py:58
  89.2 46.9 %collective-permute-start.33 = (bf16[256,2048]{1,0:T(8,128)(2,1)}, bf16[256,2048]{1,0:T(8,128)(2,1)}, u32[]{:S(2)}, u32[]{:S(2)}) collective-permute-start(bf16[256,2048]{1,0:T(8,128)(2,1)} %bitcast.55), channel_id=1, source_target_pairs={{0,16},{4,20},{8,24},{12,28},{16,0},{20,4},{24,8},{28,12},{1,17},{... | collective-permute-start | bytes 3145736 | tf_op jit(solution)/shard_map/ppermute | solution.py:41
  95.5 43.9 %collective-permute-start.30 = (bf16[256,2048]{1,0:T(8,128)(2,1)}, bf16[256,2048]{1,0:T(8,128)(2,1)S(1)}, u32[]{:S(2)}, u32[]{:S(2)}) collective-permute-start(bf16[256,2048]{1,0:T(8,128)(2,1)} %bitcast.55), channel_id=1, source_target_pairs={{0,4},{4,0},{8,12},{12,8},{16,20},{20,16},{24,28},{28,24},{1,5},{5... | collective-permute-start | bytes 3145736 | tf_op jit(solution)/shard_map/ppermute | solution.py:41
  136.1 78.1 %collective-permute-start.31 = (bf16[256,2048]{1,0:T(8,128)(2,1)}, bf16[256,2048]{1,0:T(8,128)(2,1)}, u32[]{:S(2)}, u32[]{:S(2)}) collective-permute-start(bf16[256,2048]{1,0:T(8,128)(2,1)} %bitcast.55), channel_id=1, source_target_pairs={{0,8},{4,12},{8,0},{12,4},{16,24},{20,28},{24,16},{28,20},{1,9},{5... | collective-permute-start | bytes 3145736 | tf_op jit(solution)/shard_map/ppermute | solution.py:41
  139.5 134.8 %collective-permute-start.70 = (bf16[512,2048]{1,0:T(8,128)(2,1)}, bf16[512,2048]{1,0:T(8,128)(2,1)}, u32[]{:S(2)}, u32[]{:S(2)}) collective-permute-start(bf16[512,2048]{1,0:T(8,128)(2,1)} %bitcast.218), channel_id=1, source_target_pairs={{0,16},{4,20},{8,24},{12,28},{16,0},{20,4},{24,8},{28,12},{1,17},{... | collective-permute-start | bytes 6291464 | tf_op jit(solution)/shard_map/ppermute | solution.py:41
  142.6 53.2 %collective-permute-start.10 = (bf16[256,1536]{1,0:T(8,128)(2,1)S(1)}, bf16[256,1536]{1,0:T(8,128)(2,1)S(1)}, u32[]{:S(2)}, u32[]{:S(2)}) collective-permute-start(bf16[256,1536]{1,0:T(8,128)(2,1)S(1)} %collective-permute-done.9), channel_id=1, source_target_pairs={{0,4},{4,0},{8,12},{12,8},{16,20},{20,16},{24,28},{28,24},{1,5},{5... | collective-permute-start | bytes 2359304 | tf_op jit(solution)/shard_map/ppermute | solution.py:41
  142.8 53.0 %collective-permute-start.12 = (bf16[128,1536]{1,0:T(8,128)(2,1)S(1)}, bf16[128,1536]{1,0:T(8,128)(2,1)S(1)}, u32[]{:S(2)}, u32[]{:S(2)}) collective-permute-start(bf16[128,1536]{1,0:T(8,128)(2,1)S(1)} %slice.639), channel_id=1, source_target_pairs={{0,16},{4,20},{8,24},{12,28},{16,0},{20,4},{24,8},{28,12},{1,17},{... | collective-permute-start | bytes 1179656 | tf_op jit(solution)/shard_map/ppermute | solution.py:41
  170.3 76.0 %collective-permute-start.35 = (bf16[128,2048]{1,0:T(8,128)(2,1)}, bf16[128,2048]{1,0:T(8,128)(2,1)}, u32[]{:S(2)}, u32[]{:S(2)}) collective-permute-start(bf16[128,2048]{1,0:T(8,128)(2,1)} %slice.649), channel_id=1, source_target_pairs={{0,8},{4,12},{8,0},{12,4},{16,24},{20,28},{24,16},{28,20},{1,9},{5... | collective-permute-start | bytes 1572872 | tf_op jit(solution)/shard_map/ppermute | solution.py:41
  241.1 48.8 %collective-permute-start.68 = (bf16[512,2048]{1,0:T(8,128)(2,1)}, bf16[512,2048]{1,0:T(8,128)(2,1)S(1)}, u32[]{:S(2)}, u32[]{:S(2)}) collective-permute-start(bf16[512,2048]{1,0:T(8,128)(2,1)} %bitcast.218), channel_id=1, source_target_pairs={{0,8},{4,12},{8,0},{12,4},{16,24},{20,28},{24,16},{28,20},{1,9},{5... | collective-permute-start | bytes 6291464 | tf_op jit(solution)/shard_map/ppermute | solution.py:41
  246.3 44.3 %collective-permute-start.67 = (bf16[512,2048]{1,0:T(8,128)(2,1)}, bf16[512,2048]{1,0:T(8,128)(2,1)S(1)}, u32[]{:S(2)}, u32[]{:S(2)}) collective-permute-start(bf16[512,2048]{1,0:T(8,128)(2,1)} %bitcast.218), channel_id=1, source_target_pairs={{0,4},{4,0},{8,12},{12,8},{16,20},{20,16},{24,28},{28,24},{1,5},{5... | collective-permute-start | bytes 6291464 | tf_op jit(solution)/shard_map/ppermute | solution.py:41
  276.1 47.2 %collective-permute-start.72 = (bf16[256,2048]{1,0:T(8,128)(2,1)S(1)}, bf16[256,2048]{1,0:T(8,128)(2,1)S(1)}, u32[]{:S(2)}, u32[]{:S(2)}) collective-permute-start(bf16[256,2048]{1,0:T(8,128)(2,1)S(1)} %get-tuple-element.107), channel_id=1, source_target_pairs={{0,8},{4,12},{8,0},{12,4},{16,24},{20,28},{24,16},{28,20},{1,9},{5... | collective-permute-start | bytes 3145736 | tf_op jit(solution)/shard_map/ppermute | solution.py:41
  290.0 33.4 %collective-permute-start.73 = (bf16[256,2048]{1,0:T(8,128)(2,1)S(1)}, bf16[256,2048]{1,0:T(8,128)(2,1)S(1)}, u32[]{:S(2)}, u32[]{:S(2)}) collective-permute-start(bf16[256,2048]{1,0:T(8,128)(2,1)S(1)} %get-tuple-element.110), channel_id=1, source_target_pairs={{0,16},{4,20},{8,24},{12,28},{16,0},{20,4},{24,8},{28,12},{1,17},{... | collective-permute-start | bytes 3145736 | tf_op jit(solution)/shard_map/ppermute | solution.py:41
  317.8 46.9 %collective-permute-start.42 = (bf16[512,2048]{1,0:T(8,128)(2,1)S(1)}, bf16[512,2048]{1,0:T(8,128)(2,1)}, u32[]{:S(2)}, u32[]{:S(2)}) collective-permute-start(bf16[512,2048]{1,0:T(8,128)(2,1)S(1)} %multiply_convert_fusion.6), channel_id=1, source_target_pairs={{0,16},{4,20},{8,24},{12,28},{16,0},{20,4},{24,8},{28,12},{1,17},{... | collective-permute-start | bytes 6291464 | tf_op jit(solution)/shard_map/ppermute | solution.py:41
  321.6 47.4 %collective-permute-start.40 = (bf16[512,2048]{1,0:T(8,128)(2,1)S(1)}, bf16[512,2048]{1,0:T(8,128)(2,1)}, u32[]{:S(2)}, u32[]{:S(2)}) collective-permute-start(bf16[512,2048]{1,0:T(8,128)(2,1)S(1)} %multiply_convert_fusion.6), channel_id=1, source_target_pairs={{0,8},{4,12},{8,0},{12,4},{16,24},{20,28},{24,16},{28,20},{1,9},{5... | collective-permute-start | bytes 6291464 | tf_op jit(solution)/shard_map/ppermute | solution.py:41
  323.3 49.3 %collective-permute-start.39 = (bf16[512,2048]{1,0:T(8,128)(2,1)S(1)}, bf16[512,2048]{1,0:T(8,128)(2,1)}, u32[]{:S(2)}, u32[]{:S(2)}) collective-permute-start(bf16[512,2048]{1,0:T(8,128)(2,1)S(1)} %multiply_convert_fusion.6), channel_id=1, source_target_pairs={{0,4},{4,0},{8,12},{12,8},{16,20},{20,16},{24,28},{28,24},{1,5},{5... | collective-permute-start | bytes 6291464 | tf_op jit(solution)/shard_map/ppermute | solution.py:41
  467.8 73.8 %all-to-all-start.2 = ((f32[32,2,128]{2,1,0:T(2,128)}), f32[32,2,128]{2,1,0:T(2,128)S(1)}, u32[]{:S(2)}, u32[]{:S(2)}) async-start(f32[32,2,128]{2,1,0:T(2,128)} %bitcast.320), calls=%async_computation.2 | async-start | bytes 65536 | tf_op jit(solution)/shard_map/all_to_all | solution.py:356
  498.2 43.6 %collective-permute-start.52 = (bf16[512,2048]{1,0:T(8,128)(2,1)}, bf16[512,2048]{1,0:T(8,128)(2,1)}, u32[]{:S(2)}, u32[]{:S(2)}) collective-permute-start(bf16[512,2048]{1,0:T(8,128)(2,1)} %bitcast.196), channel_id=1, source_target_pairs={{0,4},{4,0},{8,12},{12,8},{16,20},{20,16},{24,28},{28,24},{1,5},{5... | collective-permute-start | bytes 6291464 | tf_op jit(solution)/shard_map/ppermute | solution.py:41
  498.5 62.2 %collective-permute-start.48 = (bf16[512,2048]{1,0:T(8,128)(2,1)}, bf16[512,2048]{1,0:T(8,128)(2,1)}, u32[]{:S(2)}, u32[]{:S(2)}) collective-permute-start(bf16[512,2048]{1,0:T(8,128)(2,1)} %bitcast.166), channel_id=1, source_target_pairs={{0,4},{4,0},{8,12},{12,8},{16,20},{20,16},{24,28},{28,24},{1,5},{5... | collective-permute-start | bytes 6291464 | tf_op jit(solution)/shard_map/ppermute | solution.py:41
  498.7 46.4 %collective-permute-start.49 = (bf16[512,2048]{1,0:T(8,128)(2,1)}, bf16[512,2048]{1,0:T(8,128)(2,1)}, u32[]{:S(2)}, u32[]{:S(2)}) collective-permute-start(bf16[512,2048]{1,0:T(8,128)(2,1)} %bitcast.176), channel_id=1, source_target_pairs={{0,4},{4,0},{8,12},{12,8},{16,20},{20,16},{24,28},{28,24},{1,5},{5... | collective-permute-start | bytes 6291464 | tf_op jit(solution)/shard_map/ppermute | solution.py:41
  499.0 49.1 %collective-permute-start.51 = (bf16[512,2048]{1,0:T(8,128)(2,1)}, bf16[512,2048]{1,0:T(8,128)(2,1)}, u32[]{:S(2)}, u32[]{:S(2)}) collective-permute-start(bf16[512,2048]{1,0:T(8,128)(2,1)} %bitcast.186), channel_id=1, source_target_pairs={{0,4},{4,0},{8,12},{12,8},{16,20},{20,16},{24,28},{28,24},{1,5},{5... | collective-permute-start | bytes 6291464 | tf_op jit(solution)/shard_map/ppermute | solution.py:41
  551.0 55.8 %collective-permute-start.53 = (bf16[256,2048]{1,0:T(8,128)(2,1)S(1)}, bf16[256,2048]{1,0:T(8,128)(2,1)S(1)}, u32[]{:S(2)}, u32[]{:S(2)}) collective-permute-start(bf16[256,2048]{1,0:T(8,128)(2,1)S(1)} %get-tuple-element.102), channel_id=1, source_target_pairs={{0,8},{4,12},{8,0},{12,4},{16,24},{20,28},{24,16},{28,20},{1,9},{5... | collective-permute-start | bytes 3145736 | tf_op jit(solution)/shard_map/ppermute | solution.py:41
  555.4 50.5 %collective-permute-start.56 = (bf16[256,2048]{1,0:T(8,128)(2,1)S(1)}, bf16[256,2048]{1,0:T(8,128)(2,1)S(1)}, u32[]{:S(2)}, u32[]{:S(2)}) collective-permute-start(bf16[256,2048]{1,0:T(8,128)(2,1)S(1)} %get-tuple-element.103), channel_id=1, source_target_pairs={{0,16},{4,20},{8,24},{12,28},{16,0},{20,4},{24,8},{28,12},{1,17},{... | collective-permute-start | bytes 3145736 | tf_op jit(solution)/shard_map/ppermute | solution.py:41
  558.3 46.4 %collective-permute-start.81 = (bf16[256,2048]{1,0:T(8,128)(2,1)S(1)}, bf16[256,2048]{1,0:T(8,128)(2,1)S(1)}, u32[]{:S(2)}, u32[]{:S(2)}) collective-permute-start(bf16[256,2048]{1,0:T(8,128)(2,1)S(1)} %get-tuple-element.97), channel_id=1, source_target_pairs={{0,8},{4,12},{8,0},{12,4},{16,24},{20,28},{24,16},{28,20},{1,9},{5... | collective-permute-start | bytes 3145736 | tf_op jit(solution)/shard_map/ppermute | solution.py:41
  560.8 42.0 %collective-permute-start.84 = (bf16[256,2048]{1,0:T(8,128)(2,1)S(1)}, bf16[256,2048]{1,0:T(8,128)(2,1)S(1)}, u32[]{:S(2)}, u32[]{:S(2)}) collective-permute-start(bf16[256,2048]{1,0:T(8,128)(2,1)S(1)} %get-tuple-element.98), channel_id=1, source_target_pairs={{0,16},{4,20},{8,24},{12,28},{16,0},{20,4},{24,8},{28,12},{1,17},{... | collective-permute-start | bytes 3145736 | tf_op jit(solution)/shard_map/ppermute | solution.py:41
  563.8 58.1 %collective-permute-start.78 = (bf16[256,2048]{1,0:T(8,128)(2,1)S(1)}, bf16[256,2048]{1,0:T(8,128)(2,1)S(1)}, u32[]{:S(2)}, u32[]{:S(2)}) collective-permute-start(bf16[256,2048]{1,0:T(8,128)(2,1)S(1)} %slice.724), channel_id=1, source_target_pairs={{0,8},{4,12},{8,0},{12,4},{16,24},{20,28},{24,16},{28,20},{1,9},{5... | collective-permute-start | bytes 3145736 | tf_op jit(solution)/shard_map/ppermute | solution.py:41
  604.7 39.7 %collective-permute-start.85 = (bf16[256,2048]{1,0:T(8,128)(2,1)S(1)}, bf16[256,2048]{1,0:T(8,128)(2,1)S(1)}, u32[]{:S(2)}, u32[]{:S(2)}) collective-permute-start(bf16[256,2048]{1,0:T(8,128)(2,1)S(1)} %add_convert_fusion), channel_id=1, source_target_pairs={{0,8},{4,12},{8,0},{12,4},{16,24},{20,28},{24,16},{28,20},{1,9},{5... | collective-permute-start | bytes 3145736 | tf_op jit(solution)/shard_map/ppermute | solution.py:41
  605.9 45.5 %collective-permute-start.82 = (bf16[256,2048]{1,0:T(8,128)(2,1)S(1)}, bf16[256,2048]{1,0:T(8,128)(2,1)S(1)}, u32[]{:S(2)}, u32[]{:S(2)}) collective-permute-start(bf16[256,2048]{1,0:T(8,128)(2,1)S(1)} %add_convert_fusion.1), channel_id=1, source_target_pairs={{0,16},{4,20},{8,24},{12,28},{16,0},{20,4},{24,8},{28,12},{1,17},{... | collective-permute-start | bytes 3145736 | tf_op jit(solution)/shard_map/ppermute | solution.py:41
  606.8 60.1 %collective-permute-start.50 = (bf16[256,2048]{1,0:T(8,128)(2,1)S(1)}, bf16[256,2048]{1,0:T(8,128)(2,1)S(1)}, u32[]{:S(2)}, u32[]{:S(2)}) collective-permute-start(bf16[256,2048]{1,0:T(8,128)(2,1)S(1)} %slice.692), channel_id=1, source_target_pairs={{0,8},{4,12},{8,0},{12,4},{16,24},{20,28},{24,16},{28,20},{1,9},{5... | collective-permute-start | bytes 3145736 | tf_op jit(solution)/shard_map/ppermute | solution.py:41
  622.0 51.9 %collective-permute-start.55 = (bf16[256,2048]{1,0:T(8,128)(2,1)S(1)}, bf16[256,2048]{1,0:T(8,128)(2,1)S(1)}, u32[]{:S(2)}, u32[]{:S(2)}) collective-permute-start(bf16[256,2048]{1,0:T(8,128)(2,1)S(1)} %slice.704), channel_id=1, source_target_pairs={{0,16},{4,20},{8,24},{12,28},{16,0},{20,4},{24,8},{28,12},{1,17},{... | collective-permute-start | bytes 3145736 | tf_op jit(solution)/shard_map/ppermute | solution.py:41
  628.9 60.0 %collective-permute-start.57 = (bf16[256,2048]{1,0:T(8,128)(2,1)S(1)}, bf16[256,2048]{1,0:T(8,128)(2,1)S(1)}, u32[]{:S(2)}, u32[]{:S(2)}) collective-permute-start(bf16[256,2048]{1,0:T(8,128)(2,1)S(1)} %add_convert_fusion.2), channel_id=1, source_target_pairs={{0,8},{4,12},{8,0},{12,4},{16,24},{20,28},{24,16},{28,20},{1,9},{5... | collective-permute-start | bytes 3145736 | tf_op jit(solution)/shard_map/ppermute | solution.py:41
  644.4 49.8 %collective-permute-start.54 = (bf16[256,2048]{1,0:T(8,128)(2,1)S(1)}, bf16[256,2048]{1,0:T(8,128)(2,1)S(1)}, u32[]{:S(2)}, u32[]{:S(2)}) collective-permute-start(bf16[256,2048]{1,0:T(8,128)(2,1)S(1)} %add_convert_fusion.3), channel_id=1, source_target_pairs={{0,16},{4,20},{8,24},{12,28},{16,0},{20,4},{24,8},{28,12},{1,17},{... | collective-permute-start | bytes 3145736 | tf_op jit(solution)/shard_map/ppermute | solution.py:41
  653.0 46.7 %collective-permute-start.86 = (bf16[128,2048]{1,0:T(8,128)(2,1)S(1)}, bf16[128,2048]{1,0:T(8,128)(2,1)S(1)}, u32[]{:S(2)}, u32[]{:S(2)}) collective-permute-start(bf16[128,2048]{1,0:T(8,128)(2,1)S(1)} %get-tuple-element.94), channel_id=1, source_target_pairs={{0,1},{1,2},{2,3},{3,0},{4,5},{5,6},{6,7},{7,4},{8,9},{9,10},{10,1... | collective-permute-start | bytes 1572872 | tf_op jit(solution)/shard_map/ppermute | solution.py:45
  666.9 33.4 %collective-permute-start.88 = (bf16[128,2048]{1,0:T(8,128)(2,1)S(1)}, bf16[128,2048]{1,0:T(8,128)(2,1)S(1)}, u32[]{:S(2)}, u32[]{:S(2)}) collective-permute-start(bf16[128,2048]{1,0:T(8,128)(2,1)S(1)} %get-tuple-element.95), channel_id=1, source_target_pairs={{0,3},{1,0},{2,1},{3,2},{4,7},{5,4},{6,5},{7,6},{8,11},{9,8},{10,9... | collective-permute-start | bytes 1572872 | tf_op jit(solution)/shard_map/ppermute | solution.py:45
  673.8 43.1 %collective-permute-start.87 = (bf16[128,2048]{1,0:T(8,128)(2,1)S(1)}, bf16[128,2048]{1,0:T(8,128)(2,1)S(1)}, u32[]{:S(2)}, u32[]{:S(2)}) collective-permute-start(bf16[128,2048]{1,0:T(8,128)(2,1)S(1)} %get-tuple-element.96), channel_id=1, source_target_pairs={{0,2},{1,3},{2,0},{3,1},{4,6},{5,7},{6,4},{7,5},{8,10},{9,11},{10,... | collective-permute-start | bytes 1572872 | tf_op jit(solution)/shard_map/ppermute | solution.py:45
  699.7 48.3 %collective-permute-start.59 = (bf16[128,2048]{1,0:T(8,128)(2,1)S(1)}, bf16[128,2048]{1,0:T(8,128)(2,1)S(1)}, u32[]{:S(2)}, u32[]{:S(2)}) collective-permute-start(bf16[128,2048]{1,0:T(8,128)(2,1)S(1)} %get-tuple-element.101), channel_id=1, source_target_pairs={{0,2},{1,3},{2,0},{3,1},{4,6},{5,7},{6,4},{7,5},{8,10},{9,11},{10,... | collective-permute-start | bytes 1572872 | tf_op jit(solution)/shard_map/ppermute | solution.py:45
  774.6 175.9 %all-to-all-start.5 = ((f32[32,40,128]{2,1,0:T(8,128)}), f32[32,40,128]{2,1,0:T(8,128)}, u32[]{:S(2)}, u32[]{:S(2)}) async-start(f32[32,40,128]{2,1,0:T(8,128)} %bitcast.505), calls=%async_computation.5 | async-start | bytes 1310720 | tf_op jit(solution)/shard_map/all_to_all | solution.py:436
  878.5 43.1 %collective-permute-start.99 = (bf16[128,2048]{1,0:T(8,128)(2,1)S(1)}, bf16[128,2048]{1,0:T(8,128)(2,1)S(1)}, u32[]{:S(2)}, u32[]{:S(2)}) collective-permute-start(bf16[128,2048]{1,0:T(8,128)(2,1)S(1)} %get-tuple-element.93), channel_id=1, source_target_pairs={{0,2},{1,3},{2,0},{3,1},{4,6},{5,7},{6,4},{7,5},{8,10},{9,11},{10,... | collective-permute-start | bytes 1572872 | tf_op jit(solution)/shard_map/ppermute | solution.py:45
  879.6 66.8 %collective-permute-start.113 = (bf16[128,512]{1,0:T(8,128)(2,1)}, bf16[128,512]{1,0:T(8,128)(2,1)}, u32[]{:S(2)}, u32[]{:S(2)}) collective-permute-start(bf16[128,512]{1,0:T(8,128)(2,1)} %slice.753), channel_id=1, source_target_pairs={{0,8},{4,12},{8,0},{12,4},{16,24},{20,28},{24,16},{28,20},{1,9},{5... | collective-permute-start | bytes 393224 | tf_op jit(solution)/shard_map/ppermute | solution.py:41
  881.1 66.8 %collective-permute-start.118 = (bf16[128,512]{1,0:T(8,128)(2,1)}, bf16[128,512]{1,0:T(8,128)(2,1)}, u32[]{:S(2)}, u32[]{:S(2)}) collective-permute-start(bf16[128,512]{1,0:T(8,128)(2,1)} %slice.757), channel_id=1, source_target_pairs={{0,16},{4,20},{8,24},{12,28},{16,0},{20,4},{24,8},{28,12},{1,17},{... | collective-permute-start | bytes 393224 | tf_op jit(solution)/shard_map/ppermute | solution.py:41
  890.7 57.8 %collective-permute-start.117 = (bf16[128,512]{1,0:T(8,128)(2,1)}, bf16[128,512]{1,0:T(8,128)(2,1)}, u32[]{:S(2)}, u32[]{:S(2)}) collective-permute-start(bf16[128,512]{1,0:T(8,128)(2,1)} %add_convert_fusion.9), channel_id=1, source_target_pairs={{0,16},{4,20},{8,24},{12,28},{16,0},{20,4},{24,8},{28,12},{1,17},{... | collective-permute-start | bytes 393224 | tf_op jit(solution)/shard_map/ppermute | solution.py:41
  899.1 54.1 %collective-permute-start.120 = (bf16[128,512]{1,0:T(8,128)(2,1)}, bf16[128,512]{1,0:T(8,128)(2,1)}, u32[]{:S(2)}, u32[]{:S(2)}) collective-permute-start(bf16[128,512]{1,0:T(8,128)(2,1)} %add_convert_fusion.8), channel_id=1, source_target_pairs={{0,8},{4,12},{8,0},{12,4},{16,24},{20,28},{24,16},{28,20},{1,9},{5... | collective-permute-start | bytes 393224 | tf_op jit(solution)/shard_map/ppermute | solution.py:41
  984.9 46.2 %all-to-all-start.3 = ((f32[4,64,1536]{2,1,0:T(8,128)}), f32[4,64,1536]{2,1,0:T(8,128)}, u32[]{:S(2)}, u32[]{:S(2)}) async-start(f32[4,64,1536]{2,1,0:T(8,128)} %bitcast.358), calls=%async_computation.3 | async-start | bytes 3145728 | tf_op jit(solution)/shard_map/all_to_all | solution.py:81
  (163 other events, 2887.1 us)

commit v2 on v1

v2 whole, which is shorter than its diff:
```python
import functools
import math

import jax
import jax.numpy as jnp
from jax import lax
from jax.experimental import pallas as pl
from jax.experimental.pallas import tpu as pltpu
from jax.sharding import PartitionSpec as P

H = 16
HD = 128
E = 64
TOP = 8
FH = 512
CAP = 24

EPS = 1e-05
MASKED = -1e30
ROPE_BASE = 10000.0
HIGHEST = lax.Precision.HIGHEST
F32 = jnp.float32
BF = jnp.bfloat16
ALL = ("fsdp", "ctx")
LANES = 128
VMEM_LIMIT = 60 * 1024 * 1024


def pick(stacked, index):
    return lax.dynamic_index_in_dim(stacked, index, 0, keepdims=False)


def after(value, *others):
    return held([value], *others)[0]


def held(values, *others):
    if not others:
        return list(values)
    values = list(values)
    anywhere = pl.BlockSpec(memory_space=pl.ANY)
    done = pl.pallas_call(
        lambda *refs: None,
        out_shape=[jax.ShapeDtypeStruct(v.shape, v.dtype) for v in values],
        in_specs=[anywhere] * (len(values) + len(others)),
        out_specs=[anywhere] * len(values),
        input_output_aliases={i: i for i in range(len(values))},
    )(*values, *others)
    return list(done)


def held_pieces(blocks, *gate):
    flat = held([a for b in blocks for a in b], *gate)
    return [[flat.pop(0) for _ in b] for b in blocks]


def add_low(*terms):
    return sum(t.astype(F32) for t in terms).astype(BF)


class Links:
    def __init__(self, nf, nc):
        self.nf, self.nc = nf, nc
        self.native = nf == 8 and nc == 4
        self.cores = 2 if self.native else 1
        self.f = lax.axis_index("fsdp")
        self.c = lax.axis_index("ctx")
        ms = jnp.arange(nf, dtype=jnp.int32)
        self.frel = self.f ^ ms if self.native else ms

    def swap(self, value, mask):
        return lax.ppermute(value, "fsdp", [(i, i ^ mask) for i in range(self.nf)])

    def cswap(self, value, mask):
        return lax.ppermute(value, "ctx", [(i, i ^ mask) for i in range(self.nc)])

    def exchange(self, value):
        return lax.all_to_all(value, "ctx", split_axis=0, concat_axis=0, tiled=True)

    def gather(self, value, *gate):
        return self.exchange(after(jnp.broadcast_to(value, (self.nc,) + value.shape), *gate))

    def slots(self, value):
        if not self.native:
            whole = lax.all_gather(value, "ctx", axis=0)
            return [whole[k] for k in range(self.nc)]
        return [value] + [self.cswap(value, k) for k in range(1, self.nc)]

    def sum_slots(self, parts):
        if not self.native:
            whole = jnp.stack(parts)
            return [lax.psum_scatter(whole, "ctx", scatter_dimension=0, tiled=False)]
        return [parts[0]] + [self.cswap(parts[k], k) for k in range(1, self.nc)]

    def relative(self, value, planes=False):
        if not self.native:
            return value
        dims = value.shape
        for bit, place in ((4, self.f), (2, self.f), (1, self.f), (2, self.c), (1, self.c)):
            lead = 0 if place is self.f else 1
            if lead and planes:
                continue
            n = dims[lead]
            split = dims[:lead] + (n // (2 * bit), 2, bit) + dims[lead + 1 :]
            cut = value.reshape(split)
            parts = jnp.split(cut, 2, axis=lead + 1)
            flipped = jnp.concatenate(parts[::-1], axis=lead + 1)
            value = jnp.where((place & bit) > 0, flipped, cut).reshape(dims)
        return value

    def plane_start(self, value):
        if not self.native:
            return [value]
        return [value, self.swap(value, 2), self.swap(value, 4)]

    def plane_end(self, begun, *gate):
        if not self.native:
            whole = lax.all_gather(begun[0], "fsdp", axis=0)
            return [[whole[m]] for m in range(self.nf)], begun
        value, from_x, from_y = begun
        half = value.shape[0] // 2
        from_x, from_y = held([from_x, from_y], *gate)
        sent = [from_y[:half], from_x[half:]]
        diag_a = self.swap(sent[0], 2)
        diag_b = self.swap(sent[1], 4)
        return [[value], [from_x], [from_y], [diag_a, diag_b]], sent

    def all_blocks(self, pieces):
        blocks = [b[0] if len(b) == 1 else jnp.concatenate(b) for b in pieces]
        if not self.native:
            return blocks
        return [a for b in blocks for a in (b, self.swap(b, 1))]

    def dense_plan(self, rows):
        if not self.native:
            return [(m, 0, rows, 0, m * rows) for m in range(self.nf)], [self.nf * rows]
        h = rows // 2
        order = [(2, 0), (6, 0), (4, h), (6, h), (4, 0), (2, h), (0, 0), (0, h)]
        entries = []
        for core in (0, 1):
            for place, (m, first) in enumerate(order):
                entries.append((m + core, first, h, core, place * h))
        return entries, [8 * h, 8 * h]

    def dense_start(self, arrays, rows, *gate):
        if not self.native:
            return arrays
        mine, other = arrays
        near = after(self.swap(other, 1), *gate)
        h = rows // 2
        spans = [(0, 2), (2, 2), (4, 1), (5, 1), (6, 2)]
        sums = [
            add_low(mine[a * h : (a + n) * h], near[a * h : (a + n) * h]) for a, n in spans
        ]
        return self.reduce_start(sums)

    def plane_plan(self, rows):
        if not self.native:
            return [(m, 0, rows, 0, m * rows) for m in range(self.nf)], [self.nf * rows]
        h = rows // 2
        entries = [(2, 0, h, 0, 0), (6, 0, h, 0, h), (4, h, h, 1, 0), (6, h, h, 1, h)]
        entries += [(4, 0, h, 2, 0), (2, h, h, 3, 0), (0, 0, rows, 4, 0)]
        return entries, [rows, rows, h, h, rows]

    def reduce_start(self, arrays):
        if not self.native:
            return arrays
        to_x, to_y, rest_y, rest_x, own = arrays
        return [self.swap(to_x, 2), self.swap(to_y, 4), rest_y, rest_x, own]

    def reduce_next(self, begun, *gate):
        if not self.native:
            return begun
        got_x, got_y, rest_y, rest_x, own = begun
        if gate:
            got_x, got_y = held([got_x, got_y], *gate)
        h = rest_y.shape[0]
        last_y = add_low(rest_y, got_x[h:])
        last_x = add_low(rest_x, got_y[h:])
        return [got_x, got_y, self.swap(last_y, 4), self.swap(last_x, 2), own, last_y, last_x]

    def reduce_end(self, begun, rows, *gate):
        if not self.native:
            whole = begun[0].reshape((self.nf, rows) + begun[0].shape[1:])
            return lax.psum_scatter(whole, "fsdp", scatter_dimension=0, tiled=False)
        got_x, got_y, last_y, last_x, own = begun[:5]
        if gate:
            last_y, last_x = held([last_y, last_x], *gate)
        h = rows // 2
        return jnp.concatenate(
            [add_low(own[:h], got_x[:h], last_y), add_low(own[h:], got_y[:h], last_x)]
        )


def mm(a, b):
    return lax.dot_general(a, b, (((1,), (0,)), ((), ())), preferred_element_type=F32)


def mm_nt(a, b):
    return lax.dot_general(a, b, (((1,), (1,)), ((), ())), preferred_element_type=F32)


def mm_tn(a, b):
    return lax.dot_general(a, b, (((0,), (0,)), ((), ())), preferred_element_type=F32)


def call(
    kernel, outs, gflop, mbytes, ins=None, grid=(), out_specs=None, scratch=(), aliases=None, spec=None, gate=()
):
    args = dict(
        out_shape=outs,
        input_output_aliases=aliases or {},
        cost_estimate=pl.CostEstimate(
            flops=int(gflop * 5e7), bytes_accessed=int(mbytes * 5e4), transcendentals=0
        ),
        compiler_params=pltpu.CompilerParams(vmem_limit_bytes=VMEM_LIMIT),
    )
    if spec is not None:
        return pl.pallas_call(kernel, grid_spec=spec, **args)
    given, waits = len(ins), len(gate)

    def body(*refs):
        kernel(*refs[:given], *refs[given + waits :])

    args["scratch_shapes"] = list(scratch)
    args["in_specs"] = list(ins) + [pl.BlockSpec(memory_space=pl.ANY)] * waits
    if grid:
        args["grid"] = grid
    if out_specs is not None:
        args["out_specs"] = out_specs
    made = pl.pallas_call(body, **args)
    return lambda *operands: made(*operands, *gate)


SMEM = pl.BlockSpec(memory_space=pltpu.SMEM)
VMEM = pl.BlockSpec(memory_space=pltpu.VMEM)


def shape(dims, dtype):
    return jax.ShapeDtypeStruct(tuple(dims), dtype)


def qkv_kernel(nf, frel, gain, xs, *refs):
    ws = refs[:nf]
    normed, raw, value, sums = refs[nf:]
    width = value.shape[1]
    block = ws[0].shape[0]
    x = xs[...].astype(F32)
    inv = lax.rsqrt(jnp.mean(x * x, axis=-1, keepdims=True) + EPS)
    normed[...] = (x * inv * gain[...]).astype(BF)
    total = None
    for m in range(nf):
        cols = pl.ds(pl.multiple_of(frel[m] * block, block), block)
        term = mm(normed[:, cols], ws[m][:, : 3 * width])
        total = term if total is None else total + term
    q, k = total[:, :width], total[:, width : 2 * width]
    raw[0] = q
    raw[1] = k
    value[...] = total[:, 2 * width :].astype(BF)
    for i, part in enumerate((q, k)):
        column = jnp.sum(part * part, axis=-1, keepdims=True)
        sums[i] = jnp.broadcast_to(column, (column.shape[0], LANES)).T[:8]


def turn(v, cos, sin):
    half = HD // 2
    other = jnp.concatenate([v[:, half:], v[:, :half]], axis=1)
    return v * cos + other * sin


def attend_kernel(scale, raw, value, inv, gain, cos, sin, mask, low, mixed):
    q = turn(raw[0] * inv[0] * gain[0], cos[...], sin[...]).astype(BF)
    k = turn(raw[1] * inv[1] * gain[1], cos[...], sin[...]).astype(BF)
    low[0] = q
    low[1] = k
    scores = jnp.where(mask[...] > 0, mm_nt(q, k) * scale, MASKED)
    top = jnp.max(scores, axis=-1, keepdims=True)
    e = jnp.exp(scores - top)
    probs = e / jnp.sum(e, axis=-1, keepdims=True)
    mixed[...] = mm(probs.astype(BF), value[...]).astype(BF)


def attend_back_kernel(
    scale, raw, low, value, inv, gain, cos, sin, mask, dmixed, u, dv, stats, dgain
):
    q, k, v = low[0], low[1], value[...]
    scores = jnp.where(mask[...] > 0, mm_nt(q, k) * scale, MASKED)
    top = jnp.max(scores, axis=-1, keepdims=True)
    e = jnp.exp(scores - top)
    probs = e / jnp.sum(e, axis=-1, keepdims=True)
    dm = dmixed[...]
    dprobs = mm_nt(dm, v)
    delta = jnp.sum(probs * dprobs, axis=-1, keepdims=True)
    ds = (probs * (dprobs - delta)).astype(BF)
    dv[...] = mm_tn(probs.astype(BF), dm).astype(BF)
    first = pl.program_id(0) == 0
    for i, grad in enumerate((mm(ds, k) * scale, mm_tn(ds, q) * scale)):
        turned = turn(grad, cos[...], -sin[...])
        ui = turned * gain[i]
        u[i] = ui
        line = jnp.sum(turned * raw[i] * inv[i], axis=0, keepdims=True)
        dgain[i] = jnp.broadcast_to(line, (8, line.shape[1]))
        column = jnp.sum(ui * raw[i], axis=-1, keepdims=True)
        flat = jnp.broadcast_to(column, (column.shape[0], LANES)).T[:8]
        stats[i] = jnp.where(first, flat, stats[i] + flat)


def out_kernel(nf, frel, x, gain, mixed, *refs):
    ws = refs[:nf]
    hidden, inv_out, moe, rows = refs[nf:]
    width = mixed.shape[2]
    block = ws[0].shape[0]
    for k in range(mixed.shape[0]):
        rows[:, k * width : (k + 1) * width] = mixed[k]
    total = x[...].astype(F32)
    for m in range(nf):
        cols = pl.ds(pl.multiple_of(frel[m] * block, block), block)
        total = total + mm(rows[:, cols], ws[m][...])
    hidden[...] = total
    inv = lax.rsqrt(jnp.mean(total * total, axis=-1, keepdims=True) + EPS)
    inv_out[...] = jnp.broadcast_to(inv, inv_out.shape)
    moe[...] = (total * inv * gain[...]).astype(BF)


def hidden_back_kernel(nf, nt, frel, hidden, inv_in, moe, g, gain, router, dprob, *refs):
    terms, ws = refs[:nt], refs[nt : nt + nf]
    dhidden, drouter, dgain, low_rows, dmixed, mix_rows = refs[nt + nf :]
    width = dmixed.shape[2]
    block = ws[0].shape[0]
    logits = mm(moe[...], router[...])
    lane = lax.broadcasted_iota(jnp.int32, logits.shape, 1)
    logits = jnp.where(lane < E, logits, MASKED)
    e = jnp.exp(logits - jnp.max(logits, axis=-1, keepdims=True))
    probs = e / jnp.sum(e, axis=-1, keepdims=True)
    dp = dprob[...]
    dlogits = probs * (dp - jnp.sum(probs * dp, axis=-1, keepdims=True))
    high = dlogits.astype(BF)
    rest = (dlogits - high.astype(F32)).astype(BF)
    drouter[...] = mm_tn(moe[...], high) + mm_tn(moe[...], rest)
    dmoe = mm_nt(high, router[...]) + mm_nt(rest, router[...])
    for term in terms:
        dmoe = dmoe + term[...].astype(F32)
    hid = hidden[...]
    inv = inv_in[:, :1]
    u = dmoe * gain[...]
    mean = jnp.mean(u * hid, axis=-1, keepdims=True)
    line = jnp.sum(dmoe * hid * inv, axis=0, keepdims=True)
    dgain[...] = jnp.broadcast_to(line, dgain.shape)
    dh = g[...].astype(F32) + inv * u - hid * (inv * inv * inv) * mean
    dhidden[...] = dh
    low_rows[...] = dh.astype(BF)
    for m in range(nf):
        cols = pl.ds(pl.multiple_of(frel[m] * block, block), block)
        mix_rows[:, cols] = mm_nt(low_rows[...], ws[m][...]).astype(BF)
    for k in range(dmixed.shape[0]):
        dmixed[k] = mix_rows[:, k * width : (k + 1) * width]


def dnormed_kernel(nf, frel, u, raw, inv, mean, dv, x, *refs):
    ws = refs[:nf]
    dqkv, total, line = refs[nf:]
    width = dv.shape[1]
    block = ws[0].shape[0]
    for i in range(2):
        r = inv[i][:, :1]
        b = mean[i][:, :1]
        dqkv[:, i * width : (i + 1) * width] = (r * u[i] - raw[i] * (r * r * r * b)).astype(BF)
    dqkv[:, 2 * width :] = dv[...]
    for m in range(nf):
        cols = pl.ds(pl.multiple_of(frel[m] * block, block), block)
        total[:, cols] = mm_nt(dqkv[...], ws[m][:, : 3 * width]).astype(BF)
    xf = x[...].astype(F32)
    x_inv = lax.rsqrt(jnp.mean(xf * xf, axis=-1, keepdims=True) + EPS)
    terms = jnp.sum(total[...].astype(F32) * xf * x_inv, axis=0, keepdims=True)
    line[...] = jnp.broadcast_to(terms, line.shape)


def place(plan, outs, blocks):
    for m, first, count, which, row in plan:
        outs[which][row : row + count, :] = blocks[m][first : first + count, :]


def place_grad_kernel(nf, plan, frel, left, right, extra, *outs):
    block = left.shape[1] // nf
    for m in range(nf):
        cols = pl.ds(pl.multiple_of(frel[m] * block, block), block)
        term = mm_tn(left[:, cols], right[...]).astype(BF)
        term = jnp.concatenate([term, extra[cols, :]], axis=1)
        place([p for p in plan if p[0] == m], outs, {m: term})


def take_kernel(sizes, experts, slots, *refs):
    cores = slots.shape[1] // (experts * 2 * CAP)
    xs, outs = refs[:-cores], refs[-cores:]
    two = 2 * CAP
    at = 0
    for m, size in enumerate(sizes):
        rows = [r[...] for r in xs[at : at + size]]
        at += size
        got = mm(slots[m], rows[0] if size == 1 else jnp.concatenate(rows, axis=0)).astype(BF)
        for e in range(experts * cores):
            outs[e // experts][e % experts, m * two : (m + 1) * two, :] = got[e * two : (e + 1) * two]


def take_placed_kernel(places, slots, x, out):
    del places
    got = mm(slots[0], x[0]).astype(BF)
    count = got.shape[0] // out.shape[0]
    for e in range(out.shape[0]):
        out[e] = got[e * count : (e + 1) * count]


def put_kernel(blocks, step, plan, slots, *refs):
    cores = step
    rows, outs = refs[:cores], refs[cores:]
    two = 2 * CAP
    for m in range(blocks):
        cut = [
            part[j, m * two : (m + 1) * two, :] for part in rows for j in range(part.shape[0])
        ]
        low = mm(slots[m], jnp.concatenate(cut, axis=0)).astype(BF)
        place([p for p in plan if p[0] == m * step], outs, {m * step: low})


def expert_kernel(halves, cores, first, router, w_in, w_out, *refs):
    xs, gs = refs[:cores], refs[cores : -3 - cores]
    dslots = refs[-3 - cores : -3]
    dproj, inner_out, dgate = refs[-3:]
    xr = jnp.concatenate([r[0] for r in xs], axis=0)
    gr = jnp.concatenate([r[0] for r in gs], axis=0)
    logits = mm(xr, router[...])
    lane = lax.broadcasted_iota(jnp.int32, logits.shape, 1)
    logits = jnp.where(lane < E, logits, MASKED)
    e = jnp.exp(logits - jnp.max(logits, axis=-1, keepdims=True))
    mine = first[0] + pl.program_id(0)
    chosen = jnp.sum(jnp.where(lane == mine, e, 0.0), axis=-1, keepdims=True)
    gate = chosen / jnp.sum(e, axis=-1, keepdims=True)
    back = mm_nt(gr, w_out[0])
    dg = 0.0
    ds = 0.0
    for h in range(halves):
        projected = mm(xr, w_in[h])
        a, up = projected[:, :FH], projected[:, FH:]
        sig = jax.nn.sigmoid(a)
        act = a * sig
        inner = act * up
        b = back[:, h * FH : (h + 1) * FH]
        dg = dg + jnp.sum(inner * b, axis=-1, keepdims=True)
        inner_out[0, :, h * FH : (h + 1) * FH] = (inner * gate).astype(BF)
        db = b * gate
        dproj[h, :, :FH] = (db * up * (sig * (1.0 + a * (1.0 - sig)))).astype(BF)
        dproj[h, :, FH:] = (db * act).astype(BF)
        ds = ds + mm_nt(dproj[h], w_in[h])
    low = ds.astype(BF)
    count = dslots[0].shape[1]
    for i in range(cores):
        dslots[i][0] = low[i * count : (i + 1) * count]
    dgate[0] = jnp.broadcast_to(dg, dgate.shape[1:])


def result_kernel(inner, w_out, *outs):
    low = mm(inner[0], w_out[0]).astype(BF)
    count = outs[0].shape[1]
    for i, out in enumerate(outs):
        out[0] = low[i * count : (i + 1) * count]


def weight_grad_kernel(whole, parts, *refs):
    total = None
    for w, ps in zip(whole, parts):
        at = 0
        for p in ps:
            n = refs[p].shape[1]
            term = (refs[w][0, at : at + n, :], refs[p][0])
            at += n
            term = mm_tn(term[1], term[0]) if w > p else mm_tn(term[0], term[1])
            total = term if total is None else total + term
    refs[-1][0] = total


def rotary_tables(positions):
    half = HD // 2
    frequency = ROPE_BASE ** (-(jnp.arange(half, dtype=F32) * 2.0 / HD))
    angles = positions.astype(F32)[:, None] * frequency[None, :]
    cos, sin = jnp.cos(angles), jnp.sin(angles)
    return jnp.concatenate([cos, cos], axis=1), jnp.concatenate([-sin, sin], axis=1)


def shards(
    tokens,
    doc_starts,
    expert_ids,
    w_query,
    w_key,
    w_value,
    w_attn_out,
    w_router,
    g_attn,
    g_query,
    g_key,
    g_ffn,
    w_in,
    w_out,
    cotangent,
):
    nf, nc = lax.axis_size("fsdp"), lax.axis_size("ctx")
    ndev = nf * nc
    links = Links(nf, nc)
    frel = links.frel
    x_own, g_own = tokens[0], cotangent[0]
    tok, dim = x_own.shape
    seq = tok * nc
    width = dim // nc
    heads = H // nc
    own_rows = w_query.shape[0]
    fsdp_rows = own_rows * nc
    starts = doc_starts[0]

    by_cols = [w.reshape(own_rows, nc, width) for w in (w_query, w_key, w_value)]
    by_cols = jnp.concatenate(by_cols, axis=2).transpose(1, 0, 2)
    per_row = tok * TOP // own_rows
    small_width = -(-(E + 4 + per_row) // LANES) * LANES
    small = [w_router] + [g[:, None] for g in (g_attn, g_query, g_key, g_ffn)]
    small += [expert_ids[0].T.reshape(own_rows, per_row).astype(BF)]
    small += [jnp.zeros((own_rows, small_width - E - 4 - per_row), BF)]
    x_copies = jnp.broadcast_to(x_own, (nc,) + x_own.shape)
    g_copies = jnp.broadcast_to(g_own, (nc,) + g_own.shape)
    to_all = jnp.concatenate([w_attn_out] + small, axis=1)
    to_all = jnp.broadcast_to(to_all, (nc,) + to_all.shape)
    got = links.exchange(jnp.concatenate([by_cols, to_all], axis=2)).reshape(fsdp_rows, -1)
    cols_o = 3 * width + dim
    qkv_rows = jnp.concatenate([got[:, : 3 * width], got[:, cols_o:]], axis=1)
    w_o_rows = got[:, 3 * width : cols_o]
    qkv_begun = links.plane_start(qkv_rows)
    w_qkv = links.all_blocks(links.plane_end(qkv_begun)[0])
    group = 2
    groups = nc // group
    x_all = links.exchange(after(x_copies, got)).reshape(seq, dim)
    w_o_begun = links.plane_start(after(w_o_rows, w_qkv[-1]))
    w_o_pieces, w_o_sent = links.plane_end(w_o_begun)
    small_all = jnp.stack([w[:, 3 * width :] for w in w_qkv])
    small_all = small_all.reshape(nf, nc, own_rows, small_width)
    small_all = links.relative(small_all, planes=True).reshape(dim, small_width)
    router = jnp.where(jnp.arange(LANES) < E, small_all[:, :LANES], 0)
    gains = small_all[:, E : E + 4].T.reshape(4, 1, dim).astype(F32)
    gain_attn, gain_query, gain_key, gain_ffn = gains
    ids_all = small_all[:, E + 4 : E + 4 + per_row].astype(jnp.int32)
    ids_all = ids_all.reshape(nf, nc, TOP, tok)

    normed, raw, value, sums = call(
        functools.partial(qkv_kernel, nf),
        [
            shape((seq, dim), BF),
            shape((2, seq, width), F32),
            shape((seq, width), BF),
            shape((2, 8, seq), F32),
        ],
        3.2,
        13,
        ins=[SMEM] + [VMEM] * (2 + nf),
        gate=w_o_sent,
    )(frel, gain_attn, x_all, *w_qkv)

    w_o = links.all_blocks(w_o_pieces)
    if links.native:
        g_groups = [jnp.concatenate([g_own, links.cswap(after(g_own, sums), 1)])]
    else:
        g_groups = links.slots(g_own)
        g_groups = [jnp.concatenate(g_groups[i * group : (i + 1) * group]) for i in range(groups)]
    g_all = [lax.all_gather(g, "fsdp", axis=0) for g in g_groups]

    def columns(flat):
        return jnp.broadcast_to(flat[:, :, None], (2, seq, LANES))

    sums = jnp.sum(links.gather(sums), axis=0)[:, 0]
    inv = columns(lax.rsqrt(sums / dim + EPS))
    positions = jnp.arange(seq, dtype=jnp.int32)
    cos, sin = rotary_tables(positions)
    head_gain = jnp.stack([gain_query, gain_key]).reshape(2, nc, 1, width)
    head_gain = lax.dynamic_index_in_dim(head_gain, links.c, 1, keepdims=False)
    scale = 1.0 / math.sqrt(HD)
    docs = jnp.sum((starts[None, :] <= positions[:, None]).astype(jnp.int32), axis=1)
    allowed = (positions[None, :] <= positions[:, None]) & (docs[None, :] == docs[:, None])
    mask = allowed.astype(F32)

    def whole(*dims):
        return pl.BlockSpec(dims, lambda h: (0,) * len(dims))

    pair_spec = pl.BlockSpec((2, seq, HD), lambda h: (0, 0, h))
    head_spec = pl.BlockSpec((seq, HD), lambda h: (0, h))
    gain_spec = pl.BlockSpec((2, 1, HD), lambda h: (0, 0, h))
    table_specs = [whole(seq, HD), whole(seq, HD), whole(seq, seq)]
    low, mixed = call(
        functools.partial(attend_kernel, scale),
        [shape((2, seq, width), BF), shape((seq, width), BF)],
        0.6,
        7,
        grid=(heads,),
        ins=[pair_spec, head_spec, whole(2, seq, LANES), gain_spec] + table_specs,
        out_specs=[pair_spec, head_spec],
    )(raw, value, inv, head_gain, cos, sin, mask)
    mixed_rows = links.exchange(mixed.reshape(nc, tok, width))
    pieces = w_in.shape[0]
    halves = min(2, pieces)
    experts = pieces // halves
    device = links.f * nc + links.c
    first_expert = device * pieces // 2
    cores = links.cores
    mine = first_expert + jnp.arange(experts, dtype=jnp.int32)
    theirs = ((links.f ^ 1) * nc + links.c) * pieces // 2 + jnp.arange(experts, dtype=jnp.int32)
    both = jnp.concatenate([mine, theirs]) if cores == 2 else mine
    ids_rel = links.relative(ids_all).transpose(1, 0, 2, 3)
    before = (jnp.arange(tok)[:, None] < jnp.arange(tok)[None, :]).astype(BF)
    ranks = jnp.arange(CAP, dtype=F32)[:, None]

    def slots_of(ids, names):
        named = jnp.any(ids[:, :, None] == names[:, None, None], axis=3)
        rank = jnp.einsum("kmet,ts->kmes", named.astype(BF), before, preferred_element_type=F32)
        return (named[:, :, :, None] & (rank[:, :, :, None] == ranks)).astype(BF)

    blocks = nf // cores
    slots = slots_of(ids_rel[:, ::cores], both)
    slot_sets = [slots[:, :, :experts]]
    if cores == 2:
        slot_sets.append(slots_of(ids_rel[:, 1::2], mine))
    rows_all = experts * cores * group * CAP
    eye = jnp.eye(group, dtype=BF)[:, None, :, None]
    spread = slots.reshape(groups, group, blocks, experts * cores, CAP, tok)
    spread = spread.transpose(0, 2, 3, 1, 4, 5)[:, :, :, :, :, None] * eye
    spread = spread.reshape(groups, blocks, rows_all, group * tok)
    taking = [spread[i] for i in range(groups)]
    placing = []
    for i in range(groups if cores == 1 else 1):
        sets = jnp.stack([s[i * group : (i + 1) * group] for s in slot_sets])
        sets = sets.transpose(0, 2, 3, 1, 4, 5)[:, :, :, :, :, None] * eye
        placing.append(sets.reshape(nf, experts * group * CAP, group * tok))
    putting = [spread[i].transpose(0, 2, 1) for i in range(groups)]
    hidden, inv_ffn, moe_in, mixed_all = call(
        functools.partial(out_kernel, nf),
        [shape((tok, dim), F32), shape((tok, LANES), F32)] + [shape((tok, dim), BF)] * 2,
        1.1,
        12,
        ins=[SMEM] + [VMEM] * (3 + nf),
        gate=taking + putting + placing,
    )(frel, x_own, gain_ffn, mixed_rows, *w_o)

    part = blocks * group * CAP
    nrow = part * cores
    tile = 1024

    def tiles(*dims):
        return pl.BlockSpec(dims[:-1] + (tile,), lambda d: (0,) * (len(dims) - 1) + (d,))

    def fixed(array):
        return pl.BlockSpec(array.shape, lambda d: (0,) * array.ndim)

    def take_rows(i, entries, *gate):
        arrays = [a for entry in entries for a in entry]
        parts = call(
            functools.partial(take_kernel, [len(entry) for entry in entries], experts),
            [shape((experts, part, dim), BF)] * cores,
            1.6,
            8,
            grid=(dim // tile,),
            ins=[fixed(taking[i])] + [tiles(*a.shape) for a in arrays],
            out_specs=[tiles(experts, part, dim)] * cores,
            gate=gate,
        )(taking[i], *arrays)
        if cores == 1:
            return parts
        return [parts[0], links.swap(parts[1], 1)]

    plan, plan_rows = links.plane_plan(group * tok)

    def put_rows(i, parts, *gate):
        if cores == 2:
            parts = [parts[0], links.swap(parts[1], 1)]
        return call(
            functools.partial(put_kernel, blocks, cores, plan),
            [shape((n, dim), BF) for n in plan_rows],
            1.6,
            8,
            grid=(dim // tile,),
            ins=[fixed(putting[i])] + [tiles(experts, part, dim)] * cores,
            out_specs=[tiles(n, dim) for n in plan_rows],
            gate=gate,
        )(putting[i], *parts)

    def grouped(pieces):
        return [jnp.concatenate(pieces[i * group : (i + 1) * group]) for i in range(groups)]

    def take_placed(i, whole):
        order = [m for p in range(cores) for m in range(p, nf, cores)]
        sets = placing[i]
        places = jnp.array(order, jnp.int32)
        places = links.f ^ places if links.native else places
        return call(
            take_placed_kernel,
            shape((experts, nrow, dim), BF),
            0.8,
            12,
            spec=pltpu.PrefetchScalarGridSpec(
                num_scalar_prefetch=1,
                grid=(nf,),
                in_specs=[pl.BlockSpec((1,) + sets.shape[1:], lambda m, at: (m, 0, 0))]
                + [pl.BlockSpec((1, group * tok, dim), lambda m, at: (at[m], 0, 0))],
                out_specs=pl.BlockSpec((experts, group * CAP, dim), lambda m, at: (0, m, 0)),
            ),
        )(places, sets, whole)

    g_rows = [[take_placed(i, g)] for i, g in enumerate(g_all)]

    def pick_far(stacked):
        return [pick(stacked, links.c ^ 2), pick(stacked, links.c ^ 3)]

    if links.native:
        near = links.cswap(moe_in, 1)
        far = links.gather(moe_in, near)
        x_begun = [links.plane_start(jnp.concatenate([moe_in, near]))]
        seen, sent = links.plane_end(x_begun[0], g_rows[0][0])
        far = after(far, *sent)
        g_far = links.exchange(after(g_copies, far))
        x_begun.append(links.plane_start(jnp.concatenate(pick_far(far))))
        x_rows = [take_rows(0, seen, x_begun[1][0])]
    else:
        x_groups = grouped(links.slots(moe_in))
        x_rows = [take_rows(i, links.plane_end(links.plane_start(x))[0]) for i, x in enumerate(x_groups)]
    w_out_e = w_out.reshape(experts, halves * FH, dim)
    inner_width = halves * FH

    def by_expert(*dims):
        return pl.BlockSpec(dims, lambda j: (j,) + (0,) * (len(dims) - 1))

    dtile = 512
    n = groups * cores
    of_group = [list(range(i * cores, (i + 1) * cores)) for i in range(groups)]

    def grad_out_pieces(inners, g_rows, *gate):
        flat = [a for parts in g_rows for a in parts]
        g_parts, at = [], groups
        for parts in g_rows:
            g_parts.append(list(range(at, at + len(parts))))
            at += len(parts)
        return call(
            functools.partial(
                weight_grad_kernel,
                list(range(groups)),
                g_parts,
            ),
            shape(w_out_e.shape, F32),
            6.5,
            26,
            grid=(experts, halves),
            ins=[pl.BlockSpec((1, nrow, FH), lambda j, h: (j, 0, h))] * groups
            + [pl.BlockSpec((1, g.shape[1], dim), lambda j, h: (j, 0, 0)) for g in flat],
            out_specs=pl.BlockSpec((1, FH, dim), lambda j, h: (j, h, 0)),
            gate=gate,
        )(*inners, *flat)

    def grad_in_pieces(j, total, *gate):
        flat = [a for parts in x_rows for a in parts]
        return call(
            functools.partial(weight_grad_kernel, [n + i for i in range(groups)], of_group),
            shape(w_in.shape, F32),
            6.5,
            25,
            grid=(halves, dim // dtile),
            ins=[pl.BlockSpec((1, part, dtile), lambda p, d: (j, 0, d))] * n
            + [pl.BlockSpec((1, nrow, 2 * FH), lambda p, d: (j * halves + p, 0, 0))] * groups
            + [pl.BlockSpec(memory_space=pl.ANY)] * (j > 0),
            out_specs=pl.BlockSpec((1, dtile, 2 * FH), lambda p, d: (j * halves + p, d, 0)),
            aliases={n + groups: 0} if j else {},
            gate=gate,
        )(*flat, *dprojs, *([total] if j else []))

    def expert(i, *gate):
        rows_in = [by_expert(1, part, dim)] * cores
        return call(
            functools.partial(expert_kernel, halves, cores),
            [shape((experts, part, dim), BF)] * cores
            + [
                shape((pieces, nrow, 2 * FH), BF),
                shape((experts, nrow, inner_width), BF),
                shape((experts, nrow, LANES), F32),
            ],
            34,
            30,
            grid=(experts,),
            ins=[
                SMEM,
                pl.BlockSpec((dim, LANES), lambda j: (0, 0)),
                by_expert(halves, dim, 2 * FH),
                by_expert(1, inner_width, dim),
            ]
            + rows_in
            + [by_expert(1, g.shape[1], dim) for g in g_rows[i]],
            out_specs=rows_in
            + [
                by_expert(halves, nrow, 2 * FH),
                by_expert(1, nrow, inner_width),
                by_expert(1, nrow, LANES),
            ],
            gate=gate,
        )(first_expert.reshape(1), router, w_in, w_out_e, *x_rows[i], *g_rows[i])

    def result(inner, *gate):
        return call(
            result_kernel,
            [shape((experts, part, dim), BF)] * cores,
            3.4,
            14,
            grid=(experts,),
            ins=[by_expert(1, nrow, inner_width), by_expert(1, inner_width, dim)],
            out_specs=[by_expert(1, part, dim)] * cores,
            gate=gate,
        )(inner, w_out_e)

    def cut_group(total):
        return [total[b * tok : (b + 1) * tok] for b in range(group)]

    done, begun, more, totals = [], [], [], []
    last = x_rows[0][0]
    for i in range(groups):
        done.append(expert(i, last))
        if links.native and i == 0:
            pieces_x, sent = links.plane_end(x_begun[1], done[0][0])
            g_begun = links.plane_start(jnp.concatenate(pick_far(after(g_far, *sent))))
            arrays = put_rows(0, done[0][:cores], g_begun[0])
            x_rows.append(take_rows(1, pieces_x, arrays[0]))
            pieces_g, sent = links.plane_end(g_begun, x_rows[1][0])
            arrays = held(arrays, *sent)
            g_rows.append(take_rows(1, pieces_g))
            last = g_rows[1][0]
        elif i == 1:
            more.append(links.reduce_next(begun[0], done[1][0]))
            arrays = put_rows(1, done[1][:cores], *more[0][-2:])
            last = arrays[0]
        else:
            arrays = put_rows(i, done[i][:cores], done[i][0])
            last = arrays[0]
        begun.append(links.reduce_start(arrays))
    dgate = jnp.stack([d[cores + 2][:, :, 0] for d in done], axis=1)
    dgate = dgate.reshape(experts, groups, cores, blocks, group, CAP).transpose(2, 1, 4, 3, 0, 5)
    dgate = dgate.reshape(cores, nc, blocks, experts, CAP, 1)
    dgate_tok = jnp.stack(
        [jnp.sum(s.astype(F32) * d, axis=3) for s, d in zip(slot_sets, dgate)], axis=2
    ).reshape(nc, nf, experts, tok)
    dgate_tok = links.relative(dgate_tok.transpose(1, 0, 2, 3))
    dgate_back = lax.all_to_all(
        dgate_tok.reshape(ndev, experts, tok), ALL, split_axis=0, concat_axis=0, tiled=True
    )
    results, out_arrays, out_begun = [], [], []
    for i in range(groups):
        results.append(result(done[i][cores + 1], last))
        last = results[i][0]
    totals.append(links.reduce_end(more[0], group * tok, last))
    out_arrays.append(put_rows(0, results[0], totals[0]))
    last = out_arrays[0][0]
    for i in range(1, groups):
        more.append(links.reduce_next(begun[i], last))
        last = more[i][-1]
        out_begun.append(links.reduce_start(held(out_arrays[i - 1], last)))
        out_arrays.append(put_rows(i, results[i], last))
        last = out_arrays[i][0]
    dprojs = [d[cores] for d in done]
    inners = [d[cores + 1] for d in done]
    for i in range(1, groups):
        totals.append(links.reduce_end(more[i], group * tok, last))
        last = totals[i]
    dmoe_terms = links.sum_slots([t for total in totals for t in cut_group(total)])
    grad_w_out = grad_out_pieces(inners, g_rows, last)
    out_begun.append(links.reduce_start(held(out_arrays[-1], grad_w_out)))
    dmoe_terms = held(dmoe_terms, grad_w_out)
    dgate_back = after(dgate_back, grad_w_out)
    dprob = jnp.sum(dgate_back.reshape(E, ndev * experts // E, tok), axis=1).T
    dprob = jnp.pad(dprob, ((0, 0), (0, LANES - E)))

    back = call(
        functools.partial(hidden_back_kernel, nf, len(dmoe_terms)),
        [shape((tok, dim), F32), shape((dim, LANES), F32), shape((8, dim), F32)]
        + [shape((tok, dim), BF), shape((nc, tok, width), BF)],
        1.3,
        15,
        ins=[SMEM] + [VMEM] * (7 + len(dmoe_terms) + nf),
        scratch=[pltpu.VMEM((tok, dim), BF)],
    )(frel, hidden, inv_ffn, moe_in, g_own, gain_ffn, router, dprob, *dmoe_terms, *w_o)
    dhidden, grad_router, grad_gain_ffn, dlow, dmixed = back
    dmixed = links.exchange(dmixed)
    grad_plan, grad_rows = links.dense_plan(fsdp_rows)

    def dense_terms(left, right, extra, *gate):
        return call(
            functools.partial(place_grad_kernel, nf, grad_plan),
            [shape((r, right.shape[1] + LANES), BF) for r in grad_rows],
            right.shape[0] * right.shape[1] * dim * 2e-9,
            right.shape[1] * dim * 2e-6,
            ins=[SMEM, VMEM, VMEM, VMEM],
            gate=gate,
        )(frel, left, right, extra)

    last = dlow
    out_more = []
    for b in out_begun:
        out_more.append(links.reduce_next(b, last))
        last = out_more[-1][-1]
    grad_w_in = grad_in_pieces(0, None, last)
    last = grad_w_in
    dmixed = after(dmixed, last).reshape(seq, width)

    u, dvalue, stats, dgain = call(
        functools.partial(attend_back_kernel, scale),
        [
            shape((2, seq, width), F32),
            shape((seq, width), BF),
            shape((2, 8, seq), F32),
            shape((2, 8, width), F32),
        ],
        1.4,
        10,
        grid=(heads,),
        ins=[pair_spec, pair_spec, head_spec, whole(2, seq, LANES), gain_spec]
        + table_specs
        + [head_spec],
        out_specs=[
            pair_spec,
            head_spec,
            whole(2, 8, seq),
            pl.BlockSpec((2, 8, HD), lambda h: (0, 0, h)),
        ],
    )(raw, low, value, inv, head_gain, cos, sin, mask, dmixed)
    with_ffn = jnp.where(jnp.arange(LANES) == E, grad_gain_ffn[0][:, None], grad_router)
    grad_o_terms = dense_terms(mixed_all, dlow, with_ffn.astype(BF), stats)
    mean = columns(jnp.sum(links.gather(stats), axis=0)[:, 0] / dim)
    last = grad_o_terms[0]
    out_totals = []
    for m in out_more:
        out_totals.append(links.reduce_end(m, group * tok, last))
        last = out_totals[-1]
    out_terms = links.sum_slots([t for o in out_totals for t in cut_group(o)])
    mean = after(mean, last)
    dqkv, dnormed_terms, dgain_attn = call(
        functools.partial(dnormed_kernel, nf),
        [shape((seq, 3 * width), BF), shape((seq, dim), BF), shape((8, dim), F32)],
        3.3,
        15,
        ins=[SMEM] + [VMEM] * (6 + nf),
    )(frel, u, raw, inv, mean, dvalue, x_all, *w_qkv)
    dnormed_terms = links.exchange(dnormed_terms.reshape(nc, tok, dim))

    def placed(vector):
        return lax.dynamic_update_slice(jnp.zeros((dim,), F32), vector, (links.c * width,))

    grad_o_begun = links.dense_start(grad_o_terms, fsdp_rows, dqkv)
    gain_terms = jnp.stack([dgain_attn[0], placed(dgain[0, 0]), placed(dgain[1, 0])])
    gain_terms = jnp.pad(gain_terms.astype(BF), ((0, LANES - 3), (0, 0))).T
    grad_qkv_terms = dense_terms(normed, dqkv, gain_terms, *grad_o_begun[2:3])
    grad_qkv_begun = links.dense_start(grad_qkv_terms, fsdp_rows, grad_qkv_terms[0])
    last = grad_qkv_begun[-1]
    for j in range(1, experts):
        grad_w_in = grad_in_pieces(j, grad_w_in, last)
        last = grad_w_in
    grad_o_more = links.reduce_next(grad_o_begun, last)
    grad_qkv_more = links.reduce_next(grad_qkv_begun, grad_o_more[-1])
    out_terms = held(out_terms, grad_qkv_more[-1])
    grad_o_total = links.reduce_end(grad_o_more, fsdp_rows, out_terms[-1])
    grad_o = links.exchange(grad_o_total.reshape(nc, own_rows, -1))
    grad_qkv_total = links.reduce_end(grad_qkv_more, fsdp_rows, grad_o_total)
    dnormed_terms = after(dnormed_terms, grad_qkv_total)
    dnormed = jnp.sum(dnormed_terms.astype(F32), axis=0)
    x_float = x_own.astype(F32)
    x_inv = lax.rsqrt(jnp.mean(x_float * x_float, axis=-1, keepdims=True) + EPS)
    ux = dnormed * gain_attn
    x_mean = jnp.mean(ux * x_float, axis=-1, keepdims=True)
    input_grad = (dhidden + x_inv * ux - x_float * x_inv**3 * x_mean)[None]

    output = (hidden + sum(t.astype(F32) for t in out_terms)).astype(BF)
    grad_o = jnp.sum(grad_o.astype(F32), axis=0)
    grad_attn_out, router_sum = grad_o[:, :dim], grad_o[:, dim:]
    grad_qkv = links.exchange(grad_qkv_total.reshape(nc, own_rows, -1)).astype(F32)
    gain_sum = jnp.sum(grad_qkv[:, :, 3 * width :], axis=0).T
    grad_dense = grad_qkv[:, :, : 3 * width].reshape(nc, own_rows, 3, width).transpose(2, 1, 0, 3)
    grad_dense = grad_dense.reshape(3, own_rows, dim)
    return (
        output[None],
        input_grad,
        grad_dense[0],
        grad_dense[1],
        grad_dense[2],
        grad_attn_out,
        router_sum[:, :E],
        gain_sum[0],
        gain_sum[1],
        gain_sum[2],
        router_sum[:, E],
        grad_w_in,
        grad_w_out.reshape(w_out.shape),
    )


def solution(mesh):
    rows = P(ALL, None)
    vec = P(ALL)
    cube = P(ALL, None, None)
    stream = P("fsdp", "ctx", None)
    weights = (rows,) * 5 + (vec,) * 4 + (cube,) * 2
    return jax.shard_map(
        shards,
        mesh=mesh,
        in_specs=(stream, P("fsdp", None), stream) + weights + (stream,),
        out_specs=(stream, stream) + weights,
        check_vma=False,
    )
```

time: 1050 us -> 896 us (0.85)
  Pallas kernels: 0 us -> 238 us
  matrix products: 192 us -> 0.28 us
  waiting for transfers between devices: 418 us -> 268 us
  starting transfers between devices: 189 us -> 119 us
  local copies, waits for them, and re-layouts: 160 us -> 106 us
  blocking collectives: 0 us -> 50.1 us
  between operations: 3.81 us -> 16.2 us
    pallas_call x0 -> x56, Pallas kernels: none -> 238 us  [the longest x22 229 us: call(): return lambda *operands: made(*operands, *gate)]
    dot_general x70 -> x2, matrix products: 181 us -> 0.28 us  [slots_of(): jnp.einsum('kmet,ts->kmes', named.astype(BF), before, preferred_element_t...]
    ppermute x76 -> x61, waiting for transfers between devices: 234 us -> 134 us  [swap(): return lax.ppermute(value, 'fsdp', [(i, i ^ mask) for i in range(self.nf)])]
    ppermute x45 -> x8, waiting for transfers between devices: 162 us -> 72.3 us  [cswap(): return lax.ppermute(value, 'ctx', [(i, i ^ mask) for i in range(self.nc)])]
    ppermute x45 -> x8, starting transfers between devices: 86.4 us -> 13 us  [cswap(): return lax.ppermute(value, 'ctx', [(i, i ^ mask) for i in range(self.nc)])]
    all_to_all x0 -> x1, blocking collectives: none -> 50.1 us  [exchange(): return lax.all_to_all(value, 'ctx', split_axis=0, concat_axis=0, tiled=True)]
    all_to_all x7 -> x11, waiting for transfers between devices: 22.3 us -> 61.6 us  [the longest x10 51.1 us: exchange(): return lax.all_to_all(value, 'ctx', split_axis=0, concat_axis=0, tiled=True)]
    unnamed x252 -> x214, local copies, waits for them, and re-layouts: 59.6 us -> 33.6 us
  transfers between devices with their start and end apart: 128 -> 81, of which waited for: 43 -> 35; matrix products, arithmetic and copies ran while one was open for 33% -> 16% of each run, Pallas kernels for 0% -> 23%
where the time goes in v2:
time: 896 us; the launch traced here: 882 us
  waiting for transfers between devices  268 us (30%)
  Pallas kernels  238 us (27%)
  starting transfers between devices  119 us (13%)
  local copies, waits for them, and re-layouts  106 us (12%)
  other arithmetic  85.2 us (10%)
  blocking collectives  50.1 us (6%)
  between operations  16.2 us (2%)
    pallas_call x22, Pallas kernels, call(): return lambda *operands: made(*operands, *gate)  229 us
    ppermute x61, waiting for transfers between devices, swap(): return lax.ppermute(value, 'fsdp', [(i, i ^ mask) for i in range(self.nf)])  134 us
    ppermute x8, waiting for transfers between devices, cswap(): return lax.ppermute(value, 'ctx', [(i, i ^ mask) for i in range(self.nc)])  72.3 us
    all_to_all x10, starting transfers between devices, exchange(): return lax.all_to_all(value, 'ctx', split_axis=0, concat_axis=0, tiled=True)  51.7 us
    all_to_all x10, waiting for transfers between devices, exchange(): return lax.all_to_all(value, 'ctx', split_axis=0, concat_axis=0, tiled=True)  51.1 us
    ppermute x61, starting transfers between devices, swap(): return lax.ppermute(value, 'fsdp', [(i, i ^ mask) for i in range(self.nf)])  50.6 us
    all_to_all x1, blocking collectives, exchange(): return lax.all_to_all(value, 'ctx', split_axis=0, concat_axis=0, tiled=True)  50.1 us
    convert_element_type x20, other arithmetic, add_low(): return sum((t.astype(F32) for t in terms)).astype(BF)  46.6 us
  transfers between devices with their start and end apart: 81, of which 35 were waited for; matrix products, arithmetic and copies ran while one was open for 16% of the time, Pallas kernels for 23%

profile of v2, /device:TPU:0, one launch (start us, length us, event | category | flops | bytes accessed | tf_op | source)
XLA Modules:
  0.0 882.2 jit_solution(14173789201040200162)
XLA Ops:
  13.6 50.1 %all_to_all.60 = bf16[4,64,3712]{2,1,0:T(8,128)(2,1)S(1)} all-to-all(bf16[4,64,3712]{2,1,0:T(8,128)(2,1)S(1)} %pad_maximum_fusion), channel_id=1, replica_groups=mesh['fsdp'=8,'ctx'=4] {'ctx'}, dimensions={0} | all-to-all | bytes 3801088 | tf_op jit(solution)/shard_map/all_to_all | solution.py:78
  76.3 8.6 collective-permute-done.3.refs_7_.refs_11_
  110.6 15.7 %collective-permute-done.8.refs_8_.refs_16_ = bf16[256,2048]{1,0:T(8,128)(2,1)} collective-permute-done((bf16[256,2048]{1,0:T(8,128)(2,1)}, bf16[256,2048]{1,0:T(8,128)(2,1)}, u32[]{:S(2)}, u32[]{:S(2)}) %collective-permute-start.8) | collective-permute-done | bytes 1048608 | tf_op jit(solution)/shard_map/ppermute | solution.py:72
  131.4 9.6 %shard_map.257 = (bf16[512,2048]{1,0:T(8,128)(2,1)}, f32[2,512,512]{2,1,0:T(8,128)}, bf16[512,512]{1,0:T(8,128)(2,1)}, f32[2,8,512]{2,1,0:T(8,128)}) custom-call(s32[8]{0:T(128)} %iota_xor_fusion.refs_0_, f32[1,2048]{1,0:T(1,128)} %copy.312.refs_1_, bf16[512,2048]{1,0:T(8,128)(2,1)} %bitcast.266, bf16[256,1664]{1,0:T(8,128)(2,1)} %pad_maximum_fusion.9.refs_3_.refs_7_, ...), custom_call_target="tpu_custom_call" | custom-call | flops 160000000 | bytes 650000 | tf_op jit(solution)/shard_map/pallas_call | solution.py:232
  141.0 13.3 %collective-permute-done.19 = bf16[128,2048]{1,0:T(8,128)(2,1)S(1)} collective-permute-done((bf16[128,2048]{1,0:T(8,128)(2,1)}, bf16[128,2048]{1,0:T(8,128)(2,1)S(1)}, u32[]{:S(2)}, u32[]{:S(2)}) %collective-permute-start.19) | collective-permute-done | bytes 524320 | tf_op jit(solution)/shard_map/ppermute | solution.py:75
  176.2 4.7 all-to-all-done.2
  181.5 5.5 collective-permute-done.13
  191.3 7.1 shard_map.258
  198.4 4.6 all-to-all-start.3
  212.9 5.3 all-to-all-done.3.refs_3_
  218.2 6.2 shard_map.259
  224.4 13.4 %collective-permute-done.16.refs_1_ = bf16[128,2048]{1,0:T(8,128)(2,1)S(1)} collective-permute-done((bf16[128,2048]{1,0:T(8,128)(2,1)}, bf16[128,2048]{1,0:T(8,128)(2,1)S(1)}, u32[]{:S(2)}, u32[]{:S(2)}) %collective-permute-start.16) | collective-permute-done | bytes 524320 | tf_op jit(solution)/shard_map/ppermute | solution.py:75
  248.5 9.0 %shard_map.261.refs_2_.refs_6_ = bf16[2,384,2048]{2,1,0:T(8,128)(2,1)} custom-call(s32[8]{0:T(128)} %broadcast_xor_fusion.places, bf16[8,96,256]{2,1,0:T(8,128)(2,1)} %broadcast_multiply_fusion.1.refs_16_.slots, bf16[8,256,2048]{2,1,0:T(8,128)(2,1)} %bitcast.279), custom_call_target="tpu_custom_call" | custom-call | flops 40000000 | bytes 600000 | tf_op jit(solution)/shard_map/pallas_call | solution.py:697
  257.5 12.3 %collective-permute-done.17.refs_0_ = bf16[256,2048]{1,0:T(8,128)(2,1)S(1)} collective-permute-done((bf16[256,2048]{1,0:T(8,128)(2,1)}, bf16[256,2048]{1,0:T(8,128)(2,1)S(1)}, u32[]{:S(2)}, u32[]{:S(2)}) %collective-permute-start.17) | collective-permute-done | bytes 1048608 | tf_op jit(solution)/shard_map/ppermute | solution.py:72
  274.6 16.8 %all-to-all-done.4.refs_0_ = bf16[4,128,2048]{2,1,0:T(8,128)(2,1)S(1)} async-done(((bf16[4,128,2048]{2,1,0:T(8,128)(2,1)}), bf16[4,128,2048]{2,1,0:T(8,128)(2,1)S(1)}, u32[]{:S(2)}, u32[]{:S(2)}) %all-to-all-start.4) | async-done | bytes 2097184 | tf_op jit(solution)/shard_map/all_to_all | solution.py:78
  294.5 4.9 all-to-all-start.5
  302.5 10.1 %collective-permute-done.20.refs_4_ = bf16[128,2048]{1,0:T(8,128)(2,1)} collective-permute-done((bf16[128,2048]{1,0:T(8,128)(2,1)}, bf16[128,2048]{1,0:T(8,128)(2,1)}, u32[]{:S(2)}, u32[]{:S(2)}) %collective-permute-start.20) | collective-permute-done | bytes 524320 | tf_op jit(solution)/shard_map/ppermute | solution.py:72
  321.9 32.1 %shard_map.266 = (bf16[2,192,2048]{2,1,0:T(8,128)(2,1)}, bf16[2,192,2048]{2,1,0:T(8,128)(2,1)}, bf16[4,384,1024]{2,1,0:T(8,128)(2,1)}, bf16[2,384,1024]{2,1,0:T(8,128)(2,1)}, f32[2,384,128]{2,1,0:T(8,128)}) custom-call(s32[1]{0:T(128)} %bitcast.64.refs_0_, bf16[2048,128]{1,0:T(8,128)(2,1)} %get-tuple-element.256.refs_1_.refs_6_, ...), custom_call_target="tpu_custom_call" | custom-call | flops 1700000000 | bytes 1500000 | tf_op jit(solution)/shard_map/pallas_call | solution.py:232
  363.6 4.3 shard_map.270
  367.9 28.3 %collective-permute-done.25.refs_4_ = bf16[128,2048]{1,0:T(8,128)(2,1)S(1)} collective-permute-done((bf16[128,2048]{1,0:T(8,128)(2,1)S(1)}, bf16[128,2048]{1,0:T(8,128)(2,1)S(1)}, u32[]{:S(2)}, u32[]{:S(2)}) %collective-permute-start.25) | collective-permute-done | bytes 524320 | tf_op jit(solution)/shard_map/ppermute | solution.py:72
  407.4 10.7 %collective-permute-done.31.refs_4_ = bf16[128,2048]{1,0:T(8,128)(2,1)S(1)} collective-permute-done((bf16[128,2048]{1,0:T(8,128)(2,1)S(1)}, bf16[128,2048]{1,0:T(8,128)(2,1)S(1)}, u32[]{:S(2)}, u32[]{:S(2)}) %collective-permute-start.31) | collective-permute-done | bytes 524320 | tf_op jit(solution)/shard_map/ppermute | solution.py:72
  419.9 4.4 shard_map.273
  430.3 32.2 %shard_map.274 = (bf16[2,192,2048]{2,1,0:T(8,128)(2,1)}, bf16[2,192,2048]{2,1,0:T(8,128)(2,1)}, bf16[4,384,1024]{2,1,0:T(8,128)(2,1)}, bf16[2,384,1024]{2,1,0:T(8,128)(2,1)}, f32[2,384,128]{2,1,0:T(8,128)}) custom-call(s32[1]{0:T(128)} %bitcast.64.refs_0_, bf16[2048,128]{1,0:T(8,128)(2,1)} %get-tuple-element.256.refs_1_.refs_6_, ...), custom_call_target="tpu_custom_call" | custom-call | flops 1700000000 | bytes 1500000 | tf_op jit(solution)/shard_map/pallas_call | solution.py:232
  471.6 4.3 shard_map.277
  475.9 7.2 shard_map.278
  485.7 7.5 shard_map.279
  504.1 4.9 collective-permute-done.40.refs_0_
  543.3 15.6 %shard_map.286.refs_1_.refs_4_.refs_5_ = f32[2,1024,2048]{2,1,0:T(8,128)} custom-call(bf16[2,384,1024]{2,1,0:T(8,128)(2,1)} %get-tuple-element.142.refs_0_, bf16[2,384,1024]{2,1,0:T(8,128)(2,1)} %get-tuple-element.170.refs_0_.refs_1_, bf16[2,384,2048]{2,1,0:T(8,128)(2,1)} %shard_map.261.refs_2_.refs_6_, ...), custom_call_target="tpu_custom_call" | custom-call | flops 325000000 | bytes 1300000 | tf_op jit(solution)/shard_map/pallas_call | solution.py:232
  560.7 8.3 collective-permute-done.48.refs_2_
  569.3 10.5 %all-to-all-done.6.refs_0_ = f32[32,2,128]{2,1,0:T(2,128)S(1)} async-done(((f32[32,2,128]{2,1,0:T(2,128)}), f32[32,2,128]{2,1,0:T(2,128)S(1)}, u32[]{:S(2)}, u32[]{:S(2)}) %all-to-all-start.6) | async-done | bytes 32800 | tf_op jit(solution)/shard_map/all_to_all | solution.py:849
  581.9 10.0 %shard_map.289 = (f32[128,2048]{1,0:T(8,128)}, f32[2048,128]{1,0:T(8,128)}, f32[8,2048]{1,0:T(8,128)}, bf16[128,2048]{1,0:T(8,128)(2,1)}, bf16[4,128,512]{2,1,0:T(8,128)(2,1)}) custom-call(s32[8]{0:T(128)} %iota_xor_fusion.refs_0_, f32[128,2048]{1,0:T(8,128)} %get-tuple-element.136.refs_1_, f32[128,128]{1,0:T(8,128)} %get-tuple-element.185.refs_2_, ...), custom_call_target="tpu_custom_call" | custom-call | flops 65000000 | bytes 750000 | tf_op jit(solution)/shard_map/pallas_call | solution.py:232
  591.9 5.0 all-to-all-start.7
  606.5 16.6 %shard_map.293.refs_1_.refs_6_ = f32[4,2048,1024]{2,1,0:T(8,128)} custom-call(bf16[2,192,2048]{2,1,0:T(8,128)(2,1)} %get-tuple-element.140.refs_4_.refs_7_.refs_0_, bf16[2,192,2048]{2,1,0:T(8,128)(2,1)} %copy-done.8, bf16[2,192,2048]{2,1,0:T(8,128)(2,1)} %get-tuple-element.148.refs_2_.refs_4_, bf16[2,192,2048]{2,1,0:T(8,128)(2,1)} %copy-done.9, ...), custom_call_target="tpu_custom_call" | custom-call | flops 325000000 | bytes 1250000 | tf_op jit(solution)/shard_map/pallas_call | solution.py:232
  623.9 11.5 %shard_map.295 = (f32[2,512,512]{2,1,0:T(8,128)}, bf16[512,512]{1,0:T(8,128)(2,1)}, f32[2,8,512]{2,1,0:T(8,128)}, f32[2,8,512]{2,1,0:T(8,128)}) custom-call(f32[2,512,512]{2,1,0:T(8,128)} %get-tuple-element.132.refs_0_.refs_2_, bf16[2,512,512]{2,1,0:T(8,128)(2,1)} %get-tuple-element.207.refs_1_, bf16[512,512]{1,0:T(8,128)(2,1)} %get-tuple-element.133.refs_1_.refs_2_, ...), custom_call_target="tpu_custom_call" | custom-call | flops 70000000 | bytes 500000 | tf_op jit(solution)/shard_map/pallas_call | solution.py:232
  635.5 7.3 shard_map.296
  650.5 5.3 all-to-all-start.8
  676.4 11.1 %shard_map.300 = (bf16[512,1536]{1,0:T(8,128)(2,1)}, bf16[512,2048]{1,0:T(8,128)(2,1)}, f32[8,2048]{1,0:T(8,128)}) custom-call(s32[8]{0:T(128)} %iota_xor_fusion.refs_0_, f32[2,512,512]{2,1,0:T(8,128)} %get-tuple-element.229.refs_1_, f32[2,512,512]{2,1,0:T(8,128)} %get-tuple-element.132.refs_0_.refs_2_, f32[2,512,128]{2,1,0:T(8,128)} %broadcast_in_dim.100.refs_2_.refs_3_, ...), custom_call_target="tpu_custom_call" | custom-call | flops 165000000 | bytes 750000 | tf_op jit(solution)/shard_map/pallas_call | solution.py:232
  691.8 8.3 shard_map.302
  700.1 5.0 add_convert_fusion
  707.7 5.3 all-to-all-start.9
  718.8 16.6 %shard_map.304.refs_2_ = f32[4,2048,1024]{2,1,0:T(8,128)} custom-call(bf16[2,192,2048]{2,1,0:T(8,128)(2,1)} %get-tuple-element.140.refs_4_.refs_7_.refs_0_, bf16[2,192,2048]{2,1,0:T(8,128)(2,1)} %copy-done.8, bf16[2,192,2048]{2,1,0:T(8,128)(2,1)} %get-tuple-element.148.refs_2_.refs_4_, ...), custom_call_target="tpu_custom_call", output_to_operand_aliasing={{}: (6, {})} | custom-call | flops 325000000 | bytes 1250000 | tf_op jit(solution)/shard_map/pallas_call | solution.py:232
  745.4 5.5 collective-permute-done.61.refs_0_
  758.9 8.3 collective-permute-done.54.refs_1_
  767.2 28.9 %collective-permute-done.57.refs_2_ = bf16[128,2048]{1,0:T(8,128)(2,1)} collective-permute-done((bf16[128,2048]{1,0:T(8,128)(2,1)}, bf16[128,2048]{1,0:T(8,128)(2,1)}, u32[]{:S(2)}, u32[]{:S(2)}) %collective-permute-start.57) | collective-permute-done | bytes 524320 | tf_op jit(solution)/shard_map/ppermute | solution.py:75
  801.3 11.9 %all-to-all-start.11 = ((bf16[4,64,2176]{2,1,0:T(8,128)(2,1)}), bf16[4,64,2176]{2,1,0:T(8,128)(2,1)}, u32[]{:S(2)}, u32[]{:S(2)}) async-start(bf16[4,64,2176]{2,1,0:T(8,128)(2,1)} %bitcast.118), calls=%async_computation.11 | async-start | bytes 2228224 | tf_op jit(solution)/shard_map/all_to_all | solution.py:78
  817.4 7.2 collective-permute-done.65.refs_0_
  831.3 8.7 all-to-all-done.11
  849.2 15.6 %all-to-all-done.10 = bf16[4,64,1664]{2,1,0:T(8,128)(2,1)S(1)} async-done(((bf16[4,64,1664]{2,1,0:T(8,128)(2,1)}), bf16[4,64,1664]{2,1,0:T(8,128)(2,1)S(1)}, u32[]{:S(2)}, u32[]{:S(2)}) %all-to-all-start.10) | async-done | bytes 852000 | tf_op jit(solution)/shard_map/all_to_all | solution.py:78
  (596 shorter events, 310.1 us)
Async XLA Ops:
  71.7 58.3 %all-to-all-start.1 = ((bf16[4,128,2048]{2,1,0:T(8,128)(2,1)}), bf16[4,128,2048]{2,1,0:T(8,128)(2,1)S(1)}, u32[]{:S(2)}, u32[]{:S(2)}) async-start(bf16[4,128,2048]{2,1,0:T(8,128)(2,1)} %shard_map.255), calls=%async_computation.1 | async-start | bytes 4194304 | tf_op jit(solution)/shard_map/all_to_all | solution.py:78
  75.4 173.1 %all-gather.3.cloned.1.call-start = ((), (), s32[]{:S(2)}) async-start(), calls=%async_computation.12 | async-start | bytes 9437184 | tf_op jit(solution)/shard_map/all_gather | solution.py:570
  100.7 25.5 %collective-permute-start.8 = (bf16[256,2048]{1,0:T(8,128)(2,1)}, bf16[256,2048]{1,0:T(8,128)(2,1)}, u32[]{:S(2)}, u32[]{:S(2)}) collective-permute-start(bf16[256,2048]{1,0:T(8,128)(2,1)} %shard_map.256.refs_4_.refs_12_), channel_id=1, source_target_pairs={{0,16},{4,20},{8,24},{12,28},{16,0},{20,4},{24,8},{28,12},{1,17},{... | collective-permute-start | bytes 3145736 | tf_op jit(solution)/shard_map/ppermute | solution.py:72
  102.2 25.9 %collective-permute-start.9 = (bf16[256,2048]{1,0:T(8,128)(2,1)}, bf16[256,2048]{1,0:T(8,128)(2,1)}, u32[]{:S(2)}, u32[]{:S(2)}) collective-permute-start(bf16[256,2048]{1,0:T(8,128)(2,1)} %shard_map.256.refs_4_.refs_12_), channel_id=1, source_target_pairs={{0,8},{4,12},{8,0},{12,4},{16,24},{20,28},{24,16},{28,20},{1,9},{5... | collective-permute-start | bytes 3145736 | tf_op jit(solution)/shard_map/ppermute | solution.py:72
  164.6 48.3 %collective-permute-start.10 = (bf16[256,2048]{1,0:T(8,128)(2,1)S(1)}, bf16[256,2048]{1,0:T(8,128)(2,1)}, u32[]{:S(2)}, u32[]{:S(2)}) collective-permute-start(bf16[256,2048]{1,0:T(8,128)(2,1)S(1)} %copy-done.5), channel_id=1, source_target_pairs={{0,4},{4,0},{8,12},{12,8},{16,20},{20,16},{24,28},{28,24},{1,5},{5... | collective-permute-start | bytes 3145736 | tf_op jit(solution)/shard_map/ppermute | solution.py:72
  175.7 42.5 %collective-permute-start.11 = (bf16[256,2048]{1,0:T(8,128)(2,1)}, bf16[256,2048]{1,0:T(8,128)(2,1)}, u32[]{:S(2)}, u32[]{:S(2)}) collective-permute-start(bf16[256,2048]{1,0:T(8,128)(2,1)} %collective-permute-done.9.refs_6_.refs_14_), channel_id=1, source_target_pairs={{0,4},{4,0},{8,12},{12,8},{16,20},{20,16},{24,28},{28,24},{1,5},{5... | collective-permute-start | bytes 3145736 | tf_op jit(solution)/shard_map/ppermute | solution.py:72
  175.7 42.5 %collective-permute-start.12 = (bf16[256,2048]{1,0:T(8,128)(2,1)}, bf16[256,2048]{1,0:T(8,128)(2,1)}, u32[]{:S(2)}, u32[]{:S(2)}) collective-permute-start(bf16[256,2048]{1,0:T(8,128)(2,1)} %collective-permute-done.8.refs_8_.refs_16_), channel_id=1, source_target_pairs={{0,4},{4,0},{8,12},{12,8},{16,20},{20,16},{24,28},{28,24},{1,5},{5... | collective-permute-start | bytes 3145736 | tf_op jit(solution)/shard_map/ppermute | solution.py:72
  189.4 28.8 %collective-permute-start.15 = (bf16[256,2048]{1,0:T(8,128)(2,1)S(1)}, bf16[256,2048]{1,0:T(8,128)(2,1)}, u32[]{:S(2)}, u32[]{:S(2)}) collective-permute-start(bf16[256,2048]{1,0:T(8,128)(2,1)S(1)} %constant_dynamic-update-slice_fusion.2.refs_10_.refs_18_), channel_id=1, source_target_pairs={{0,4},{4,0},{8,12},{12,8},{16,20},{20,16},{24,28},{28,24},{1,5},{5... | collective-permute-start | bytes 3145736 | tf_op jit(solution)/shard_map/ppermute | solution.py:72
  240.7 50.8 %all-to-all-start.4 = ((bf16[4,128,2048]{2,1,0:T(8,128)(2,1)}), bf16[4,128,2048]{2,1,0:T(8,128)(2,1)S(1)}, u32[]{:S(2)}, u32[]{:S(2)}) async-start(bf16[4,128,2048]{2,1,0:T(8,128)(2,1)} %shard_map.263), calls=%async_computation.4 | async-start | bytes 4194304 | tf_op jit(solution)/shard_map/all_to_all | solution.py:78
  246.1 23.7 %collective-permute-start.17 = (bf16[256,2048]{1,0:T(8,128)(2,1)}, bf16[256,2048]{1,0:T(8,128)(2,1)S(1)}, u32[]{:S(2)}, u32[]{:S(2)}) collective-permute-start(bf16[256,2048]{1,0:T(8,128)(2,1)} %constant_dynamic-update-slice_fusion.4.refs_1_), channel_id=1, source_target_pairs={{0,8},{4,12},{8,0},{12,4},{16,24},{20,28},{24,16},{28,20},{1,9},{5... | collective-permute-start | bytes 3145736 | tf_op jit(solution)/shard_map/ppermute | solution.py:72
  246.9 23.5 %collective-permute-start.18 = (bf16[256,2048]{1,0:T(8,128)(2,1)}, bf16[256,2048]{1,0:T(8,128)(2,1)}, u32[]{:S(2)}, u32[]{:S(2)}) collective-permute-start(bf16[256,2048]{1,0:T(8,128)(2,1)} %constant_dynamic-update-slice_fusion.4.refs_1_), channel_id=1, source_target_pairs={{0,16},{4,20},{8,24},{12,28},{16,0},{20,4},{24,8},{28,12},{1,17},{... | collective-permute-start | bytes 3145736 | tf_op jit(solution)/shard_map/ppermute | solution.py:72
  294.5 63.5 %all-to-all-start.5 = ((bf16[4,128,2048]{2,1,0:T(8,128)(2,1)}), bf16[4,128,2048]{2,1,0:T(8,128)(2,1)}, u32[]{:S(2)}, u32[]{:S(2)}) async-start(bf16[4,128,2048]{2,1,0:T(8,128)(2,1)} %shard_map.268), calls=%async_computation.5 | async-start | bytes 4194304 | tf_op jit(solution)/shard_map/all_to_all | solution.py:78
  317.1 37.1 %collective-permute-start.23 = (bf16[256,2048]{1,0:T(8,128)(2,1)S(1)}, bf16[256,2048]{1,0:T(8,128)(2,1)}, u32[]{:S(2)}, u32[]{:S(2)}) collective-permute-start(bf16[256,2048]{1,0:T(8,128)(2,1)S(1)} %copy-done.11), channel_id=1, source_target_pairs={{0,8},{4,12},{8,0},{12,4},{16,24},{20,28},{24,16},{28,20},{1,9},{5... | collective-permute-start | bytes 3145736 | tf_op jit(solution)/shard_map/ppermute | solution.py:72
  318.4 35.8 %collective-permute-start.24 = (bf16[256,2048]{1,0:T(8,128)(2,1)S(1)}, bf16[256,2048]{1,0:T(8,128)(2,1)}, u32[]{:S(2)}, u32[]{:S(2)}) collective-permute-start(bf16[256,2048]{1,0:T(8,128)(2,1)S(1)} %copy-done.11), channel_id=1, source_target_pairs={{0,16},{4,20},{8,24},{12,28},{16,0},{20,4},{24,8},{28,12},{1,17},{... | collective-permute-start | bytes 3145736 | tf_op jit(solution)/shard_map/ppermute | solution.py:72
  359.4 42.0 %collective-permute-start.29 = (bf16[256,2048]{1,0:T(8,128)(2,1)S(1)}, bf16[256,2048]{1,0:T(8,128)(2,1)S(1)}, u32[]{:S(2)}, u32[]{:S(2)}) collective-permute-start(bf16[256,2048]{1,0:T(8,128)(2,1)S(1)} %pad_maximum_fusion.4.refs_3_.refs_1_), channel_id=1, source_target_pairs={{0,8},{4,12},{8,0},{12,4},{16,24},{20,28},{24,16},{28,20},{1,9},{5... | collective-permute-start | bytes 3145736 | tf_op jit(solution)/shard_map/ppermute | solution.py:72
  360.8 40.7 %collective-permute-start.30 = (bf16[256,2048]{1,0:T(8,128)(2,1)S(1)}, bf16[256,2048]{1,0:T(8,128)(2,1)}, u32[]{:S(2)}, u32[]{:S(2)}) collective-permute-start(bf16[256,2048]{1,0:T(8,128)(2,1)S(1)} %pad_maximum_fusion.4.refs_3_.refs_1_), channel_id=1, source_target_pairs={{0,16},{4,20},{8,24},{12,28},{16,0},{20,4},{24,8},{28,12},{1,17},{... | collective-permute-start | bytes 3145736 | tf_op jit(solution)/shard_map/ppermute | solution.py:72
  362.3 33.9 %collective-permute-start.25 = (bf16[128,2048]{1,0:T(8,128)(2,1)S(1)}, bf16[128,2048]{1,0:T(8,128)(2,1)S(1)}, u32[]{:S(2)}, u32[]{:S(2)}) collective-permute-start(bf16[128,2048]{1,0:T(8,128)(2,1)S(1)} %copy-done.64), channel_id=1, source_target_pairs={{0,8},{4,12},{8,0},{12,4},{16,24},{20,28},{24,16},{28,20},{1,9},{5... | collective-permute-start | bytes 1572872 | tf_op jit(solution)/shard_map/ppermute | solution.py:72
  362.8 34.5 %collective-permute-start.26 = (bf16[128,2048]{1,0:T(8,128)(2,1)S(1)}, bf16[128,2048]{1,0:T(8,128)(2,1)}, u32[]{:S(2)}, u32[]{:S(2)}) collective-permute-start(bf16[128,2048]{1,0:T(8,128)(2,1)S(1)} %copy-done.63), channel_id=1, source_target_pairs={{0,16},{4,20},{8,24},{12,28},{16,0},{20,4},{24,8},{28,12},{1,17},{... | collective-permute-start | bytes 1572872 | tf_op jit(solution)/shard_map/ppermute | solution.py:72
  424.5 40.7 %collective-permute-start.35 = (bf16[256,2048]{1,0:T(8,128)(2,1)}, bf16[256,2048]{1,0:T(8,128)(2,1)}, u32[]{:S(2)}, u32[]{:S(2)}) collective-permute-start(bf16[256,2048]{1,0:T(8,128)(2,1)} %get-tuple-element.161), channel_id=1, source_target_pairs={{0,8},{4,12},{8,0},{12,4},{16,24},{20,28},{24,16},{28,20},{1,9},{5... | collective-permute-start | bytes 3145736 | tf_op jit(solution)/shard_map/ppermute | solution.py:72
  425.6 39.6 %collective-permute-start.36 = (bf16[256,2048]{1,0:T(8,128)(2,1)}, bf16[256,2048]{1,0:T(8,128)(2,1)}, u32[]{:S(2)}, u32[]{:S(2)}) collective-permute-start(bf16[256,2048]{1,0:T(8,128)(2,1)} %get-tuple-element.162), channel_id=1, source_target_pairs={{0,16},{4,20},{8,24},{12,28},{16,0},{20,4},{24,8},{28,12},{1,17},{... | collective-permute-start | bytes 3145736 | tf_op jit(solution)/shard_map/ppermute | solution.py:72
  467.4 25.9 %collective-permute-start.39 = (bf16[128,2048]{1,0:T(8,128)(2,1)S(1)}, bf16[128,2048]{1,0:T(8,128)(2,1)S(1)}, u32[]{:S(2)}, u32[]{:S(2)}) collective-permute-start(bf16[128,2048]{1,0:T(8,128)(2,1)S(1)} %add_convert_fusion.27.refs_4_), channel_id=1, source_target_pairs={{0,8},{4,12},{8,0},{12,4},{16,24},{20,28},{24,16},{28,20},{1,9},{5... | collective-permute-start | bytes 1572872 | tf_op jit(solution)/shard_map/ppermute | solution.py:72
  469.6 23.7 %collective-permute-start.38 = (bf16[128,2048]{1,0:T(8,128)(2,1)S(1)}, bf16[128,2048]{1,0:T(8,128)(2,1)}, u32[]{:S(2)}, u32[]{:S(2)}) collective-permute-start(bf16[128,2048]{1,0:T(8,128)(2,1)S(1)} %add_convert_fusion.28.refs_3_), channel_id=1, source_target_pairs={{0,16},{4,20},{8,24},{12,28},{16,0},{20,4},{24,8},{28,12},{1,17},{... | collective-permute-start | bytes 1572872 | tf_op jit(solution)/shard_map/ppermute | solution.py:72
  483.3 25.7 %collective-permute-start.40 = (bf16[256,2048]{1,0:T(8,128)(2,1)}, bf16[256,2048]{1,0:T(8,128)(2,1)S(1)}, u32[]{:S(2)}, u32[]{:S(2)}) collective-permute-start(bf16[256,2048]{1,0:T(8,128)(2,1)} %get-tuple-element.166.refs_2_), channel_id=1, source_target_pairs={{0,8},{4,12},{8,0},{12,4},{16,24},{20,28},{24,16},{28,20},{1,9},{5... | collective-permute-start | bytes 3145736 | tf_op jit(solution)/shard_map/ppermute | solution.py:72
  484.4 25.4 %collective-permute-start.41 = (bf16[256,2048]{1,0:T(8,128)(2,1)}, bf16[256,2048]{1,0:T(8,128)(2,1)}, u32[]{:S(2)}, u32[]{:S(2)}) collective-permute-start(bf16[256,2048]{1,0:T(8,128)(2,1)} %get-tuple-element.180), channel_id=1, source_target_pairs={{0,16},{4,20},{8,24},{12,28},{16,0},{20,4},{24,8},{28,12},{1,17},{... | collective-permute-start | bytes 3145736 | tf_op jit(solution)/shard_map/ppermute | solution.py:72
  493.3 25.2 %collective-permute-start.46 = (bf16[2,192,2048]{2,1,0:T(8,128)(2,1)}, bf16[2,192,2048]{2,1,0:T(8,128)(2,1)}, u32[]{:S(2)}, u32[]{:S(2)}) collective-permute-start(bf16[2,192,2048]{2,1,0:T(8,128)(2,1)} %get-tuple-element.191), channel_id=1, source_target_pairs={{0,4},{4,0},{8,12},{12,8},{16,20},{20,16},{24,28},{28,24},{1,5},{5... | collective-permute-start | bytes 4718600 | tf_op jit(solution)/shard_map/ppermute | solution.py:72
  515.8 43.1 %collective-permute-start.47 = (bf16[128,2048]{1,0:T(8,128)(2,1)}, bf16[128,2048]{1,0:T(8,128)(2,1)S(1)}, u32[]{:S(2)}, u32[]{:S(2)}) collective-permute-start(bf16[128,2048]{1,0:T(8,128)(2,1)} %get-tuple-element.285), channel_id=1, source_target_pairs={{0,1},{1,0},{2,3},{3,2},{4,5},{5,4},{6,7},{7,6},{8,9},{9,8},{10,11... | collective-permute-start | bytes 1572872 | tf_op jit(solution)/shard_map/ppermute | solution.py:75
  517.6 80.2 %collective-permute-start.42 = (bf16[256,2048]{1,0:T(8,128)(2,1)}, bf16[256,2048]{1,0:T(8,128)(2,1)S(1)}, u32[]{:S(2)}, u32[]{:S(2)}) collective-permute-start(bf16[256,2048]{1,0:T(8,128)(2,1)} %get-tuple-element.183), channel_id=1, source_target_pairs={{0,8},{4,12},{8,0},{12,4},{16,24},{20,28},{24,16},{28,20},{1,9},{5... | collective-permute-start | bytes 3145736 | tf_op jit(solution)/shard_map/ppermute | solution.py:72
  518.5 79.3 %collective-permute-start.43 = (bf16[256,2048]{1,0:T(8,128)(2,1)}, bf16[256,2048]{1,0:T(8,128)(2,1)}, u32[]{:S(2)}, u32[]{:S(2)}) collective-permute-start(bf16[256,2048]{1,0:T(8,128)(2,1)} %get-tuple-element.184), channel_id=1, source_target_pairs={{0,16},{4,20},{8,24},{12,28},{16,0},{20,4},{24,8},{28,12},{1,17},{... | collective-permute-start | bytes 3145736 | tf_op jit(solution)/shard_map/ppermute | solution.py:72
  532.8 36.2 %collective-permute-start.48 = (bf16[128,2048]{1,0:T(8,128)(2,1)}, bf16[128,2048]{1,0:T(8,128)(2,1)S(1)}, u32[]{:S(2)}, u32[]{:S(2)}) collective-permute-start(bf16[128,2048]{1,0:T(8,128)(2,1)} %get-tuple-element.282), channel_id=1, source_target_pairs={{0,2},{1,3},{2,0},{3,1},{4,6},{5,7},{6,4},{7,5},{8,10},{9,11},{10,... | collective-permute-start | bytes 1572872 | tf_op jit(solution)/shard_map/ppermute | solution.py:75
  535.5 46.4 %collective-permute-start.49 = (bf16[128,2048]{1,0:T(8,128)(2,1)}, bf16[128,2048]{1,0:T(8,128)(2,1)}, u32[]{:S(2)}, u32[]{:S(2)}) collective-permute-start(bf16[128,2048]{1,0:T(8,128)(2,1)} %get-tuple-element.283), channel_id=1, source_target_pairs={{0,3},{1,2},{2,1},{3,0},{4,7},{5,6},{6,5},{7,4},{8,11},{9,10},{10,... | collective-permute-start | bytes 1572872 | tf_op jit(solution)/shard_map/ppermute | solution.py:75
  537.7 42.1 %all-to-all-start.6 = ((f32[32,2,128]{2,1,0:T(2,128)}), f32[32,2,128]{2,1,0:T(2,128)S(1)}, u32[]{:S(2)}, u32[]{:S(2)}) async-start(f32[32,2,128]{2,1,0:T(2,128)} %fusion.39), calls=%async_computation.6 | async-start | bytes 65536 | tf_op jit(solution)/shard_map/all_to_all | solution.py:849
  558.9 44.3 %collective-permute-start.52 = (bf16[256,2048]{1,0:T(8,128)(2,1)}, bf16[256,2048]{1,0:T(8,128)(2,1)S(1)}, u32[]{:S(2)}, u32[]{:S(2)}) collective-permute-start(bf16[256,2048]{1,0:T(8,128)(2,1)} %get-tuple-element.216), channel_id=1, source_target_pairs={{0,8},{4,12},{8,0},{12,4},{16,24},{20,28},{24,16},{28,20},{1,9},{5... | collective-permute-start | bytes 3145736 | tf_op jit(solution)/shard_map/ppermute | solution.py:72
  569.0 34.1 %collective-permute-start.53 = (bf16[256,2048]{1,0:T(8,128)(2,1)}, bf16[256,2048]{1,0:T(8,128)(2,1)}, u32[]{:S(2)}, u32[]{:S(2)}) collective-permute-start(bf16[256,2048]{1,0:T(8,128)(2,1)} %get-tuple-element.217), channel_id=1, source_target_pairs={{0,16},{4,20},{8,24},{12,28},{16,0},{20,4},{24,8},{28,12},{1,17},{... | collective-permute-start | bytes 3145736 | tf_op jit(solution)/shard_map/ppermute | solution.py:72
  591.9 31.1 %all-to-all-start.7 = ((bf16[4,128,512]{2,1,0:T(8,128)(2,1)}), bf16[4,128,512]{2,1,0:T(8,128)(2,1)S(1)}, u32[]{:S(2)}, u32[]{:S(2)}) async-start(bf16[4,128,512]{2,1,0:T(8,128)(2,1)} %get-tuple-element.208), calls=%async_computation.7 | async-start | bytes 1048576 | tf_op jit(solution)/shard_map/all_to_all | solution.py:78
  642.8 46.9 %collective-permute-start.59 = (bf16[1024,2176]{1,0:T(8,128)(2,1)}, bf16[1024,2176]{1,0:T(8,128)(2,1)}, u32[]{:S(2)}, u32[]{:S(2)}) collective-permute-start(bf16[1024,2176]{1,0:T(8,128)(2,1)} %get-tuple-element.234), channel_id=1, source_target_pairs={{0,4},{4,0},{8,12},{12,8},{16,20},{20,16},{24,28},{28,24},{1,5},{5... | collective-permute-start | bytes 13369352 | tf_op jit(solution)/shard_map/ppermute | solution.py:72
  646.2 24.0 %collective-permute-start.56 = (bf16[128,2048]{1,0:T(8,128)(2,1)S(1)}, bf16[128,2048]{1,0:T(8,128)(2,1)}, u32[]{:S(2)}, u32[]{:S(2)}) collective-permute-start(bf16[128,2048]{1,0:T(8,128)(2,1)S(1)} %copy-done.48), channel_id=1, source_target_pairs={{0,8},{4,12},{8,0},{12,4},{16,24},{20,28},{24,16},{28,20},{1,9},{5... | collective-permute-start | bytes 1572872 | tf_op jit(solution)/shard_map/ppermute | solution.py:72
  705.1 30.3 %collective-permute-start.63 = (bf16[256,2176]{1,0:T(8,128)(2,1)}, bf16[256,2176]{1,0:T(8,128)(2,1)}, u32[]{:S(2)}, u32[]{:S(2)}) collective-permute-start(bf16[256,2176]{1,0:T(8,128)(2,1)} %get-tuple-element.260), channel_id=1, source_target_pairs={{0,8},{4,12},{8,0},{12,4},{16,24},{20,28},{24,16},{28,20},{1,9},{5... | collective-permute-start | bytes 3342344 | tf_op jit(solution)/shard_map/ppermute | solution.py:72
  706.2 29.2 %collective-permute-start.64 = (bf16[256,2176]{1,0:T(8,128)(2,1)}, bf16[256,2176]{1,0:T(8,128)(2,1)}, u32[]{:S(2)}, u32[]{:S(2)}) collective-permute-start(bf16[256,2176]{1,0:T(8,128)(2,1)} %get-tuple-element.259), channel_id=1, source_target_pairs={{0,16},{4,20},{8,24},{12,28},{16,0},{20,4},{24,8},{28,12},{1,17},{... | collective-permute-start | bytes 3342344 | tf_op jit(solution)/shard_map/ppermute | solution.py:72
  707.7 93.6 %all-to-all-start.9 = ((bf16[4,128,2048]{2,1,0:T(8,128)(2,1)}), bf16[4,128,2048]{2,1,0:T(8,128)(2,1)S(1)}, u32[]{:S(2)}, u32[]{:S(2)}) async-start(bf16[4,128,2048]{2,1,0:T(8,128)(2,1)} %bitcast.297), calls=%async_computation.9 | async-start | bytes 4194304 | tf_op jit(solution)/shard_map/all_to_all | solution.py:78
  717.3 33.6 %collective-permute-start.61 = (bf16[256,1664]{1,0:T(8,128)(2,1)}, bf16[256,1664]{1,0:T(8,128)(2,1)S(1)}, u32[]{:S(2)}, u32[]{:S(2)}) collective-permute-start(bf16[256,1664]{1,0:T(8,128)(2,1)} %get-tuple-element.265), channel_id=1, source_target_pairs={{0,8},{4,12},{8,0},{12,4},{16,24},{20,28},{24,16},{28,20},{1,9},{5... | collective-permute-start | bytes 2555912 | tf_op jit(solution)/shard_map/ppermute | solution.py:72
  718.3 35.6 %collective-permute-start.62 = (bf16[256,1664]{1,0:T(8,128)(2,1)}, bf16[256,1664]{1,0:T(8,128)(2,1)}, u32[]{:S(2)}, u32[]{:S(2)}) collective-permute-start(bf16[256,1664]{1,0:T(8,128)(2,1)} %get-tuple-element.264), channel_id=1, source_target_pairs={{0,16},{4,20},{8,24},{12,28},{16,0},{20,4},{24,8},{28,12},{1,17},{... | collective-permute-start | bytes 2555912 | tf_op jit(solution)/shard_map/ppermute | solution.py:72
  738.5 58.5 %collective-permute-start.67 = (bf16[128,2176]{1,0:T(8,128)(2,1)}, bf16[128,2176]{1,0:T(8,128)(2,1)}, u32[]{:S(2)}, u32[]{:S(2)}) collective-permute-start(bf16[128,2176]{1,0:T(8,128)(2,1)} %add_convert_fusion.8), channel_id=1, source_target_pairs={{0,16},{4,20},{8,24},{12,28},{16,0},{20,4},{24,8},{28,12},{1,17},{... | collective-permute-start | bytes 1671176 | tf_op jit(solution)/shard_map/ppermute | solution.py:72
  742.4 54.6 %collective-permute-start.68 = (bf16[128,2176]{1,0:T(8,128)(2,1)}, bf16[128,2176]{1,0:T(8,128)(2,1)}, u32[]{:S(2)}, u32[]{:S(2)}) collective-permute-start(bf16[128,2176]{1,0:T(8,128)(2,1)} %add_convert_fusion.9.refs_2_), channel_id=1, source_target_pairs={{0,8},{4,12},{8,0},{12,4},{16,24},{20,28},{24,16},{28,20},{1,9},{5... | collective-permute-start | bytes 1671176 | tf_op jit(solution)/shard_map/ppermute | solution.py:72
  743.4 23.8 %collective-permute-start.54 = (bf16[128,2048]{1,0:T(8,128)(2,1)}, bf16[128,2048]{1,0:T(8,128)(2,1)S(1)}, u32[]{:S(2)}, u32[]{:S(2)}) collective-permute-start(bf16[128,2048]{1,0:T(8,128)(2,1)} %get-tuple-element.280), channel_id=1, source_target_pairs={{0,1},{1,0},{2,3},{3,2},{4,5},{5,4},{6,7},{7,6},{8,9},{9,8},{10,11... | collective-permute-start | bytes 1572872 | tf_op jit(solution)/shard_map/ppermute | solution.py:75
  751.0 45.2 %collective-permute-start.57 = (bf16[128,2048]{1,0:T(8,128)(2,1)}, bf16[128,2048]{1,0:T(8,128)(2,1)}, u32[]{:S(2)}, u32[]{:S(2)}) collective-permute-start(bf16[128,2048]{1,0:T(8,128)(2,1)} %get-tuple-element.279), channel_id=1, source_target_pairs={{0,2},{1,3},{2,0},{3,1},{4,6},{5,7},{6,4},{7,5},{8,10},{9,11},{10,... | collective-permute-start | bytes 1572872 | tf_op jit(solution)/shard_map/ppermute | solution.py:75
  753.9 42.3 %collective-permute-start.58 = (bf16[128,2048]{1,0:T(8,128)(2,1)}, bf16[128,2048]{1,0:T(8,128)(2,1)S(1)}, u32[]{:S(2)}, u32[]{:S(2)}) collective-permute-start(bf16[128,2048]{1,0:T(8,128)(2,1)} %get-tuple-element.278), channel_id=1, source_target_pairs={{0,3},{1,2},{2,1},{3,0},{4,7},{5,6},{6,5},{7,4},{8,11},{9,10},{10,... | collective-permute-start | bytes 1572872 | tf_op jit(solution)/shard_map/ppermute | solution.py:75
  801.3 38.7 %all-to-all-start.11 = ((bf16[4,64,2176]{2,1,0:T(8,128)(2,1)}), bf16[4,64,2176]{2,1,0:T(8,128)(2,1)}, u32[]{:S(2)}, u32[]{:S(2)}) async-start(bf16[4,64,2176]{2,1,0:T(8,128)(2,1)} %bitcast.118), calls=%async_computation.11 | async-start | bytes 2228224 | tf_op jit(solution)/shard_map/all_to_all | solution.py:78
  840.0 24.8 %all-to-all-start.10 = ((bf16[4,64,1664]{2,1,0:T(8,128)(2,1)}), bf16[4,64,1664]{2,1,0:T(8,128)(2,1)S(1)}, u32[]{:S(2)}, u32[]{:S(2)}) async-start(bf16[4,64,1664]{2,1,0:T(8,128)(2,1)} %bitcast.116), calls=%async_computation.10 | async-start | bytes 1703936 | tf_op jit(solution)/shard_map/all_to_all | solution.py:78
  (131 other events, 1046.1 us)
Sparse Core Ops, SparseCore 0:
  155.6 59.4 all-gather.2

commit v3 on v2

--- a/solution.py
+++ b/solution.py
@@ -91,6 +91,15 @@
             whole = jnp.stack(parts)
             return [lax.psum_scatter(whole, "ctx", scatter_dimension=0, tiled=False)]
         return [parts[0]] + [self.cswap(parts[k], k) for k in range(1, self.nc)]
+
+    def sum_at_once(self, parts):
+        whole = jnp.stack(parts)
+        if not self.native:
+            return lax.psum_scatter(whole, "ctx", scatter_dimension=0, tiled=True)
+        for bit in (1, 2):
+            flipped = jnp.stack([whole[k ^ bit] for k in range(self.nc)])
+            whole = jnp.where((self.c & bit) > 0, flipped, whole)
+        return self.exchange(whole)
 
     def relative(self, value, planes=False):
         if not self.native:
@@ -532,10 +541,11 @@
     qkv_rows = jnp.concatenate([got[:, : 3 * width], got[:, cols_o:]], axis=1)
     w_o_rows = got[:, 3 * width : cols_o]
     qkv_begun = links.plane_start(qkv_rows)
-    w_qkv = links.all_blocks(links.plane_end(qkv_begun)[0])
+    x_sent = after(x_copies, got)
+    w_qkv = links.all_blocks(links.plane_end(qkv_begun, x_sent)[0])
     group = 2
     groups = nc // group
-    x_all = links.exchange(after(x_copies, got)).reshape(seq, dim)
+    x_all = links.exchange(x_sent).reshape(seq, dim)
     w_o_begun = links.plane_start(after(w_o_rows, w_qkv[-1]))
     w_o_pieces, w_o_sent = links.plane_end(w_o_begun)
     small_all = jnp.stack([w[:, 3 * width :] for w in w_qkv])
@@ -547,6 +557,11 @@
     ids_all = small_all[:, E + 4 : E + 4 + per_row].astype(jnp.int32)
     ids_all = ids_all.reshape(nf, nc, TOP, tok)
 
+    positions = jnp.arange(seq, dtype=jnp.int32)
+    cos, sin = rotary_tables(positions)
+    docs = jnp.sum((starts[None, :] <= positions[:, None]).astype(jnp.int32), axis=1)
+    allowed = (positions[None, :] <= positions[:, None]) & (docs[None, :] == docs[:, None])
+    mask = allowed.astype(F32)
     normed, raw, value, sums = call(
         functools.partial(qkv_kernel, nf),
         [
@@ -558,12 +573,13 @@
         3.2,
         13,
         ins=[SMEM] + [VMEM] * (2 + nf),
-        gate=w_o_sent,
+        gate=w_o_sent + [mask, cos, sin],
     )(frel, gain_attn, x_all, *w_qkv)
 
     w_o = links.all_blocks(w_o_pieces)
     if links.native:
-        g_groups = [jnp.concatenate([g_own, links.cswap(after(g_own, sums), 1)])]
+        g_one = links.cswap(after(g_own, w_qkv[-1]), 1)
+        g_groups = [jnp.concatenate([g_own, after(g_one, sums)])]
     else:
         g_groups = links.slots(g_own)
         g_groups = [jnp.concatenate(g_groups[i * group : (i + 1) * group]) for i in range(groups)]
@@ -574,14 +590,9 @@
 
     sums = jnp.sum(links.gather(sums), axis=0)[:, 0]
     inv = columns(lax.rsqrt(sums / dim + EPS))
-    positions = jnp.arange(seq, dtype=jnp.int32)
-    cos, sin = rotary_tables(positions)
     head_gain = jnp.stack([gain_query, gain_key]).reshape(2, nc, 1, width)
     head_gain = lax.dynamic_index_in_dim(head_gain, links.c, 1, keepdims=False)
     scale = 1.0 / math.sqrt(HD)
-    docs = jnp.sum((starts[None, :] <= positions[:, None]).astype(jnp.int32), axis=1)
-    allowed = (positions[None, :] <= positions[:, None]) & (docs[None, :] == docs[:, None])
-    mask = allowed.astype(F32)
 
     def whole(*dims):
         return pl.BlockSpec(dims, lambda h: (0,) * len(dims))
@@ -609,7 +620,7 @@
     mine = first_expert + jnp.arange(experts, dtype=jnp.int32)
     theirs = ((links.f ^ 1) * nc + links.c) * pieces // 2 + jnp.arange(experts, dtype=jnp.int32)
     both = jnp.concatenate([mine, theirs]) if cores == 2 else mine
-    ids_rel = links.relative(ids_all).transpose(1, 0, 2, 3)
+    ids_rel = links.relative(after(ids_all, mixed)).transpose(1, 0, 2, 3)
     before = (jnp.arange(tok)[:, None] < jnp.arange(tok)[None, :]).astype(BF)
     ranks = jnp.arange(CAP, dtype=F32)[:, None]
 
@@ -718,7 +729,7 @@
         far = links.gather(moe_in, near)
         x_begun = [links.plane_start(jnp.concatenate([moe_in, near]))]
         seen, sent = links.plane_end(x_begun[0], g_rows[0][0])
-        far = after(far, *sent)
+        far = after(far, *seen[3])
         g_far = links.exchange(after(g_copies, far))
         x_begun.append(links.plane_start(jnp.concatenate(pick_far(far))))
         x_rows = [take_rows(0, seen, x_begun[1][0])]
@@ -868,12 +879,12 @@
         totals.append(links.reduce_end(more[i], group * tok, last))
         last = totals[i]
     dmoe_terms = links.sum_slots([t for total in totals for t in cut_group(total)])
-    grad_w_out = grad_out_pieces(inners, g_rows, last)
+    dgate_back = after(dgate_back, out_arrays[0][0])
+    dprob = jnp.sum(dgate_back.reshape(E, ndev * experts // E, tok), axis=1).T
+    dprob = jnp.pad(dprob, ((0, 0), (0, LANES - E)))
+    grad_w_out = grad_out_pieces(inners, g_rows, last, dprob)
     out_begun.append(links.reduce_start(held(out_arrays[-1], grad_w_out)))
     dmoe_terms = held(dmoe_terms, grad_w_out)
-    dgate_back = after(dgate_back, grad_w_out)
-    dprob = jnp.sum(dgate_back.reshape(E, ndev * experts // E, tok), axis=1).T
-    dprob = jnp.pad(dprob, ((0, 0), (0, LANES - E)))
 
     back = call(
         functools.partial(hidden_back_kernel, nf, len(dmoe_terms)),
@@ -936,7 +947,7 @@
     for m in out_more:
         out_totals.append(links.reduce_end(m, group * tok, last))
         last = out_totals[-1]
-    out_terms = links.sum_slots([t for o in out_totals for t in cut_group(o)])
+    out_terms = links.sum_at_once([t for o in out_totals for t in cut_group(o)])
     mean = after(mean, last)
     dqkv, dnormed_terms, dgain_attn = call(
         functools.partial(dnormed_kernel, nf),
@@ -945,7 +956,6 @@
         15,
         ins=[SMEM] + [VMEM] * (6 + nf),
     )(frel, u, raw, inv, mean, dvalue, x_all, *w_qkv)
-    dnormed_terms = links.exchange(dnormed_terms.reshape(nc, tok, dim))
 
     def placed(vector):
         return lax.dynamic_update_slice(jnp.zeros((dim,), F32), vector, (links.c * width,))
@@ -953,16 +963,19 @@
     grad_o_begun = links.dense_start(grad_o_terms, fsdp_rows, dqkv)
     gain_terms = jnp.stack([dgain_attn[0], placed(dgain[0, 0]), placed(dgain[1, 0])])
     gain_terms = jnp.pad(gain_terms.astype(BF), ((0, LANES - 3), (0, 0))).T
-    grad_qkv_terms = dense_terms(normed, dqkv, gain_terms, *grad_o_begun[2:3])
-    grad_qkv_begun = links.dense_start(grad_qkv_terms, fsdp_rows, grad_qkv_terms[0])
+    last = dqkv
+    for j in range(1, experts):
+        grad_w_in = grad_in_pieces(j, grad_w_in, dqkv, *grad_o_begun[2:3])
+        last = grad_w_in
+    grad_qkv_terms = dense_terms(normed, dqkv, gain_terms, last, out_terms)
+    last = grad_qkv_terms[0]
+    dnormed_terms = after(dnormed_terms.reshape(nc, tok, dim), out_terms)
+    grad_qkv_begun = links.dense_start(grad_qkv_terms, fsdp_rows, last, dnormed_terms)
+    dnormed_terms = links.exchange(dnormed_terms)
     last = grad_qkv_begun[-1]
-    for j in range(1, experts):
-        grad_w_in = grad_in_pieces(j, grad_w_in, last)
-        last = grad_w_in
     grad_o_more = links.reduce_next(grad_o_begun, last)
     grad_qkv_more = links.reduce_next(grad_qkv_begun, grad_o_more[-1])
-    out_terms = held(out_terms, grad_qkv_more[-1])
-    grad_o_total = links.reduce_end(grad_o_more, fsdp_rows, out_terms[-1])
+    grad_o_total = links.reduce_end(grad_o_more, fsdp_rows, grad_qkv_more[-1])
     grad_o = links.exchange(grad_o_total.reshape(nc, own_rows, -1))
     grad_qkv_total = links.reduce_end(grad_qkv_more, fsdp_rows, grad_o_total)
     dnormed_terms = after(dnormed_terms, grad_qkv_total)
@@ -973,7 +986,7 @@
     x_mean = jnp.mean(ux * x_float, axis=-1, keepdims=True)
     input_grad = (dhidden + x_inv * ux - x_float * x_inv**3 * x_mean)[None]
 
-    output = (hidden + sum(t.astype(F32) for t in out_terms)).astype(BF)
+    output = (hidden + jnp.sum(out_terms.astype(F32), axis=0)).astype(BF)
     grad_o = jnp.sum(grad_o.astype(F32), axis=0)
     grad_attn_out, router_sum = grad_o[:, :dim], grad_o[:, dim:]
     grad_qkv = links.exchange(grad_qkv_total.reshape(nc, own_rows, -1)).astype(F32)

time: 896 us -> 848 us (0.946)
  blocking collectives: 50.1 us -> 0 us
    all_to_all x1 -> x0, blocking collectives: 50.1 us -> none  [exchange(): return lax.all_to_all(value, 'ctx', split_axis=0, concat_axis=0, tiled=True)]
    all_to_all x10 -> x12, waiting for transfers between devices: 51.1 us -> 97.4 us  [exchange(): return lax.all_to_all(value, 'ctx', split_axis=0, concat_axis=0, tiled=True)]
    ppermute x8 -> x5, waiting for transfers between devices: 72.3 us -> 27 us  [cswap(): return lax.ppermute(value, 'ctx', [(i, i ^ mask) for i in range(self.nc)])]
    all_to_all x10 -> x12, starting transfers between devices: 51.7 us -> 64 us  [exchange(): return lax.all_to_all(value, 'ctx', split_axis=0, concat_axis=0, tiled=True)]
    unnamed x214 -> x208, local copies, waits for them, and re-layouts: 33.6 us -> 38.7 us
  transfers between devices with their start and end apart: 81 -> 80, of which waited for: 35 -> 30; matrix products, arithmetic and copies ran while one was open for 16% -> 16% of each run, Pallas kernels for 23% -> 27%
where the time goes in v3:
time: 848 us; the launch traced here: 836 us
  waiting for transfers between devices  264 us (31%)
  Pallas kernels  238 us (28%)
  starting transfers between devices  127 us (15%)
  local copies, waits for them, and re-layouts  109 us (13%)
  other arithmetic  81.4 us (10%)
  between operations  16.4 us (2%)
    pallas_call x22, Pallas kernels, call(): return lambda *operands: made(*operands, *gate)  229 us
    ppermute x61, waiting for transfers between devices, swap(): return lax.ppermute(value, 'fsdp', [(i, i ^ mask) for i in range(self.nf)])  134 us
    all_to_all x12, waiting for transfers between devices, exchange(): return lax.all_to_all(value, 'ctx', split_axis=0, concat_axis=0, tiled=True)  97.4 us
    all_to_all x12, starting transfers between devices, exchange(): return lax.all_to_all(value, 'ctx', split_axis=0, concat_axis=0, tiled=True)  64 us
    ppermute x61, starting transfers between devices, swap(): return lax.ppermute(value, 'fsdp', [(i, i ^ mask) for i in range(self.nf)])  48.7 us
    convert_element_type x20, other arithmetic, add_low(): return sum((t.astype(F32) for t in terms)).astype(BF)  44.4 us
    unnamed x208, local copies, waits for them, and re-layouts  38.7 us
    ppermute x5, waiting for transfers between devices, cswap(): return lax.ppermute(value, 'ctx', [(i, i ^ mask) for i in range(self.nc)])  27 us
  transfers between devices with their start and end apart: 80, of which 30 were waited for; matrix products, arithmetic and copies ran while one was open for 16% of the time, Pallas kernels for 27%

profile of v3, /device:TPU:0, one launch (start us, length us, event | category | flops | bytes accessed | tf_op | source)
XLA Modules:
  0.0 836.2 jit_solution(5795505725115117487)
XLA Ops:
  14.8 6.4 all-to-all-start
  21.4 43.9 %all-to-all-done = bf16[4,64,3712]{2,1,0:T(8,128)(2,1)S(1)} async-done(((bf16[4,64,3712]{2,1,0:T(8,128)(2,1)}), bf16[4,64,3712]{2,1,0:T(8,128)(2,1)S(1)}, u32[]{:S(2)}, u32[]{:S(2)}) %all-to-all-start) | async-done | bytes 1900576 | tf_op jit(solution)/shard_map/all_to_all | solution.py:78
  81.2 5.4 collective-permute-done.2.refs_1_
  94.9 7.5 collective-permute-done.5
  115.7 16.9 %collective-permute-done.9.refs_6_.refs_14_ = bf16[256,2048]{1,0:T(8,128)(2,1)} collective-permute-done((bf16[256,2048]{1,0:T(8,128)(2,1)}, bf16[256,2048]{1,0:T(8,128)(2,1)}, u32[]{:S(2)}, u32[]{:S(2)}) %collective-permute-start.9) | collective-permute-done | bytes 1048608 | tf_op jit(solution)/shard_map/ppermute | solution.py:72
  137.7 9.6 %shard_map.258 = (bf16[512,2048]{1,0:T(8,128)(2,1)}, f32[2,512,512]{2,1,0:T(8,128)}, bf16[512,512]{1,0:T(8,128)(2,1)}, f32[2,8,512]{2,1,0:T(8,128)}) custom-call(s32[8]{0:T(128)} %iota_xor_fusion.refs_0_, f32[1,2048]{1,0:T(1,128)} %copy.312.refs_1_, bf16[512,2048]{1,0:T(8,128)(2,1)} %bitcast.271, bf16[256,1664]{1,0:T(8,128)(2,1)} %pad_maximum_fusion.9.refs_3_.refs_7_, ...), custom_call_target="tpu_custom_call" | custom-call | flops 160000000 | bytes 650000 | tf_op jit(solution)/shard_map/pallas_call | solution.py:241
  164.3 7.0 shard_map.259
  171.3 5.1 all-to-all-start.3
  191.2 6.3 shard_map.261
  199.1 12.9 %collective-permute-done.16.refs_1_ = bf16[128,2048]{1,0:T(8,128)(2,1)S(1)} collective-permute-done((bf16[128,2048]{1,0:T(8,128)(2,1)}, bf16[128,2048]{1,0:T(8,128)(2,1)S(1)}, u32[]{:S(2)}, u32[]{:S(2)}) %collective-permute-start.16) | collective-permute-done | bytes 524320 | tf_op jit(solution)/shard_map/ppermute | solution.py:75
  214.8 5.0 all-to-all-start.4
  223.7 9.0 %shard_map.264.refs_2_.refs_6_ = bf16[2,384,2048]{2,1,0:T(8,128)(2,1)} custom-call(s32[8]{0:T(128)} %broadcast_xor_fusion.places, bf16[8,96,256]{2,1,0:T(8,128)(2,1)} %broadcast_multiply_fusion.1.refs_16_.slots, bf16[8,256,2048]{2,1,0:T(8,128)(2,1)} %bitcast.285), custom_call_target="tpu_custom_call" | custom-call | flops 40000000 | bytes 600000 | tf_op jit(solution)/shard_map/pallas_call | solution.py:708
  232.7 13.5 %collective-permute-done.18.refs_1_ = bf16[256,2048]{1,0:T(8,128)(2,1)S(1)} collective-permute-done((bf16[256,2048]{1,0:T(8,128)(2,1)}, bf16[256,2048]{1,0:T(8,128)(2,1)S(1)}, u32[]{:S(2)}, u32[]{:S(2)}) %collective-permute-start.18) | collective-permute-done | bytes 1048608 | tf_op jit(solution)/shard_map/ppermute | solution.py:72
  253.6 14.3 %all-to-all-done.4.refs_0_ = bf16[4,128,2048]{2,1,0:T(8,128)(2,1)S(1)} async-done(((bf16[4,128,2048]{2,1,0:T(8,128)(2,1)}), bf16[4,128,2048]{2,1,0:T(8,128)(2,1)S(1)}, u32[]{:S(2)}, u32[]{:S(2)}) %all-to-all-start.4) | async-done | bytes 2097184 | tf_op jit(solution)/shard_map/all_to_all | solution.py:78
  271.0 4.7 all-to-all-start.5
  286.1 32.1 %shard_map.269 = (bf16[2,192,2048]{2,1,0:T(8,128)(2,1)}, bf16[2,192,2048]{2,1,0:T(8,128)(2,1)}, bf16[4,384,1024]{2,1,0:T(8,128)(2,1)}, bf16[2,384,1024]{2,1,0:T(8,128)(2,1)}, f32[2,384,128]{2,1,0:T(8,128)}) custom-call(s32[1]{0:T(128)} %bitcast.69.refs_0_, bf16[2048,128]{1,0:T(8,128)(2,1)} %get-tuple-element.252.refs_1_.refs_6_, ...), custom_call_target="tpu_custom_call" | custom-call | flops 1700000000 | bytes 1500000 | tf_op jit(solution)/shard_map/pallas_call | solution.py:241
  333.5 27.5 %collective-permute-done.25.refs_4_ = bf16[128,2048]{1,0:T(8,128)(2,1)S(1)} collective-permute-done((bf16[128,2048]{1,0:T(8,128)(2,1)S(1)}, bf16[128,2048]{1,0:T(8,128)(2,1)S(1)}, u32[]{:S(2)}, u32[]{:S(2)}) %collective-permute-start.25) | collective-permute-done | bytes 524320 | tf_op jit(solution)/shard_map/ppermute | solution.py:72
  372.4 8.8 %collective-permute-done.31.refs_4_ = bf16[128,2048]{1,0:T(8,128)(2,1)S(1)} collective-permute-done((bf16[128,2048]{1,0:T(8,128)(2,1)S(1)}, bf16[128,2048]{1,0:T(8,128)(2,1)S(1)}, u32[]{:S(2)}, u32[]{:S(2)}) %collective-permute-start.31) | collective-permute-done | bytes 524320 | tf_op jit(solution)/shard_map/ppermute | solution.py:72
  383.3 4.5 shard_map.276
  393.6 32.1 %shard_map.277 = (bf16[2,192,2048]{2,1,0:T(8,128)(2,1)}, bf16[2,192,2048]{2,1,0:T(8,128)(2,1)}, bf16[4,384,1024]{2,1,0:T(8,128)(2,1)}, bf16[2,384,1024]{2,1,0:T(8,128)(2,1)}, f32[2,384,128]{2,1,0:T(8,128)}) custom-call(s32[1]{0:T(128)} %bitcast.69.refs_0_, bf16[2048,128]{1,0:T(8,128)(2,1)} %get-tuple-element.252.refs_1_.refs_6_, ...), custom_call_target="tpu_custom_call" | custom-call | flops 1700000000 | bytes 1500000 | tf_op jit(solution)/shard_map/pallas_call | solution.py:241
  432.9 4.3 shard_map.280
  437.2 7.1 shard_map.281
  447.0 7.6 shard_map.282
  461.1 4.3 shard_map.284
  465.5 5.7 collective-permute-done.41.refs_1_
  478.5 6.1 all-to-all-start.6
  486.4 5.7 all-to-all-done.6.refs_0_
  510.5 15.6 %shard_map.290.refs_4_.refs_5_ = f32[2,1024,2048]{2,1,0:T(8,128)} custom-call(bf16[2,384,1024]{2,1,0:T(8,128)(2,1)} %get-tuple-element.142.refs_0_, bf16[2,384,1024]{2,1,0:T(8,128)(2,1)} %get-tuple-element.170.refs_0_.refs_1_, bf16[2,384,2048]{2,1,0:T(8,128)(2,1)} %shard_map.264.refs_2_.refs_6_, ...), custom_call_target="tpu_custom_call" | custom-call | flops 325000000 | bytes 1300000 | tf_op jit(solution)/shard_map/pallas_call | solution.py:241
  527.3 14.1 %collective-permute-done.48.refs_2_ = bf16[128,2048]{1,0:T(8,128)(2,1)S(1)} collective-permute-done((bf16[128,2048]{1,0:T(8,128)(2,1)}, bf16[128,2048]{1,0:T(8,128)(2,1)S(1)}, u32[]{:S(2)}, u32[]{:S(2)}) %collective-permute-start.48) | collective-permute-done | bytes 524320 | tf_op jit(solution)/shard_map/ppermute | solution.py:75
  542.4 10.1 %shard_map.292 = (f32[128,2048]{1,0:T(8,128)}, f32[2048,128]{1,0:T(8,128)}, f32[8,2048]{1,0:T(8,128)}, bf16[128,2048]{1,0:T(8,128)(2,1)}, bf16[4,128,512]{2,1,0:T(8,128)(2,1)}) custom-call(s32[8]{0:T(128)} %iota_xor_fusion.refs_0_, f32[128,2048]{1,0:T(8,128)} %get-tuple-element.136.refs_1_, f32[128,128]{1,0:T(8,128)} %get-tuple-element.185.refs_2_, ...), custom_call_target="tpu_custom_call" | custom-call | flops 65000000 | bytes 750000 | tf_op jit(solution)/shard_map/pallas_call | solution.py:241
  553.5 13.3 %all-to-all-start.7 = ((bf16[4,128,512]{2,1,0:T(8,128)(2,1)}), bf16[4,128,512]{2,1,0:T(8,128)(2,1)S(1)}, u32[]{:S(2)}, u32[]{:S(2)}) async-start(bf16[4,128,512]{2,1,0:T(8,128)(2,1)} %get-tuple-element.208), calls=%async_computation.7 | async-start | bytes 1048576 | tf_op jit(solution)/shard_map/all_to_all | solution.py:78
  581.3 16.6 %shard_map.296.refs_1_.refs_6_ = f32[4,2048,1024]{2,1,0:T(8,128)} custom-call(bf16[2,192,2048]{2,1,0:T(8,128)(2,1)} %get-tuple-element.140.refs_4_.refs_7_.refs_0_, bf16[2,192,2048]{2,1,0:T(8,128)(2,1)} %copy-done.10, bf16[2,192,2048]{2,1,0:T(8,128)(2,1)} %get-tuple-element.148.refs_2_.refs_4_, bf16[2,192,2048]{2,1,0:T(8,128)(2,1)} %copy-done.11, ...), custom_call_target="tpu_custom_call" | custom-call | flops 325000000 | bytes 1250000 | tf_op jit(solution)/shard_map/pallas_call | solution.py:241
  598.7 11.5 %shard_map.298 = (f32[2,512,512]{2,1,0:T(8,128)}, bf16[512,512]{1,0:T(8,128)(2,1)}, f32[2,8,512]{2,1,0:T(8,128)}, f32[2,8,512]{2,1,0:T(8,128)}) custom-call(f32[2,512,512]{2,1,0:T(8,128)} %get-tuple-element.132.refs_0_.refs_2_, bf16[2,512,512]{2,1,0:T(8,128)(2,1)} %get-tuple-element.207.refs_1_, bf16[512,512]{1,0:T(8,128)(2,1)} %get-tuple-element.133.refs_1_.refs_2_, ...), custom_call_target="tpu_custom_call" | custom-call | flops 70000000 | bytes 500000 | tf_op jit(solution)/shard_map/pallas_call | solution.py:241
  611.7 5.1 all-to-all-start.9
  616.8 7.1 shard_map.299
  633.5 5.3 all-to-all-start.8
  642.3 11.0 %shard_map.303 = (bf16[512,1536]{1,0:T(8,128)(2,1)}, bf16[512,2048]{1,0:T(8,128)(2,1)}, f32[8,2048]{1,0:T(8,128)}) custom-call(s32[8]{0:T(128)} %iota_xor_fusion.refs_0_, f32[2,512,512]{2,1,0:T(8,128)} %get-tuple-element.229.refs_1_, f32[2,512,512]{2,1,0:T(8,128)} %get-tuple-element.132.refs_0_.refs_2_, f32[2,512,128]{2,1,0:T(8,128)} %broadcast_in_dim.100.refs_2_.refs_3_, ...), custom_call_target="tpu_custom_call" | custom-call | flops 165000000 | bytes 750000 | tf_op jit(solution)/shard_map/pallas_call | solution.py:241
  657.6 16.6 %shard_map.306.refs_4_ = f32[4,2048,1024]{2,1,0:T(8,128)} custom-call(bf16[2,192,2048]{2,1,0:T(8,128)(2,1)} %get-tuple-element.140.refs_4_.refs_7_.refs_0_, bf16[2,192,2048]{2,1,0:T(8,128)(2,1)} %copy-done.10, bf16[2,192,2048]{2,1,0:T(8,128)(2,1)} %get-tuple-element.148.refs_2_.refs_4_, ...), custom_call_target="tpu_custom_call", output_to_operand_aliasing={{}: (6, {})} | custom-call | flops 325000000 | bytes 1250000 | tf_op jit(solution)/shard_map/pallas_call | solution.py:241
  674.2 13.4 %all-to-all-done.8.refs_1_.refs_5_ = bf16[4,128,2048]{2,1,0:T(8,128)(2,1)S(1)} async-done(((bf16[4,128,2048]{2,1,0:T(8,128)(2,1)}), bf16[4,128,2048]{2,1,0:T(8,128)(2,1)S(1)}, u32[]{:S(2)}, u32[]{:S(2)}) %all-to-all-start.8) | async-done | bytes 2097184 | tf_op jit(solution)/shard_map/all_to_all | solution.py:78
  689.0 8.3 shard_map.307
  697.3 5.1 add_convert_fusion
  704.1 4.5 all-to-all-start.10
  718.0 12.0 %collective-permute-done.61.refs_1_ = bf16[256,2176]{1,0:T(8,128)(2,1)} collective-permute-done((bf16[256,2176]{1,0:T(8,128)(2,1)}, bf16[256,2176]{1,0:T(8,128)(2,1)}, u32[]{:S(2)}, u32[]{:S(2)}) %collective-permute-start.61) | collective-permute-done | bytes 1114144 | tf_op jit(solution)/shard_map/ppermute | solution.py:72
  737.4 10.9 %collective-permute-done.59.refs_1_ = bf16[256,1664]{1,0:T(8,128)(2,1)} collective-permute-done((bf16[256,1664]{1,0:T(8,128)(2,1)}, bf16[256,1664]{1,0:T(8,128)(2,1)}, u32[]{:S(2)}, u32[]{:S(2)}) %collective-permute-start.59) | collective-permute-done | bytes 852000 | tf_op jit(solution)/shard_map/ppermute | solution.py:72
  751.7 8.1 collective-permute-done.64.refs_0_
  771.2 8.9 %collective-permute-done.62.refs_0_ = bf16[128,1664]{1,0:T(8,128)(2,1)S(1)} collective-permute-done((bf16[128,1664]{1,0:T(8,128)(2,1)S(1)}, bf16[128,1664]{1,0:T(8,128)(2,1)S(1)}, u32[]{:S(2)}, u32[]{:S(2)}) %collective-permute-start.62) | collective-permute-done | bytes 426016 | tf_op jit(solution)/shard_map/ppermute | solution.py:72
  786.4 7.8 all-to-all-done.12
  802.6 16.1 %all-to-all-done.11 = bf16[4,64,1664]{2,1,0:T(8,128)(2,1)S(1)} async-done(((bf16[4,64,1664]{2,1,0:T(8,128)(2,1)}), bf16[4,64,1664]{2,1,0:T(8,128)(2,1)S(1)}, u32[]{:S(2)}, u32[]{:S(2)}) %all-to-all-start.11) | async-done | bytes 852000 | tf_op jit(solution)/shard_map/all_to_all | solution.py:78
  (589 shorter events, 285.2 us)
Async XLA Ops:
  14.8 50.4 %all-to-all-start = ((bf16[4,64,3712]{2,1,0:T(8,128)(2,1)}), bf16[4,64,3712]{2,1,0:T(8,128)(2,1)S(1)}, u32[]{:S(2)}, u32[]{:S(2)}) async-start(bf16[4,64,3712]{2,1,0:T(8,128)(2,1)} %pad_maximum_fusion), calls=%async_computation | async-start | bytes 3801088 | tf_op jit(solution)/shard_map/all_to_all | solution.py:78
  76.7 59.7 %all-to-all-start.1 = ((bf16[4,128,2048]{2,1,0:T(8,128)(2,1)}), bf16[4,128,2048]{2,1,0:T(8,128)(2,1)S(1)}, u32[]{:S(2)}, u32[]{:S(2)}) async-start(bf16[4,128,2048]{2,1,0:T(8,128)(2,1)} %shard_map.255.refs_2_), calls=%async_computation.1 | async-start | bytes 4194304 | tf_op jit(solution)/shard_map/all_to_all | solution.py:78
  80.3 143.5 %all-gather.3.cloned.1.call-start = ((), (), s32[]{:S(2)}) async-start(), calls=%async_computation.13 | async-start | bytes 9437184 | tf_op jit(solution)/shard_map/all_gather | solution.py:586
  107.1 25.5 %collective-permute-start.9 = (bf16[256,2048]{1,0:T(8,128)(2,1)}, bf16[256,2048]{1,0:T(8,128)(2,1)}, u32[]{:S(2)}, u32[]{:S(2)}) collective-permute-start(bf16[256,2048]{1,0:T(8,128)(2,1)} %shard_map.257.refs_4_.refs_12_), channel_id=1, source_target_pairs={{0,8},{4,12},{8,0},{12,4},{16,24},{20,28},{24,16},{28,20},{1,9},{5... | collective-permute-start | bytes 3145736 | tf_op jit(solution)/shard_map/ppermute | solution.py:72
  107.6 26.9 %collective-permute-start.8 = (bf16[256,2048]{1,0:T(8,128)(2,1)}, bf16[256,2048]{1,0:T(8,128)(2,1)}, u32[]{:S(2)}, u32[]{:S(2)}) collective-permute-start(bf16[256,2048]{1,0:T(8,128)(2,1)} %shard_map.257.refs_4_.refs_12_), channel_id=1, source_target_pairs={{0,16},{4,20},{8,24},{12,28},{16,0},{20,4},{24,8},{28,12},{1,17},{... | collective-permute-start | bytes 3145736 | tf_op jit(solution)/shard_map/ppermute | solution.py:72
  108.7 38.6 %collective-permute-start.19 = (bf16[128,2048]{1,0:T(8,128)(2,1)}, bf16[128,2048]{1,0:T(8,128)(2,1)}, u32[]{:S(2)}, u32[]{:S(2)}) collective-permute-start(bf16[128,2048]{1,0:T(8,128)(2,1)} %shard_map.262), channel_id=1, source_target_pairs={{0,1},{1,0},{2,3},{3,2},{4,5},{5,4},{6,7},{7,6},{8,9},{9,8},{10,11... | collective-permute-start | bytes 1572872 | tf_op jit(solution)/shard_map/ppermute | solution.py:75
  157.4 33.3 %collective-permute-start.10 = (bf16[256,2048]{1,0:T(8,128)(2,1)S(1)}, bf16[256,2048]{1,0:T(8,128)(2,1)}, u32[]{:S(2)}, u32[]{:S(2)}) collective-permute-start(bf16[256,2048]{1,0:T(8,128)(2,1)S(1)} %copy-done.6), channel_id=1, source_target_pairs={{0,4},{4,0},{8,12},{12,8},{16,20},{20,16},{24,28},{28,24},{1,5},{5... | collective-permute-start | bytes 3145736 | tf_op jit(solution)/shard_map/ppermute | solution.py:72
  162.8 28.4 %collective-permute-start.11 = (bf16[256,2048]{1,0:T(8,128)(2,1)}, bf16[256,2048]{1,0:T(8,128)(2,1)}, u32[]{:S(2)}, u32[]{:S(2)}) collective-permute-start(bf16[256,2048]{1,0:T(8,128)(2,1)} %collective-permute-done.9.refs_6_.refs_14_), channel_id=1, source_target_pairs={{0,4},{4,0},{8,12},{12,8},{16,20},{20,16},{24,28},{28,24},{1,5},{5... | collective-permute-start | bytes 3145736 | tf_op jit(solution)/shard_map/ppermute | solution.py:72
  162.8 28.4 %collective-permute-start.12 = (bf16[256,2048]{1,0:T(8,128)(2,1)}, bf16[256,2048]{1,0:T(8,128)(2,1)}, u32[]{:S(2)}, u32[]{:S(2)}) collective-permute-start(bf16[256,2048]{1,0:T(8,128)(2,1)} %collective-permute-done.8.refs_8_.refs_16_), channel_id=1, source_target_pairs={{0,4},{4,0},{8,12},{12,8},{16,20},{20,16},{24,28},{28,24},{1,5},{5... | collective-permute-start | bytes 3145736 | tf_op jit(solution)/shard_map/ppermute | solution.py:72
  214.8 53.1 %all-to-all-start.4 = ((bf16[4,128,2048]{2,1,0:T(8,128)(2,1)}), bf16[4,128,2048]{2,1,0:T(8,128)(2,1)S(1)}, u32[]{:S(2)}, u32[]{:S(2)}) async-start(bf16[4,128,2048]{2,1,0:T(8,128)(2,1)} %shard_map.266), calls=%async_computation.4 | async-start | bytes 4194304 | tf_op jit(solution)/shard_map/all_to_all | solution.py:78
  221.4 24.8 %collective-permute-start.18 = (bf16[256,2048]{1,0:T(8,128)(2,1)}, bf16[256,2048]{1,0:T(8,128)(2,1)S(1)}, u32[]{:S(2)}, u32[]{:S(2)}) collective-permute-start(bf16[256,2048]{1,0:T(8,128)(2,1)} %constant_dynamic-update-slice_fusion.4.refs_1_), channel_id=1, source_target_pairs={{0,16},{4,20},{8,24},{12,28},{16,0},{20,4},{24,8},{28,12},{1,17},{... | collective-permute-start | bytes 3145736 | tf_op jit(solution)/shard_map/ppermute | solution.py:72
  222.3 24.6 %collective-permute-start.17 = (bf16[256,2048]{1,0:T(8,128)(2,1)}, bf16[256,2048]{1,0:T(8,128)(2,1)}, u32[]{:S(2)}, u32[]{:S(2)}) collective-permute-start(bf16[256,2048]{1,0:T(8,128)(2,1)} %constant_dynamic-update-slice_fusion.4.refs_1_), channel_id=1, source_target_pairs={{0,8},{4,12},{8,0},{12,4},{16,24},{20,28},{24,16},{28,20},{1,9},{5... | collective-permute-start | bytes 3145736 | tf_op jit(solution)/shard_map/ppermute | solution.py:72
  271.0 52.5 %all-to-all-start.5 = ((bf16[4,128,2048]{2,1,0:T(8,128)(2,1)}), bf16[4,128,2048]{2,1,0:T(8,128)(2,1)}, u32[]{:S(2)}, u32[]{:S(2)}) async-start(bf16[4,128,2048]{2,1,0:T(8,128)(2,1)} %shard_map.271), calls=%async_computation.5 | async-start | bytes 4194304 | tf_op jit(solution)/shard_map/all_to_all | solution.py:78
  281.3 37.0 %collective-permute-start.24 = (bf16[256,2048]{1,0:T(8,128)(2,1)S(1)}, bf16[256,2048]{1,0:T(8,128)(2,1)}, u32[]{:S(2)}, u32[]{:S(2)}) collective-permute-start(bf16[256,2048]{1,0:T(8,128)(2,1)S(1)} %copy-done.16), channel_id=1, source_target_pairs={{0,16},{4,20},{8,24},{12,28},{16,0},{20,4},{24,8},{28,12},{1,17},{... | collective-permute-start | bytes 3145736 | tf_op jit(solution)/shard_map/ppermute | solution.py:72
  282.2 36.2 %collective-permute-start.23 = (bf16[256,2048]{1,0:T(8,128)(2,1)S(1)}, bf16[256,2048]{1,0:T(8,128)(2,1)}, u32[]{:S(2)}, u32[]{:S(2)}) collective-permute-start(bf16[256,2048]{1,0:T(8,128)(2,1)S(1)} %copy-done.16), channel_id=1, source_target_pairs={{0,8},{4,12},{8,0},{12,4},{16,24},{20,28},{24,16},{28,20},{1,9},{5... | collective-permute-start | bytes 3145736 | tf_op jit(solution)/shard_map/ppermute | solution.py:72
  325.0 41.0 %collective-permute-start.30 = (bf16[256,2048]{1,0:T(8,128)(2,1)S(1)}, bf16[256,2048]{1,0:T(8,128)(2,1)S(1)}, u32[]{:S(2)}, u32[]{:S(2)}) collective-permute-start(bf16[256,2048]{1,0:T(8,128)(2,1)S(1)} %pad_maximum_fusion.4.refs_3_.refs_1_), channel_id=1, source_target_pairs={{0,16},{4,20},{8,24},{12,28},{16,0},{20,4},{24,8},{28,12},{1,17},{... | collective-permute-start | bytes 3145736 | tf_op jit(solution)/shard_map/ppermute | solution.py:72
  325.9 40.1 %collective-permute-start.29 = (bf16[256,2048]{1,0:T(8,128)(2,1)S(1)}, bf16[256,2048]{1,0:T(8,128)(2,1)}, u32[]{:S(2)}, u32[]{:S(2)}) collective-permute-start(bf16[256,2048]{1,0:T(8,128)(2,1)S(1)} %pad_maximum_fusion.4.refs_3_.refs_1_), channel_id=1, source_target_pairs={{0,8},{4,12},{8,0},{12,4},{16,24},{20,28},{24,16},{28,20},{1,9},{5... | collective-permute-start | bytes 3145736 | tf_op jit(solution)/shard_map/ppermute | solution.py:72
  326.9 34.1 %collective-permute-start.25 = (bf16[128,2048]{1,0:T(8,128)(2,1)S(1)}, bf16[128,2048]{1,0:T(8,128)(2,1)S(1)}, u32[]{:S(2)}, u32[]{:S(2)}) collective-permute-start(bf16[128,2048]{1,0:T(8,128)(2,1)S(1)} %copy-done.63), channel_id=1, source_target_pairs={{0,8},{4,12},{8,0},{12,4},{16,24},{20,28},{24,16},{28,20},{1,9},{5... | collective-permute-start | bytes 1572872 | tf_op jit(solution)/shard_map/ppermute | solution.py:72
  327.9 33.0 %collective-permute-start.26 = (bf16[128,2048]{1,0:T(8,128)(2,1)S(1)}, bf16[128,2048]{1,0:T(8,128)(2,1)}, u32[]{:S(2)}, u32[]{:S(2)}) collective-permute-start(bf16[128,2048]{1,0:T(8,128)(2,1)S(1)} %copy-done.61), channel_id=1, source_target_pairs={{0,16},{4,20},{8,24},{12,28},{16,0},{20,4},{24,8},{28,12},{1,17},{... | collective-permute-start | bytes 1572872 | tf_op jit(solution)/shard_map/ppermute | solution.py:72
  387.9 40.5 %collective-permute-start.35 = (bf16[256,2048]{1,0:T(8,128)(2,1)}, bf16[256,2048]{1,0:T(8,128)(2,1)}, u32[]{:S(2)}, u32[]{:S(2)}) collective-permute-start(bf16[256,2048]{1,0:T(8,128)(2,1)} %get-tuple-element.161), channel_id=1, source_target_pairs={{0,8},{4,12},{8,0},{12,4},{16,24},{20,28},{24,16},{28,20},{1,9},{5... | collective-permute-start | bytes 3145736 | tf_op jit(solution)/shard_map/ppermute | solution.py:72
  389.0 39.4 %collective-permute-start.36 = (bf16[256,2048]{1,0:T(8,128)(2,1)}, bf16[256,2048]{1,0:T(8,128)(2,1)}, u32[]{:S(2)}, u32[]{:S(2)}) collective-permute-start(bf16[256,2048]{1,0:T(8,128)(2,1)} %get-tuple-element.162), channel_id=1, source_target_pairs={{0,16},{4,20},{8,24},{12,28},{16,0},{20,4},{24,8},{28,12},{1,17},{... | collective-permute-start | bytes 3145736 | tf_op jit(solution)/shard_map/ppermute | solution.py:72
  429.8 24.8 %collective-permute-start.39 = (bf16[128,2048]{1,0:T(8,128)(2,1)S(1)}, bf16[128,2048]{1,0:T(8,128)(2,1)S(1)}, u32[]{:S(2)}, u32[]{:S(2)}) collective-permute-start(bf16[128,2048]{1,0:T(8,128)(2,1)S(1)} %add_convert_fusion.27.refs_4_), channel_id=1, source_target_pairs={{0,8},{4,12},{8,0},{12,4},{16,24},{20,28},{24,16},{28,20},{1,9},{5... | collective-permute-start | bytes 1572872 | tf_op jit(solution)/shard_map/ppermute | solution.py:72
  444.5 26.7 %collective-permute-start.40 = (bf16[256,2048]{1,0:T(8,128)(2,1)}, bf16[256,2048]{1,0:T(8,128)(2,1)S(1)}, u32[]{:S(2)}, u32[]{:S(2)}) collective-permute-start(bf16[256,2048]{1,0:T(8,128)(2,1)} %get-tuple-element.166.refs_2_), channel_id=1, source_target_pairs={{0,8},{4,12},{8,0},{12,4},{16,24},{20,28},{24,16},{28,20},{1,9},{5... | collective-permute-start | bytes 3145736 | tf_op jit(solution)/shard_map/ppermute | solution.py:72
  445.6 25.5 %collective-permute-start.41 = (bf16[256,2048]{1,0:T(8,128)(2,1)}, bf16[256,2048]{1,0:T(8,128)(2,1)}, u32[]{:S(2)}, u32[]{:S(2)}) collective-permute-start(bf16[256,2048]{1,0:T(8,128)(2,1)} %get-tuple-element.180), channel_id=1, source_target_pairs={{0,16},{4,20},{8,24},{12,28},{16,0},{20,4},{24,8},{28,12},{1,17},{... | collective-permute-start | bytes 3145736 | tf_op jit(solution)/shard_map/ppermute | solution.py:72
  454.6 38.8 %collective-permute-start.47 = (bf16[2,192,2048]{2,1,0:T(8,128)(2,1)}, bf16[2,192,2048]{2,1,0:T(8,128)(2,1)}, u32[]{:S(2)}, u32[]{:S(2)}) collective-permute-start(bf16[2,192,2048]{2,1,0:T(8,128)(2,1)} %get-tuple-element.191), channel_id=1, source_target_pairs={{0,4},{4,0},{8,12},{12,8},{16,20},{20,16},{24,28},{28,24},{1,5},{5... | collective-permute-start | bytes 4718600 | tf_op jit(solution)/shard_map/ppermute | solution.py:72
  474.2 24.0 %collective-permute-start.45 = (bf16[128,2048]{1,0:T(8,128)(2,1)}, bf16[128,2048]{1,0:T(8,128)(2,1)}, u32[]{:S(2)}, u32[]{:S(2)}) collective-permute-start(bf16[128,2048]{1,0:T(8,128)(2,1)} %add_convert_fusion.23), channel_id=1, source_target_pairs={{0,16},{4,20},{8,24},{12,28},{16,0},{20,4},{24,8},{28,12},{1,17},{... | collective-permute-start | bytes 1572872 | tf_op jit(solution)/shard_map/ppermute | solution.py:72
  484.6 41.5 %collective-permute-start.44 = (bf16[128,2048]{1,0:T(8,128)(2,1)}, bf16[128,2048]{1,0:T(8,128)(2,1)S(1)}, u32[]{:S(2)}, u32[]{:S(2)}) collective-permute-start(bf16[128,2048]{1,0:T(8,128)(2,1)} %get-tuple-element.283), channel_id=1, source_target_pairs={{0,1},{1,0},{2,3},{3,2},{4,5},{5,4},{6,7},{7,6},{8,9},{9,8},{10,11... | collective-permute-start | bytes 1572872 | tf_op jit(solution)/shard_map/ppermute | solution.py:75
  492.7 74.0 %collective-permute-start.42 = (bf16[256,2048]{1,0:T(8,128)(2,1)}, bf16[256,2048]{1,0:T(8,128)(2,1)S(1)}, u32[]{:S(2)}, u32[]{:S(2)}) collective-permute-start(bf16[256,2048]{1,0:T(8,128)(2,1)} %get-tuple-element.183), channel_id=1, source_target_pairs={{0,8},{4,12},{8,0},{12,4},{16,24},{20,28},{24,16},{28,20},{1,9},{5... | collective-permute-start | bytes 3145736 | tf_op jit(solution)/shard_map/ppermute | solution.py:72
  493.4 73.4 %collective-permute-start.43 = (bf16[256,2048]{1,0:T(8,128)(2,1)}, bf16[256,2048]{1,0:T(8,128)(2,1)}, u32[]{:S(2)}, u32[]{:S(2)}) collective-permute-start(bf16[256,2048]{1,0:T(8,128)(2,1)} %get-tuple-element.184), channel_id=1, source_target_pairs={{0,16},{4,20},{8,24},{12,28},{16,0},{20,4},{24,8},{28,12},{1,17},{... | collective-permute-start | bytes 3145736 | tf_op jit(solution)/shard_map/ppermute | solution.py:72
  502.7 38.8 %collective-permute-start.48 = (bf16[128,2048]{1,0:T(8,128)(2,1)}, bf16[128,2048]{1,0:T(8,128)(2,1)S(1)}, u32[]{:S(2)}, u32[]{:S(2)}) collective-permute-start(bf16[128,2048]{1,0:T(8,128)(2,1)} %get-tuple-element.280), channel_id=1, source_target_pairs={{0,2},{1,3},{2,0},{3,1},{4,6},{5,7},{6,4},{7,5},{8,10},{9,11},{10,... | collective-permute-start | bytes 1572872 | tf_op jit(solution)/shard_map/ppermute | solution.py:75
  506.0 36.4 %collective-permute-start.49 = (bf16[128,2048]{1,0:T(8,128)(2,1)}, bf16[128,2048]{1,0:T(8,128)(2,1)}, u32[]{:S(2)}, u32[]{:S(2)}) collective-permute-start(bf16[128,2048]{1,0:T(8,128)(2,1)} %get-tuple-element.281), channel_id=1, source_target_pairs={{0,3},{1,2},{2,1},{3,0},{4,7},{5,6},{6,5},{7,4},{8,11},{9,10},{10,... | collective-permute-start | bytes 1572872 | tf_op jit(solution)/shard_map/ppermute | solution.py:75
  526.1 48.0 %collective-permute-start.52 = (bf16[256,2048]{1,0:T(8,128)(2,1)}, bf16[256,2048]{1,0:T(8,128)(2,1)S(1)}, u32[]{:S(2)}, u32[]{:S(2)}) collective-permute-start(bf16[256,2048]{1,0:T(8,128)(2,1)} %get-tuple-element.216), channel_id=1, source_target_pairs={{0,8},{4,12},{8,0},{12,4},{16,24},{20,28},{24,16},{28,20},{1,9},{5... | collective-permute-start | bytes 3145736 | tf_op jit(solution)/shard_map/ppermute | solution.py:72
  541.4 32.7 %collective-permute-start.53 = (bf16[256,2048]{1,0:T(8,128)(2,1)}, bf16[256,2048]{1,0:T(8,128)(2,1)}, u32[]{:S(2)}, u32[]{:S(2)}) collective-permute-start(bf16[256,2048]{1,0:T(8,128)(2,1)} %get-tuple-element.217), channel_id=1, source_target_pairs={{0,16},{4,20},{8,24},{12,28},{16,0},{20,4},{24,8},{28,12},{1,17},{... | collective-permute-start | bytes 3145736 | tf_op jit(solution)/shard_map/ppermute | solution.py:72
  553.5 44.5 %all-to-all-start.7 = ((bf16[4,128,512]{2,1,0:T(8,128)(2,1)}), bf16[4,128,512]{2,1,0:T(8,128)(2,1)S(1)}, u32[]{:S(2)}, u32[]{:S(2)}) async-start(bf16[4,128,512]{2,1,0:T(8,128)(2,1)} %get-tuple-element.208), calls=%async_computation.7 | async-start | bytes 1048576 | tf_op jit(solution)/shard_map/all_to_all | solution.py:78
  569.8 54.1 %collective-permute-start.50 = (bf16[128,2048]{1,0:T(8,128)(2,1)}, bf16[128,2048]{1,0:T(8,128)(2,1)}, u32[]{:S(2)}, u32[]{:S(2)}) collective-permute-start(bf16[128,2048]{1,0:T(8,128)(2,1)} %add_convert_fusion.20), channel_id=1, source_target_pairs={{0,16},{4,20},{8,24},{12,28},{16,0},{20,4},{24,8},{28,12},{1,17},{... | collective-permute-start | bytes 1572872 | tf_op jit(solution)/shard_map/ppermute | solution.py:72
  571.9 52.0 %collective-permute-start.51 = (bf16[128,2048]{1,0:T(8,128)(2,1)S(1)}, bf16[128,2048]{1,0:T(8,128)(2,1)}, u32[]{:S(2)}, u32[]{:S(2)}) collective-permute-start(bf16[128,2048]{1,0:T(8,128)(2,1)S(1)} %add_convert_fusion.19.refs_2_), channel_id=1, source_target_pairs={{0,8},{4,12},{8,0},{12,4},{16,24},{20,28},{24,16},{28,20},{1,9},{5... | collective-permute-start | bytes 1572872 | tf_op jit(solution)/shard_map/ppermute | solution.py:72
  577.1 51.4 %collective-permute-start.54 = (bf16[128,2048]{1,0:T(8,128)(2,1)}, bf16[128,2048]{1,0:T(8,128)(2,1)}, u32[]{:S(2)}, u32[]{:S(2)}) collective-permute-start(bf16[128,2048]{1,0:T(8,128)(2,1)} %add_convert_fusion.15), channel_id=1, source_target_pairs={{0,16},{4,20},{8,24},{12,28},{16,0},{20,4},{24,8},{28,12},{1,17},{... | collective-permute-start | bytes 1572872 | tf_op jit(solution)/shard_map/ppermute | solution.py:72
  580.1 48.3 %collective-permute-start.55 = (bf16[128,2048]{1,0:T(8,128)(2,1)}, bf16[128,2048]{1,0:T(8,128)(2,1)}, u32[]{:S(2)}, u32[]{:S(2)}) collective-permute-start(bf16[128,2048]{1,0:T(8,128)(2,1)} %add_convert_fusion.18.refs_6_), channel_id=1, source_target_pairs={{0,8},{4,12},{8,0},{12,4},{16,24},{20,28},{24,16},{28,20},{1,9},{5... | collective-permute-start | bytes 1572872 | tf_op jit(solution)/shard_map/ppermute | solution.py:72
  623.9 31.5 %collective-permute-start.56 = (bf16[1024,2176]{1,0:T(8,128)(2,1)}, bf16[1024,2176]{1,0:T(8,128)(2,1)}, u32[]{:S(2)}, u32[]{:S(2)}) collective-permute-start(bf16[1024,2176]{1,0:T(8,128)(2,1)} %get-tuple-element.236), channel_id=1, source_target_pairs={{0,4},{4,0},{8,12},{12,8},{16,20},{20,16},{24,28},{28,24},{1,5},{5... | collective-permute-start | bytes 13369352 | tf_op jit(solution)/shard_map/ppermute | solution.py:72
  633.5 54.2 %all-to-all-start.8 = ((bf16[4,128,2048]{2,1,0:T(8,128)(2,1)}), bf16[4,128,2048]{2,1,0:T(8,128)(2,1)S(1)}, u32[]{:S(2)}, u32[]{:S(2)}) async-start(bf16[4,128,2048]{2,1,0:T(8,128)(2,1)} %maximum_select_fusion.1), calls=%async_computation.8 | async-start | bytes 4194304 | tf_op jit(solution)/shard_map/all_to_all | solution.py:78
  702.4 27.7 %collective-permute-start.61 = (bf16[256,2176]{1,0:T(8,128)(2,1)}, bf16[256,2176]{1,0:T(8,128)(2,1)}, u32[]{:S(2)}, u32[]{:S(2)}) collective-permute-start(bf16[256,2176]{1,0:T(8,128)(2,1)} %get-tuple-element.255), channel_id=1, source_target_pairs={{0,16},{4,20},{8,24},{12,28},{16,0},{20,4},{24,8},{28,12},{1,17},{... | collective-permute-start | bytes 3342344 | tf_op jit(solution)/shard_map/ppermute | solution.py:72
  703.2 27.7 %collective-permute-start.60 = (bf16[256,2176]{1,0:T(8,128)(2,1)}, bf16[256,2176]{1,0:T(8,128)(2,1)}, u32[]{:S(2)}, u32[]{:S(2)}) collective-permute-start(bf16[256,2176]{1,0:T(8,128)(2,1)} %get-tuple-element.256), channel_id=1, source_target_pairs={{0,8},{4,12},{8,0},{12,4},{16,24},{20,28},{24,16},{28,20},{1,9},{5... | collective-permute-start | bytes 3342344 | tf_op jit(solution)/shard_map/ppermute | solution.py:72
  704.1 59.4 %all-to-all-start.10 = ((bf16[4,128,2048]{2,1,0:T(8,128)(2,1)}), bf16[4,128,2048]{2,1,0:T(8,128)(2,1)}, u32[]{:S(2)}, u32[]{:S(2)}) async-start(bf16[4,128,2048]{2,1,0:T(8,128)(2,1)} %shard_map.304.refs_2_), calls=%async_computation.10 | async-start | bytes 4194304 | tf_op jit(solution)/shard_map/all_to_all | solution.py:78
  715.7 32.6 %collective-permute-start.59 = (bf16[256,1664]{1,0:T(8,128)(2,1)}, bf16[256,1664]{1,0:T(8,128)(2,1)}, u32[]{:S(2)}, u32[]{:S(2)}) collective-permute-start(bf16[256,1664]{1,0:T(8,128)(2,1)} %get-tuple-element.260), channel_id=1, source_target_pairs={{0,16},{4,20},{8,24},{12,28},{16,0},{20,4},{24,8},{28,12},{1,17},{... | collective-permute-start | bytes 2555912 | tf_op jit(solution)/shard_map/ppermute | solution.py:72
  716.8 32.3 %collective-permute-start.58 = (bf16[256,1664]{1,0:T(8,128)(2,1)}, bf16[256,1664]{1,0:T(8,128)(2,1)}, u32[]{:S(2)}, u32[]{:S(2)}) collective-permute-start(bf16[256,1664]{1,0:T(8,128)(2,1)} %get-tuple-element.261), channel_id=1, source_target_pairs={{0,8},{4,12},{8,0},{12,4},{16,24},{20,28},{24,16},{28,20},{1,9},{5... | collective-permute-start | bytes 2555912 | tf_op jit(solution)/shard_map/ppermute | solution.py:72
  735.4 24.4 %collective-permute-start.64 = (bf16[128,2176]{1,0:T(8,128)(2,1)}, bf16[128,2176]{1,0:T(8,128)(2,1)}, u32[]{:S(2)}, u32[]{:S(2)}) collective-permute-start(bf16[128,2176]{1,0:T(8,128)(2,1)} %add_convert_fusion.8), channel_id=1, source_target_pairs={{0,16},{4,20},{8,24},{12,28},{16,0},{20,4},{24,8},{28,12},{1,17},{... | collective-permute-start | bytes 1671176 | tf_op jit(solution)/shard_map/ppermute | solution.py:72
  763.5 30.7 %all-to-all-start.12 = ((bf16[4,64,2176]{2,1,0:T(8,128)(2,1)}), bf16[4,64,2176]{2,1,0:T(8,128)(2,1)S(1)}, u32[]{:S(2)}, u32[]{:S(2)}) async-start(bf16[4,64,2176]{2,1,0:T(8,128)(2,1)} %bitcast.127), calls=%async_computation.12 | async-start | bytes 2228224 | tf_op jit(solution)/shard_map/all_to_all | solution.py:78
  794.2 24.5 %all-to-all-start.11 = ((bf16[4,64,1664]{2,1,0:T(8,128)(2,1)}), bf16[4,64,1664]{2,1,0:T(8,128)(2,1)S(1)}, u32[]{:S(2)}, u32[]{:S(2)}) async-start(bf16[4,64,1664]{2,1,0:T(8,128)(2,1)} %bitcast.125), calls=%async_computation.11 | async-start | bytes 1703936 | tf_op jit(solution)/shard_map/all_to_all | solution.py:78
  (127 other events, 912.6 us)
Sparse Core Ops, SparseCore 0:
  149.7 57.2 all-gather.2

commit v4 on v3

--- a/solution.py
+++ b/solution.py
@@ -865,7 +865,10 @@
         results.append(result(done[i][cores + 1], last))
         last = results[i][0]
     totals.append(links.reduce_end(more[0], group * tok, last))
-    out_arrays.append(put_rows(0, results[0], totals[0]))
+    dgate_back = after(dgate_back, results[0][0])
+    dprob = jnp.sum(dgate_back.reshape(E, ndev * experts // E, tok), axis=1).T
+    dprob = jnp.pad(dprob, ((0, 0), (0, LANES - E)))
+    out_arrays.append(put_rows(0, results[0], totals[0], dprob))
     last = out_arrays[0][0]
     for i in range(1, groups):
         more.append(links.reduce_next(begun[i], last))
@@ -879,10 +882,7 @@
         totals.append(links.reduce_end(more[i], group * tok, last))
         last = totals[i]
     dmoe_terms = links.sum_slots([t for total in totals for t in cut_group(total)])
-    dgate_back = after(dgate_back, out_arrays[0][0])
-    dprob = jnp.sum(dgate_back.reshape(E, ndev * experts // E, tok), axis=1).T
-    dprob = jnp.pad(dprob, ((0, 0), (0, LANES - E)))
-    grad_w_out = grad_out_pieces(inners, g_rows, last, dprob)
+    grad_w_out = grad_out_pieces(inners, g_rows, last)
     out_begun.append(links.reduce_start(held(out_arrays[-1], grad_w_out)))
     dmoe_terms = held(dmoe_terms, grad_w_out)
 
@@ -967,15 +967,13 @@
     for j in range(1, experts):
         grad_w_in = grad_in_pieces(j, grad_w_in, dqkv, *grad_o_begun[2:3])
         last = grad_w_in
-    grad_qkv_terms = dense_terms(normed, dqkv, gain_terms, last, out_terms)
-    last = grad_qkv_terms[0]
+    grad_o_more = links.reduce_next(grad_o_begun, last)
+    grad_qkv_terms = dense_terms(normed, dqkv, gain_terms, grad_o_more[-1], out_terms)
     dnormed_terms = after(dnormed_terms.reshape(nc, tok, dim), out_terms)
-    grad_qkv_begun = links.dense_start(grad_qkv_terms, fsdp_rows, last, dnormed_terms)
+    grad_qkv_begun = links.dense_start(grad_qkv_terms, fsdp_rows, dnormed_terms)
     dnormed_terms = links.exchange(dnormed_terms)
-    last = grad_qkv_begun[-1]
-    grad_o_more = links.reduce_next(grad_o_begun, last)
-    grad_qkv_more = links.reduce_next(grad_qkv_begun, grad_o_more[-1])
-    grad_o_total = links.reduce_end(grad_o_more, fsdp_rows, grad_qkv_more[-1])
+    grad_o_total = links.reduce_end(grad_o_more, fsdp_rows, grad_qkv_begun[-1])
+    grad_qkv_more = links.reduce_next(grad_qkv_begun, grad_o_total)
     grad_o = links.exchange(grad_o_total.reshape(nc, own_rows, -1))
     grad_qkv_total = links.reduce_end(grad_qkv_more, fsdp_rows, grad_o_total)
     dnormed_terms = after(dnormed_terms, grad_qkv_total)

time: 848 us -> 845 us (level)
  local copies, waits for them, and re-layouts: 109 us -> 99.3 us
    unnamed x208 -> x218, local copies, waits for them, and re-layouts: 38.7 us -> 29.9 us
  transfers between devices with their start and end apart: 80 -> 80, of which waited for: 30 -> 37; matrix products, arithmetic and copies ran while one was open for 16% -> 17% of each run, Pallas kernels for 27% -> 25%
where the time goes in v4:
time: 845 us; the launch traced here: 834 us
  waiting for transfers between devices  272 us (32%)
  Pallas kernels  238 us (28%)
  starting transfers between devices  124 us (15%)
  local copies, waits for them, and re-layouts  99.3 us (12%)
  other arithmetic  83.9 us (10%)
  between operations  16.3 us (2%)
    pallas_call x22, Pallas kernels, call(): return lambda *operands: made(*operands, *gate)  229 us
    ppermute x61, waiting for transfers between devices, swap(): return lax.ppermute(value, 'fsdp', [(i, i ^ mask) for i in range(self.nf)])  137 us
    all_to_all x12, waiting for transfers between devices, exchange(): return lax.all_to_all(value, 'ctx', split_axis=0, concat_axis=0, tiled=True)  104 us
    all_to_all x12, starting transfers between devices, exchange(): return lax.all_to_all(value, 'ctx', split_axis=0, concat_axis=0, tiled=True)  62.3 us
    ppermute x61, starting transfers between devices, swap(): return lax.ppermute(value, 'fsdp', [(i, i ^ mask) for i in range(self.nf)])  46 us
    convert_element_type x20, other arithmetic, add_low(): return sum((t.astype(F32) for t in terms)).astype(BF)  43.2 us
    unnamed x218, local copies, waits for them, and re-layouts  29.9 us
    ppermute x5, waiting for transfers between devices, cswap(): return lax.ppermute(value, 'ctx', [(i, i ^ mask) for i in range(self.nc)])  26.1 us
  transfers between devices with their start and end apart: 80, of which 37 were waited for; matrix products, arithmetic and copies ran while one was open for 17% of the time, Pallas kernels for 25%

profile of v4, /device:TPU:0, one launch (start us, length us, event | category | flops | bytes accessed | tf_op | source)
XLA Modules:
  0.0 833.7 jit_solution(12482777327171271737)
XLA Ops:
  14.8 6.4 all-to-all-start
  21.4 43.9 %all-to-all-done = bf16[4,64,3712]{2,1,0:T(8,128)(2,1)S(1)} async-done(((bf16[4,64,3712]{2,1,0:T(8,128)(2,1)}), bf16[4,64,3712]{2,1,0:T(8,128)(2,1)S(1)}, u32[]{:S(2)}, u32[]{:S(2)}) %all-to-all-start) | async-done | bytes 1900576 | tf_op jit(solution)/shard_map/all_to_all | solution.py:78
  81.2 5.4 collective-permute-done.1.refs_0_
  94.9 7.4 collective-permute-done.5
  116.0 16.0 %collective-permute-done.8.refs_8_.refs_16_ = bf16[256,2048]{1,0:T(8,128)(2,1)} collective-permute-done((bf16[256,2048]{1,0:T(8,128)(2,1)}, bf16[256,2048]{1,0:T(8,128)(2,1)}, u32[]{:S(2)}, u32[]{:S(2)}) %collective-permute-start.8) | collective-permute-done | bytes 1048608 | tf_op jit(solution)/shard_map/ppermute | solution.py:72
  137.2 9.6 %shard_map.258 = (bf16[512,2048]{1,0:T(8,128)(2,1)}, f32[2,512,512]{2,1,0:T(8,128)}, bf16[512,512]{1,0:T(8,128)(2,1)}, f32[2,8,512]{2,1,0:T(8,128)}) custom-call(s32[8]{0:T(128)} %iota_xor_fusion.refs_0_, f32[1,2048]{1,0:T(1,128)} %copy.312.refs_1_, bf16[512,2048]{1,0:T(8,128)(2,1)} %bitcast.272, bf16[256,1664]{1,0:T(8,128)(2,1)} %pad_maximum_fusion.9.refs_3_.refs_7_, ...), custom_call_target="tpu_custom_call" | custom-call | flops 160000000 | bytes 650000 | tf_op jit(solution)/shard_map/pallas_call | solution.py:241
  162.9 7.0 shard_map.259
  175.3 5.0 all-to-all-start.3
  189.2 6.0 all-to-all-done.3.refs_3_
  195.2 6.3 shard_map.261
  201.5 13.1 %collective-permute-done.16.refs_1_ = bf16[128,2048]{1,0:T(8,128)(2,1)S(1)} collective-permute-done((bf16[128,2048]{1,0:T(8,128)(2,1)}, bf16[128,2048]{1,0:T(8,128)(2,1)S(1)}, u32[]{:S(2)}, u32[]{:S(2)}) %collective-permute-start.16) | collective-permute-done | bytes 524320 | tf_op jit(solution)/shard_map/ppermute | solution.py:75
  224.6 9.0 %shard_map.264.refs_2_.refs_6_ = bf16[2,384,2048]{2,1,0:T(8,128)(2,1)} custom-call(s32[8]{0:T(128)} %broadcast_xor_fusion.places, bf16[8,96,256]{2,1,0:T(8,128)(2,1)} %broadcast_multiply_fusion.1.refs_16_.slots, bf16[8,256,2048]{2,1,0:T(8,128)(2,1)} %bitcast.285), custom_call_target="tpu_custom_call" | custom-call | flops 40000000 | bytes 600000 | tf_op jit(solution)/shard_map/pallas_call | solution.py:708
  233.6 12.8 %collective-permute-done.17.refs_0_ = bf16[256,2048]{1,0:T(8,128)(2,1)S(1)} collective-permute-done((bf16[256,2048]{1,0:T(8,128)(2,1)}, bf16[256,2048]{1,0:T(8,128)(2,1)S(1)}, u32[]{:S(2)}, u32[]{:S(2)}) %collective-permute-start.17) | collective-permute-done | bytes 1048608 | tf_op jit(solution)/shard_map/ppermute | solution.py:72
  252.3 15.7 %all-to-all-done.4.refs_0_ = bf16[4,128,2048]{2,1,0:T(8,128)(2,1)S(1)} async-done(((bf16[4,128,2048]{2,1,0:T(8,128)(2,1)}), bf16[4,128,2048]{2,1,0:T(8,128)(2,1)S(1)}, u32[]{:S(2)}, u32[]{:S(2)}) %all-to-all-start.4) | async-done | bytes 2097184 | tf_op jit(solution)/shard_map/all_to_all | solution.py:78
  271.2 4.7 all-to-all-start.5
  286.2 32.0 %shard_map.269 = (bf16[2,192,2048]{2,1,0:T(8,128)(2,1)}, bf16[2,192,2048]{2,1,0:T(8,128)(2,1)}, bf16[4,384,1024]{2,1,0:T(8,128)(2,1)}, bf16[2,384,1024]{2,1,0:T(8,128)(2,1)}, f32[2,384,128]{2,1,0:T(8,128)}) custom-call(s32[1]{0:T(128)} %bitcast.69.refs_0_, bf16[2048,128]{1,0:T(8,128)(2,1)} %get-tuple-element.252.refs_1_.refs_6_, ...), custom_call_target="tpu_custom_call" | custom-call | flops 1700000000 | bytes 1500000 | tf_op jit(solution)/shard_map/pallas_call | solution.py:241
  333.6 27.0 %collective-permute-done.25.refs_4_ = bf16[128,2048]{1,0:T(8,128)(2,1)S(1)} collective-permute-done((bf16[128,2048]{1,0:T(8,128)(2,1)S(1)}, bf16[128,2048]{1,0:T(8,128)(2,1)S(1)}, u32[]{:S(2)}, u32[]{:S(2)}) %collective-permute-start.25) | collective-permute-done | bytes 524320 | tf_op jit(solution)/shard_map/ppermute | solution.py:72
  370.3 9.6 %collective-permute-done.31.refs_4_ = bf16[128,2048]{1,0:T(8,128)(2,1)S(1)} collective-permute-done((bf16[128,2048]{1,0:T(8,128)(2,1)S(1)}, bf16[128,2048]{1,0:T(8,128)(2,1)S(1)}, u32[]{:S(2)}, u32[]{:S(2)}) %collective-permute-start.31) | collective-permute-done | bytes 524320 | tf_op jit(solution)/shard_map/ppermute | solution.py:72
  382.6 4.5 shard_map.276
  392.0 32.1 %shard_map.277 = (bf16[2,192,2048]{2,1,0:T(8,128)(2,1)}, bf16[2,192,2048]{2,1,0:T(8,128)(2,1)}, bf16[4,384,1024]{2,1,0:T(8,128)(2,1)}, bf16[2,384,1024]{2,1,0:T(8,128)(2,1)}, f32[2,384,128]{2,1,0:T(8,128)}) custom-call(s32[1]{0:T(128)} %bitcast.69.refs_0_, bf16[2048,128]{1,0:T(8,128)(2,1)} %get-tuple-element.252.refs_1_.refs_6_, ...), custom_call_target="tpu_custom_call" | custom-call | flops 1700000000 | bytes 1500000 | tf_op jit(solution)/shard_map/pallas_call | solution.py:241
  434.0 4.3 shard_map.280
  438.3 7.1 shard_map.281
  447.8 6.9 all-to-all-start.6
  454.7 7.2 shard_map.282
  467.6 4.7 all-to-all-done.6.refs_0_
  474.5 4.3 shard_map.285
  490.9 4.3 shard_map.288
  510.4 15.6 %shard_map.290.refs_4_.refs_5_ = f32[2,1024,2048]{2,1,0:T(8,128)} custom-call(bf16[2,384,1024]{2,1,0:T(8,128)(2,1)} %get-tuple-element.142.refs_0_, bf16[2,384,1024]{2,1,0:T(8,128)(2,1)} %get-tuple-element.170.refs_0_.refs_1_, bf16[2,384,2048]{2,1,0:T(8,128)(2,1)} %shard_map.264.refs_2_.refs_6_, ...), custom_call_target="tpu_custom_call" | custom-call | flops 325000000 | bytes 1300000 | tf_op jit(solution)/shard_map/pallas_call | solution.py:241
  526.9 12.9 %collective-permute-done.48.refs_2_ = bf16[128,2048]{1,0:T(8,128)(2,1)S(1)} collective-permute-done((bf16[128,2048]{1,0:T(8,128)(2,1)}, bf16[128,2048]{1,0:T(8,128)(2,1)S(1)}, u32[]{:S(2)}, u32[]{:S(2)}) %collective-permute-start.48) | collective-permute-done | bytes 524320 | tf_op jit(solution)/shard_map/ppermute | solution.py:75
  541.6 10.1 %shard_map.292 = (f32[128,2048]{1,0:T(8,128)}, f32[2048,128]{1,0:T(8,128)}, f32[8,2048]{1,0:T(8,128)}, bf16[128,2048]{1,0:T(8,128)(2,1)}, bf16[4,128,512]{2,1,0:T(8,128)(2,1)}) custom-call(s32[8]{0:T(128)} %iota_xor_fusion.refs_0_, f32[128,2048]{1,0:T(8,128)} %get-tuple-element.136.refs_1_, f32[128,128]{1,0:T(8,128)} %get-tuple-element.187.refs_2_, ...), custom_call_target="tpu_custom_call" | custom-call | flops 65000000 | bytes 750000 | tf_op jit(solution)/shard_map/pallas_call | solution.py:241
  551.7 12.3 %all-to-all-start.7 = ((bf16[4,128,512]{2,1,0:T(8,128)(2,1)}), bf16[4,128,512]{2,1,0:T(8,128)(2,1)S(1)}, u32[]{:S(2)}, u32[]{:S(2)}) async-start(bf16[4,128,512]{2,1,0:T(8,128)(2,1)} %get-tuple-element.208), calls=%async_computation.7 | async-start | bytes 1048576 | tf_op jit(solution)/shard_map/all_to_all | solution.py:78
  573.3 16.6 %shard_map.296.refs_1_.refs_6_ = f32[4,2048,1024]{2,1,0:T(8,128)} custom-call(bf16[2,192,2048]{2,1,0:T(8,128)(2,1)} %get-tuple-element.140.refs_4_.refs_7_.refs_0_, bf16[2,192,2048]{2,1,0:T(8,128)(2,1)} %copy-done.10, bf16[2,192,2048]{2,1,0:T(8,128)(2,1)} %get-tuple-element.148.refs_2_.refs_4_, bf16[2,192,2048]{2,1,0:T(8,128)(2,1)} %copy-done.11, ...), custom_call_target="tpu_custom_call" | custom-call | flops 325000000 | bytes 1250000 | tf_op jit(solution)/shard_map/pallas_call | solution.py:241
  590.7 11.6 %shard_map.298 = (f32[2,512,512]{2,1,0:T(8,128)}, bf16[512,512]{1,0:T(8,128)(2,1)}, f32[2,8,512]{2,1,0:T(8,128)}, f32[2,8,512]{2,1,0:T(8,128)}) custom-call(f32[2,512,512]{2,1,0:T(8,128)} %get-tuple-element.132.refs_0_.refs_2_, bf16[2,512,512]{2,1,0:T(8,128)(2,1)} %get-tuple-element.207.refs_1_, bf16[512,512]{1,0:T(8,128)(2,1)} %get-tuple-element.133.refs_1_.refs_2_, ...), custom_call_target="tpu_custom_call" | custom-call | flops 70000000 | bytes 500000 | tf_op jit(solution)/shard_map/pallas_call | solution.py:241
  602.4 7.3 shard_map.299
  617.3 5.1 all-to-all-start.9
  634.0 4.6 collective-permute-done.55.refs_1_
  643.9 5.3 all-to-all-start.8
  651.3 11.0 %shard_map.303 = (bf16[512,1536]{1,0:T(8,128)(2,1)}, bf16[512,2048]{1,0:T(8,128)(2,1)}, f32[8,2048]{1,0:T(8,128)}) custom-call(s32[8]{0:T(128)} %iota_xor_fusion.refs_0_, f32[2,512,512]{2,1,0:T(8,128)} %get-tuple-element.229.refs_1_, f32[2,512,512]{2,1,0:T(8,128)} %get-tuple-element.132.refs_0_.refs_2_, f32[2,512,128]{2,1,0:T(8,128)} %broadcast_in_dim.100.refs_2_.refs_3_, ...), custom_call_target="tpu_custom_call" | custom-call | flops 165000000 | bytes 750000 | tf_op jit(solution)/shard_map/pallas_call | solution.py:241
  663.1 5.1 add_convert_fusion
  675.2 16.6 %shard_map.306.refs_2_ = f32[4,2048,1024]{2,1,0:T(8,128)} custom-call(bf16[2,192,2048]{2,1,0:T(8,128)(2,1)} %get-tuple-element.140.refs_4_.refs_7_.refs_0_, bf16[2,192,2048]{2,1,0:T(8,128)(2,1)} %copy-done.10, bf16[2,192,2048]{2,1,0:T(8,128)(2,1)} %get-tuple-element.148.refs_2_.refs_4_, ...), custom_call_target="tpu_custom_call", output_to_operand_aliasing={{}: (6, {})} | custom-call | flops 325000000 | bytes 1250000 | tf_op jit(solution)/shard_map/pallas_call | solution.py:241
  698.8 8.4 %shard_map.308 = (bf16[1024,1664]{1,0:T(8,128)(2,1)}, bf16[1024,1664]{1,0:T(8,128)(2,1)}) custom-call(s32[8]{0:T(128)} %iota_xor_fusion.refs_0_, bf16[512,2048]{1,0:T(8,128)(2,1)} %get-tuple-element.232.refs_1_, bf16[512,1536]{1,0:T(8,128)(2,1)} %get-tuple-element.233.refs_1_.refs_7_.refs_2_, bf16[2048,128]{1,0:T(8,128)(2,1)} %pad_bitcast_fusion.refs_3_, ...), custom_call_target="tpu_custom_call" | custom-call | flops 161061280 | bytes 314572 | tf_op jit(solution)/shard_map/pallas_call | solution.py:241
  707.2 5.0 all-to-all-start.10
  722.7 8.6 %collective-permute-done.62.refs_0_ = bf16[128,2176]{1,0:T(8,128)(2,1)} collective-permute-done((bf16[128,2176]{1,0:T(8,128)(2,1)}, bf16[128,2176]{1,0:T(8,128)(2,1)}, u32[]{:S(2)}, u32[]{:S(2)}) %collective-permute-start.62) | collective-permute-done | bytes 557088 | tf_op jit(solution)/shard_map/ppermute | solution.py:72
  734.3 12.4 %collective-permute-done.60.refs_0_ = bf16[256,1664]{1,0:T(8,128)(2,1)S(1)} collective-permute-done((bf16[256,1664]{1,0:T(8,128)(2,1)}, bf16[256,1664]{1,0:T(8,128)(2,1)S(1)}, u32[]{:S(2)}, u32[]{:S(2)}) %collective-permute-start.60) | collective-permute-done | bytes 852000 | tf_op jit(solution)/shard_map/ppermute | solution.py:72
  748.6 12.5 %all-to-all-done.10.refs_0_ = bf16[4,128,2048]{2,1,0:T(8,128)(2,1)} async-done(((bf16[4,128,2048]{2,1,0:T(8,128)(2,1)}), bf16[4,128,2048]{2,1,0:T(8,128)(2,1)}, u32[]{:S(2)}, u32[]{:S(2)}) %all-to-all-start.10) | async-done | bytes 2097184 | tf_op jit(solution)/shard_map/all_to_all | solution.py:78
  769.7 8.3 collective-permute-done.64.refs_0_
  783.6 8.2 all-to-all-done.12
  800.1 16.1 %all-to-all-done.11 = bf16[4,64,1664]{2,1,0:T(8,128)(2,1)S(1)} async-done(((bf16[4,64,1664]{2,1,0:T(8,128)(2,1)}), bf16[4,64,1664]{2,1,0:T(8,128)(2,1)S(1)}, u32[]{:S(2)}, u32[]{:S(2)}) %all-to-all-start.11) | async-done | bytes 852000 | tf_op jit(solution)/shard_map/all_to_all | solution.py:78
  (599 shorter events, 291.3 us)
Async XLA Ops:
  14.8 50.4 %all-to-all-start = ((bf16[4,64,3712]{2,1,0:T(8,128)(2,1)}), bf16[4,64,3712]{2,1,0:T(8,128)(2,1)S(1)}, u32[]{:S(2)}, u32[]{:S(2)}) async-start(bf16[4,64,3712]{2,1,0:T(8,128)(2,1)} %pad_maximum_fusion), calls=%async_computation | async-start | bytes 3801088 | tf_op jit(solution)/shard_map/all_to_all | solution.py:78
  69.5 23.8 %collective-permute-start = (bf16[256,1664]{1,0:T(8,128)(2,1)}, bf16[256,1664]{1,0:T(8,128)(2,1)}, u32[]{:S(2)}, u32[]{:S(2)}) collective-permute-start(bf16[256,1664]{1,0:T(8,128)(2,1)} %pad_maximum_fusion.9.refs_3_.refs_7_), channel_id=1, source_target_pairs={{0,4},{4,0},{8,12},{12,8},{16,20},{20,16},{24,28},{28,24},{1,5},{5... | collective-permute-start | bytes 2555912 | tf_op jit(solution)/shard_map/ppermute | solution.py:72
  76.7 59.2 %all-to-all-start.1 = ((bf16[4,128,2048]{2,1,0:T(8,128)(2,1)}), bf16[4,128,2048]{2,1,0:T(8,128)(2,1)S(1)}, u32[]{:S(2)}, u32[]{:S(2)}) async-start(bf16[4,128,2048]{2,1,0:T(8,128)(2,1)} %shard_map.255.refs_2_), calls=%async_computation.1 | async-start | bytes 4194304 | tf_op jit(solution)/shard_map/all_to_all | solution.py:78
  80.3 144.3 %all-gather.3.cloned.1.call-start = ((), (), s32[]{:S(2)}) async-start(), calls=%async_computation.13 | async-start | bytes 9437184 | tf_op jit(solution)/shard_map/all_gather | solution.py:586
  106.6 25.5 %collective-permute-start.8 = (bf16[256,2048]{1,0:T(8,128)(2,1)}, bf16[256,2048]{1,0:T(8,128)(2,1)}, u32[]{:S(2)}, u32[]{:S(2)}) collective-permute-start(bf16[256,2048]{1,0:T(8,128)(2,1)} %shard_map.257.refs_4_.refs_12_), channel_id=1, source_target_pairs={{0,16},{4,20},{8,24},{12,28},{16,0},{20,4},{24,8},{28,12},{1,17},{... | collective-permute-start | bytes 3145736 | tf_op jit(solution)/shard_map/ppermute | solution.py:72
  108.1 25.9 %collective-permute-start.9 = (bf16[256,2048]{1,0:T(8,128)(2,1)}, bf16[256,2048]{1,0:T(8,128)(2,1)}, u32[]{:S(2)}, u32[]{:S(2)}) collective-permute-start(bf16[256,2048]{1,0:T(8,128)(2,1)} %shard_map.257.refs_4_.refs_12_), channel_id=1, source_target_pairs={{0,8},{4,12},{8,0},{12,4},{16,24},{20,28},{24,16},{28,20},{1,9},{5... | collective-permute-start | bytes 3145736 | tf_op jit(solution)/shard_map/ppermute | solution.py:72
  109.0 37.8 %collective-permute-start.19 = (bf16[128,2048]{1,0:T(8,128)(2,1)}, bf16[128,2048]{1,0:T(8,128)(2,1)}, u32[]{:S(2)}, u32[]{:S(2)}) collective-permute-start(bf16[128,2048]{1,0:T(8,128)(2,1)} %shard_map.262), channel_id=1, source_target_pairs={{0,1},{1,0},{2,3},{3,2},{4,5},{5,4},{6,7},{7,6},{8,9},{9,8},{10,11... | collective-permute-start | bytes 1572872 | tf_op jit(solution)/shard_map/ppermute | solution.py:75
  156.0 33.2 %collective-permute-start.10 = (bf16[256,2048]{1,0:T(8,128)(2,1)S(1)}, bf16[256,2048]{1,0:T(8,128)(2,1)}, u32[]{:S(2)}, u32[]{:S(2)}) collective-permute-start(bf16[256,2048]{1,0:T(8,128)(2,1)S(1)} %copy-done.6), channel_id=1, source_target_pairs={{0,4},{4,0},{8,12},{12,8},{16,20},{20,16},{24,28},{28,24},{1,5},{5... | collective-permute-start | bytes 3145736 | tf_op jit(solution)/shard_map/ppermute | solution.py:72
  161.3 33.8 %collective-permute-start.11 = (bf16[256,2048]{1,0:T(8,128)(2,1)}, bf16[256,2048]{1,0:T(8,128)(2,1)}, u32[]{:S(2)}, u32[]{:S(2)}) collective-permute-start(bf16[256,2048]{1,0:T(8,128)(2,1)} %collective-permute-done.9.refs_6_.refs_14_), channel_id=1, source_target_pairs={{0,4},{4,0},{8,12},{12,8},{16,20},{20,16},{24,28},{28,24},{1,5},{5... | collective-permute-start | bytes 3145736 | tf_op jit(solution)/shard_map/ppermute | solution.py:72
  161.3 33.8 %collective-permute-start.12 = (bf16[256,2048]{1,0:T(8,128)(2,1)}, bf16[256,2048]{1,0:T(8,128)(2,1)}, u32[]{:S(2)}, u32[]{:S(2)}) collective-permute-start(bf16[256,2048]{1,0:T(8,128)(2,1)} %collective-permute-done.8.refs_8_.refs_16_), channel_id=1, source_target_pairs={{0,4},{4,0},{8,12},{12,8},{16,20},{20,16},{24,28},{28,24},{1,5},{5... | collective-permute-start | bytes 3145736 | tf_op jit(solution)/shard_map/ppermute | solution.py:72
  217.5 50.5 %all-to-all-start.4 = ((bf16[4,128,2048]{2,1,0:T(8,128)(2,1)}), bf16[4,128,2048]{2,1,0:T(8,128)(2,1)S(1)}, u32[]{:S(2)}, u32[]{:S(2)}) async-start(bf16[4,128,2048]{2,1,0:T(8,128)(2,1)} %shard_map.266), calls=%async_computation.4 | async-start | bytes 4194304 | tf_op jit(solution)/shard_map/all_to_all | solution.py:78
  222.9 23.4 %collective-permute-start.17 = (bf16[256,2048]{1,0:T(8,128)(2,1)}, bf16[256,2048]{1,0:T(8,128)(2,1)S(1)}, u32[]{:S(2)}, u32[]{:S(2)}) collective-permute-start(bf16[256,2048]{1,0:T(8,128)(2,1)} %constant_dynamic-update-slice_fusion.4.refs_1_), channel_id=1, source_target_pairs={{0,8},{4,12},{8,0},{12,4},{16,24},{20,28},{24,16},{28,20},{1,9},{5... | collective-permute-start | bytes 3145736 | tf_op jit(solution)/shard_map/ppermute | solution.py:72
  224.0 23.3 %collective-permute-start.18 = (bf16[256,2048]{1,0:T(8,128)(2,1)}, bf16[256,2048]{1,0:T(8,128)(2,1)}, u32[]{:S(2)}, u32[]{:S(2)}) collective-permute-start(bf16[256,2048]{1,0:T(8,128)(2,1)} %constant_dynamic-update-slice_fusion.4.refs_1_), channel_id=1, source_target_pairs={{0,16},{4,20},{8,24},{12,28},{16,0},{20,4},{24,8},{28,12},{1,17},{... | collective-permute-start | bytes 3145736 | tf_op jit(solution)/shard_map/ppermute | solution.py:72
  271.2 52.5 %all-to-all-start.5 = ((bf16[4,128,2048]{2,1,0:T(8,128)(2,1)}), bf16[4,128,2048]{2,1,0:T(8,128)(2,1)}, u32[]{:S(2)}, u32[]{:S(2)}) async-start(bf16[4,128,2048]{2,1,0:T(8,128)(2,1)} %shard_map.271), calls=%async_computation.5 | async-start | bytes 4194304 | tf_op jit(solution)/shard_map/all_to_all | solution.py:78
  281.4 37.0 %collective-permute-start.23 = (bf16[256,2048]{1,0:T(8,128)(2,1)S(1)}, bf16[256,2048]{1,0:T(8,128)(2,1)}, u32[]{:S(2)}, u32[]{:S(2)}) collective-permute-start(bf16[256,2048]{1,0:T(8,128)(2,1)S(1)} %copy-done.14), channel_id=1, source_target_pairs={{0,8},{4,12},{8,0},{12,4},{16,24},{20,28},{24,16},{28,20},{1,9},{5... | collective-permute-start | bytes 3145736 | tf_op jit(solution)/shard_map/ppermute | solution.py:72
  282.6 35.8 %collective-permute-start.24 = (bf16[256,2048]{1,0:T(8,128)(2,1)S(1)}, bf16[256,2048]{1,0:T(8,128)(2,1)}, u32[]{:S(2)}, u32[]{:S(2)}) collective-permute-start(bf16[256,2048]{1,0:T(8,128)(2,1)S(1)} %copy-done.14), channel_id=1, source_target_pairs={{0,16},{4,20},{8,24},{12,28},{16,0},{20,4},{24,8},{28,12},{1,17},{... | collective-permute-start | bytes 3145736 | tf_op jit(solution)/shard_map/ppermute | solution.py:72
  325.1 40.6 %collective-permute-start.29 = (bf16[256,2048]{1,0:T(8,128)(2,1)S(1)}, bf16[256,2048]{1,0:T(8,128)(2,1)S(1)}, u32[]{:S(2)}, u32[]{:S(2)}) collective-permute-start(bf16[256,2048]{1,0:T(8,128)(2,1)S(1)} %pad_maximum_fusion.4.refs_3_.refs_1_), channel_id=1, source_target_pairs={{0,8},{4,12},{8,0},{12,4},{16,24},{20,28},{24,16},{28,20},{1,9},{5... | collective-permute-start | bytes 3145736 | tf_op jit(solution)/shard_map/ppermute | solution.py:72
  326.3 39.4 %collective-permute-start.30 = (bf16[256,2048]{1,0:T(8,128)(2,1)S(1)}, bf16[256,2048]{1,0:T(8,128)(2,1)}, u32[]{:S(2)}, u32[]{:S(2)}) collective-permute-start(bf16[256,2048]{1,0:T(8,128)(2,1)S(1)} %pad_maximum_fusion.4.refs_3_.refs_1_), channel_id=1, source_target_pairs={{0,16},{4,20},{8,24},{12,28},{16,0},{20,4},{24,8},{28,12},{1,17},{... | collective-permute-start | bytes 3145736 | tf_op jit(solution)/shard_map/ppermute | solution.py:72
  326.3 34.2 %collective-permute-start.25 = (bf16[128,2048]{1,0:T(8,128)(2,1)S(1)}, bf16[128,2048]{1,0:T(8,128)(2,1)S(1)}, u32[]{:S(2)}, u32[]{:S(2)}) collective-permute-start(bf16[128,2048]{1,0:T(8,128)(2,1)S(1)} %copy-done.69), channel_id=1, source_target_pairs={{0,8},{4,12},{8,0},{12,4},{16,24},{20,28},{24,16},{28,20},{1,9},{5... | collective-permute-start | bytes 1572872 | tf_op jit(solution)/shard_map/ppermute | solution.py:72
  327.2 34.3 %collective-permute-start.26 = (bf16[128,2048]{1,0:T(8,128)(2,1)S(1)}, bf16[128,2048]{1,0:T(8,128)(2,1)}, u32[]{:S(2)}, u32[]{:S(2)}) collective-permute-start(bf16[128,2048]{1,0:T(8,128)(2,1)S(1)} %copy-done.68), channel_id=1, source_target_pairs={{0,16},{4,20},{8,24},{12,28},{16,0},{20,4},{24,8},{28,12},{1,17},{... | collective-permute-start | bytes 1572872 | tf_op jit(solution)/shard_map/ppermute | solution.py:72
  388.8 38.2 %collective-permute-start.35 = (bf16[256,2048]{1,0:T(8,128)(2,1)}, bf16[256,2048]{1,0:T(8,128)(2,1)}, u32[]{:S(2)}, u32[]{:S(2)}) collective-permute-start(bf16[256,2048]{1,0:T(8,128)(2,1)} %get-tuple-element.161), channel_id=1, source_target_pairs={{0,8},{4,12},{8,0},{12,4},{16,24},{20,28},{24,16},{28,20},{1,9},{5... | collective-permute-start | bytes 3145736 | tf_op jit(solution)/shard_map/ppermute | solution.py:72
  389.8 37.2 %collective-permute-start.36 = (bf16[256,2048]{1,0:T(8,128)(2,1)}, bf16[256,2048]{1,0:T(8,128)(2,1)}, u32[]{:S(2)}, u32[]{:S(2)}) collective-permute-start(bf16[256,2048]{1,0:T(8,128)(2,1)} %get-tuple-element.162), channel_id=1, source_target_pairs={{0,16},{4,20},{8,24},{12,28},{16,0},{20,4},{24,8},{28,12},{1,17},{... | collective-permute-start | bytes 3145736 | tf_op jit(solution)/shard_map/ppermute | solution.py:72
  428.7 33.2 %collective-permute-start.39 = (bf16[128,2048]{1,0:T(8,128)(2,1)S(1)}, bf16[128,2048]{1,0:T(8,128)(2,1)}, u32[]{:S(2)}, u32[]{:S(2)}) collective-permute-start(bf16[128,2048]{1,0:T(8,128)(2,1)S(1)} %add_convert_fusion.27.refs_4_), channel_id=1, source_target_pairs={{0,8},{4,12},{8,0},{12,4},{16,24},{20,28},{24,16},{28,20},{1,9},{5... | collective-permute-start | bytes 1572872 | tf_op jit(solution)/shard_map/ppermute | solution.py:72
  430.8 31.3 %collective-permute-start.38 = (bf16[128,2048]{1,0:T(8,128)(2,1)S(1)}, bf16[128,2048]{1,0:T(8,128)(2,1)}, u32[]{:S(2)}, u32[]{:S(2)}) collective-permute-start(bf16[128,2048]{1,0:T(8,128)(2,1)S(1)} %add_convert_fusion.28.refs_3_), channel_id=1, source_target_pairs={{0,16},{4,20},{8,24},{12,28},{16,0},{20,4},{24,8},{28,12},{1,17},{... | collective-permute-start | bytes 1572872 | tf_op jit(solution)/shard_map/ppermute | solution.py:72
  445.4 29.0 %collective-permute-start.37 = (bf16[2,192,2048]{2,1,0:T(8,128)(2,1)}, bf16[2,192,2048]{2,1,0:T(8,128)(2,1)}, u32[]{:S(2)}, u32[]{:S(2)}) collective-permute-start(bf16[2,192,2048]{2,1,0:T(8,128)(2,1)} %get-tuple-element.168), channel_id=1, source_target_pairs={{0,4},{4,0},{8,12},{12,8},{16,20},{20,16},{24,28},{28,24},{1,5},{5... | collective-permute-start | bytes 4718600 | tf_op jit(solution)/shard_map/ppermute | solution.py:72
  445.5 33.3 %collective-permute-start.40 = (bf16[256,2048]{1,0:T(8,128)(2,1)}, bf16[256,2048]{1,0:T(8,128)(2,1)S(1)}, u32[]{:S(2)}, u32[]{:S(2)}) collective-permute-start(bf16[256,2048]{1,0:T(8,128)(2,1)} %get-tuple-element.166.refs_2_), channel_id=1, source_target_pairs={{0,8},{4,12},{8,0},{12,4},{16,24},{20,28},{24,16},{28,20},{1,9},{5... | collective-permute-start | bytes 3145736 | tf_op jit(solution)/shard_map/ppermute | solution.py:72
  446.5 32.4 %collective-permute-start.41 = (bf16[256,2048]{1,0:T(8,128)(2,1)}, bf16[256,2048]{1,0:T(8,128)(2,1)S(1)}, u32[]{:S(2)}, u32[]{:S(2)}) collective-permute-start(bf16[256,2048]{1,0:T(8,128)(2,1)} %get-tuple-element.182), channel_id=1, source_target_pairs={{0,16},{4,20},{8,24},{12,28},{16,0},{20,4},{24,8},{28,12},{1,17},{... | collective-permute-start | bytes 3145736 | tf_op jit(solution)/shard_map/ppermute | solution.py:72
  447.8 24.6 %all-to-all-start.6 = ((f32[32,2,128]{2,1,0:T(2,128)}), f32[32,2,128]{2,1,0:T(2,128)S(1)}, u32[]{:S(2)}, u32[]{:S(2)}) async-start(f32[32,2,128]{2,1,0:T(2,128)} %fusion.37), calls=%async_computation.6 | async-start | bytes 65536 | tf_op jit(solution)/shard_map/all_to_all | solution.py:860
  461.9 27.8 %collective-permute-start.47 = (bf16[2,192,2048]{2,1,0:T(8,128)(2,1)}, bf16[2,192,2048]{2,1,0:T(8,128)(2,1)}, u32[]{:S(2)}, u32[]{:S(2)}) collective-permute-start(bf16[2,192,2048]{2,1,0:T(8,128)(2,1)} %get-tuple-element.191), channel_id=1, source_target_pairs={{0,4},{4,0},{8,12},{12,8},{16,20},{20,16},{24,28},{28,24},{1,5},{5... | collective-permute-start | bytes 4718600 | tf_op jit(solution)/shard_map/ppermute | solution.py:72
  485.2 40.8 %collective-permute-start.44 = (bf16[128,2048]{1,0:T(8,128)(2,1)}, bf16[128,2048]{1,0:T(8,128)(2,1)S(1)}, u32[]{:S(2)}, u32[]{:S(2)}) collective-permute-start(bf16[128,2048]{1,0:T(8,128)(2,1)} %get-tuple-element.283), channel_id=1, source_target_pairs={{0,1},{1,0},{2,3},{3,2},{4,5},{5,4},{6,7},{7,6},{8,9},{9,8},{10,11... | collective-permute-start | bytes 1572872 | tf_op jit(solution)/shard_map/ppermute | solution.py:75
  488.5 76.3 %collective-permute-start.42 = (bf16[256,2048]{1,0:T(8,128)(2,1)}, bf16[256,2048]{1,0:T(8,128)(2,1)}, u32[]{:S(2)}, u32[]{:S(2)}) collective-permute-start(bf16[256,2048]{1,0:T(8,128)(2,1)} %get-tuple-element.185), channel_id=1, source_target_pairs={{0,8},{4,12},{8,0},{12,4},{16,24},{20,28},{24,16},{28,20},{1,9},{5... | collective-permute-start | bytes 3145736 | tf_op jit(solution)/shard_map/ppermute | solution.py:72
  489.7 75.1 %collective-permute-start.43 = (bf16[256,2048]{1,0:T(8,128)(2,1)}, bf16[256,2048]{1,0:T(8,128)(2,1)}, u32[]{:S(2)}, u32[]{:S(2)}) collective-permute-start(bf16[256,2048]{1,0:T(8,128)(2,1)} %get-tuple-element.186), channel_id=1, source_target_pairs={{0,16},{4,20},{8,24},{12,28},{16,0},{20,4},{24,8},{28,12},{1,17},{... | collective-permute-start | bytes 3145736 | tf_op jit(solution)/shard_map/ppermute | solution.py:72
  502.4 37.5 %collective-permute-start.48 = (bf16[128,2048]{1,0:T(8,128)(2,1)}, bf16[128,2048]{1,0:T(8,128)(2,1)S(1)}, u32[]{:S(2)}, u32[]{:S(2)}) collective-permute-start(bf16[128,2048]{1,0:T(8,128)(2,1)} %get-tuple-element.280), channel_id=1, source_target_pairs={{0,2},{1,3},{2,0},{3,1},{4,6},{5,7},{6,4},{7,5},{8,10},{9,11},{10,... | collective-permute-start | bytes 1572872 | tf_op jit(solution)/shard_map/ppermute | solution.py:75
  506.6 35.0 %collective-permute-start.49 = (bf16[128,2048]{1,0:T(8,128)(2,1)}, bf16[128,2048]{1,0:T(8,128)(2,1)}, u32[]{:S(2)}, u32[]{:S(2)}) collective-permute-start(bf16[128,2048]{1,0:T(8,128)(2,1)} %get-tuple-element.281), channel_id=1, source_target_pairs={{0,3},{1,2},{2,1},{3,0},{4,7},{5,6},{6,5},{7,4},{8,11},{9,10},{10,... | collective-permute-start | bytes 1572872 | tf_op jit(solution)/shard_map/ppermute | solution.py:75
  526.0 43.4 %collective-permute-start.52 = (bf16[256,2048]{1,0:T(8,128)(2,1)}, bf16[256,2048]{1,0:T(8,128)(2,1)S(1)}, u32[]{:S(2)}, u32[]{:S(2)}) collective-permute-start(bf16[256,2048]{1,0:T(8,128)(2,1)} %get-tuple-element.216), channel_id=1, source_target_pairs={{0,8},{4,12},{8,0},{12,4},{16,24},{20,28},{24,16},{28,20},{1,9},{5... | collective-permute-start | bytes 3145736 | tf_op jit(solution)/shard_map/ppermute | solution.py:72
  539.8 29.6 %collective-permute-start.53 = (bf16[256,2048]{1,0:T(8,128)(2,1)}, bf16[256,2048]{1,0:T(8,128)(2,1)S(1)}, u32[]{:S(2)}, u32[]{:S(2)}) collective-permute-start(bf16[256,2048]{1,0:T(8,128)(2,1)} %get-tuple-element.217), channel_id=1, source_target_pairs={{0,16},{4,20},{8,24},{12,28},{16,0},{20,4},{24,8},{28,12},{1,17},{... | collective-permute-start | bytes 3145736 | tf_op jit(solution)/shard_map/ppermute | solution.py:72
  551.7 38.2 %all-to-all-start.7 = ((bf16[4,128,512]{2,1,0:T(8,128)(2,1)}), bf16[4,128,512]{2,1,0:T(8,128)(2,1)S(1)}, u32[]{:S(2)}, u32[]{:S(2)}) async-start(bf16[4,128,512]{2,1,0:T(8,128)(2,1)} %get-tuple-element.208), calls=%async_computation.7 | async-start | bytes 1048576 | tf_op jit(solution)/shard_map/all_to_all | solution.py:78
  609.7 53.4 %collective-permute-start.56 = (bf16[1024,2176]{1,0:T(8,128)(2,1)}, bf16[1024,2176]{1,0:T(8,128)(2,1)}, u32[]{:S(2)}, u32[]{:S(2)}) collective-permute-start(bf16[1024,2176]{1,0:T(8,128)(2,1)} %get-tuple-element.236), channel_id=1, source_target_pairs={{0,4},{4,0},{8,12},{12,8},{16,20},{20,16},{24,28},{28,24},{1,5},{5... | collective-permute-start | bytes 13369352 | tf_op jit(solution)/shard_map/ppermute | solution.py:72
  614.5 24.1 %collective-permute-start.55 = (bf16[128,2048]{1,0:T(8,128)(2,1)S(1)}, bf16[128,2048]{1,0:T(8,128)(2,1)S(1)}, u32[]{:S(2)}, u32[]{:S(2)}) collective-permute-start(bf16[128,2048]{1,0:T(8,128)(2,1)S(1)} %copy-done.56), channel_id=1, source_target_pairs={{0,8},{4,12},{8,0},{12,4},{16,24},{20,28},{24,16},{28,20},{1,9},{5... | collective-permute-start | bytes 1572872 | tf_op jit(solution)/shard_map/ppermute | solution.py:72
  616.3 22.3 %collective-permute-start.54 = (bf16[128,2048]{1,0:T(8,128)(2,1)}, bf16[128,2048]{1,0:T(8,128)(2,1)}, u32[]{:S(2)}, u32[]{:S(2)}) collective-permute-start(bf16[128,2048]{1,0:T(8,128)(2,1)} %add_convert_fusion.15), channel_id=1, source_target_pairs={{0,16},{4,20},{8,24},{12,28},{16,0},{20,4},{24,8},{28,12},{1,17},{... | collective-permute-start | bytes 1572872 | tf_op jit(solution)/shard_map/ppermute | solution.py:72
  643.9 53.5 %all-to-all-start.8 = ((bf16[4,128,2048]{2,1,0:T(8,128)(2,1)}), bf16[4,128,2048]{2,1,0:T(8,128)(2,1)S(1)}, u32[]{:S(2)}, u32[]{:S(2)}) async-start(bf16[4,128,2048]{2,1,0:T(8,128)(2,1)} %maximum_select_fusion.1), calls=%async_computation.8 | async-start | bytes 4194304 | tf_op jit(solution)/shard_map/all_to_all | solution.py:78
  668.2 25.8 %collective-permute-start.57 = (bf16[256,2176]{1,0:T(8,128)(2,1)}, bf16[256,2176]{1,0:T(8,128)(2,1)S(1)}, u32[]{:S(2)}, u32[]{:S(2)}) collective-permute-start(bf16[256,2176]{1,0:T(8,128)(2,1)} %get-tuple-element.256), channel_id=1, source_target_pairs={{0,8},{4,12},{8,0},{12,4},{16,24},{20,28},{24,16},{28,20},{1,9},{5... | collective-permute-start | bytes 3342344 | tf_op jit(solution)/shard_map/ppermute | solution.py:72
  669.4 25.6 %collective-permute-start.58 = (bf16[256,2176]{1,0:T(8,128)(2,1)}, bf16[256,2176]{1,0:T(8,128)(2,1)}, u32[]{:S(2)}, u32[]{:S(2)}) collective-permute-start(bf16[256,2176]{1,0:T(8,128)(2,1)} %get-tuple-element.255), channel_id=1, source_target_pairs={{0,16},{4,20},{8,24},{12,28},{16,0},{20,4},{24,8},{28,12},{1,17},{... | collective-permute-start | bytes 3342344 | tf_op jit(solution)/shard_map/ppermute | solution.py:72
  707.2 53.9 %all-to-all-start.10 = ((bf16[4,128,2048]{2,1,0:T(8,128)(2,1)}), bf16[4,128,2048]{2,1,0:T(8,128)(2,1)}, u32[]{:S(2)}, u32[]{:S(2)}) async-start(bf16[4,128,2048]{2,1,0:T(8,128)(2,1)} %shard_map.304.refs_1_), calls=%async_computation.10 | async-start | bytes 4194304 | tf_op jit(solution)/shard_map/all_to_all | solution.py:78
  720.6 26.1 %collective-permute-start.60 = (bf16[256,1664]{1,0:T(8,128)(2,1)}, bf16[256,1664]{1,0:T(8,128)(2,1)S(1)}, u32[]{:S(2)}, u32[]{:S(2)}) collective-permute-start(bf16[256,1664]{1,0:T(8,128)(2,1)} %get-tuple-element.261), channel_id=1, source_target_pairs={{0,8},{4,12},{8,0},{12,4},{16,24},{20,28},{24,16},{28,20},{1,9},{5... | collective-permute-start | bytes 2555912 | tf_op jit(solution)/shard_map/ppermute | solution.py:72
  721.4 27.2 %collective-permute-start.61 = (bf16[256,1664]{1,0:T(8,128)(2,1)}, bf16[256,1664]{1,0:T(8,128)(2,1)}, u32[]{:S(2)}, u32[]{:S(2)}) collective-permute-start(bf16[256,1664]{1,0:T(8,128)(2,1)} %get-tuple-element.260), channel_id=1, source_target_pairs={{0,16},{4,20},{8,24},{12,28},{16,0},{20,4},{24,8},{28,12},{1,17},{... | collective-permute-start | bytes 2555912 | tf_op jit(solution)/shard_map/ppermute | solution.py:72
  761.1 30.7 %all-to-all-start.12 = ((bf16[4,64,2176]{2,1,0:T(8,128)(2,1)}), bf16[4,64,2176]{2,1,0:T(8,128)(2,1)S(1)}, u32[]{:S(2)}, u32[]{:S(2)}) async-start(bf16[4,64,2176]{2,1,0:T(8,128)(2,1)} %bitcast.127), calls=%async_computation.12 | async-start | bytes 2228224 | tf_op jit(solution)/shard_map/all_to_all | solution.py:78
  791.8 24.5 %all-to-all-start.11 = ((bf16[4,64,1664]{2,1,0:T(8,128)(2,1)}), bf16[4,64,1664]{2,1,0:T(8,128)(2,1)S(1)}, u32[]{:S(2)}, u32[]{:S(2)}) async-start(bf16[4,64,1664]{2,1,0:T(8,128)(2,1)} %bitcast.125), calls=%async_computation.11 | async-start | bytes 1703936 | tf_op jit(solution)/shard_map/all_to_all | solution.py:78
  (132 other events, 984.5 us)
Sparse Core Ops, SparseCore 0:
  149.2 59.4 all-gather.2

commit v5 on v4

--- a/solution.py
+++ b/solution.py
@@ -968,9 +968,9 @@
         grad_w_in = grad_in_pieces(j, grad_w_in, dqkv, *grad_o_begun[2:3])
         last = grad_w_in
     grad_o_more = links.reduce_next(grad_o_begun, last)
-    grad_qkv_terms = dense_terms(normed, dqkv, gain_terms, grad_o_more[-1], out_terms)
-    dnormed_terms = after(dnormed_terms.reshape(nc, tok, dim), out_terms)
-    grad_qkv_begun = links.dense_start(grad_qkv_terms, fsdp_rows, dnormed_terms)
+    dnormed_terms = after(dnormed_terms.reshape(nc, tok, dim), out_terms, grad_o_more[-1])
+    grad_qkv_terms = dense_terms(normed, dqkv, gain_terms, dnormed_terms)
+    grad_qkv_begun = links.dense_start(grad_qkv_terms, fsdp_rows, grad_qkv_terms[0])
     dnormed_terms = links.exchange(dnormed_terms)
     grad_o_total = links.reduce_end(grad_o_more, fsdp_rows, grad_qkv_begun[-1])
     grad_qkv_more = links.reduce_next(grad_qkv_begun, grad_o_total)

time: 845 us -> 849 us (level)
  waiting for transfers between devices: 272 us -> 262 us
    all_to_all x12, waiting for transfers between devices: 104 us -> 93.2 us  [exchange(): return lax.all_to_all(value, 'ctx', split_axis=0, concat_axis=0, tiled=True)]
    unnamed x218 -> x212, local copies, waits for them, and re-layouts: 29.9 us -> 33.5 us
  transfers between devices with their start and end apart: 80 -> 80, of which waited for: 37 -> 35; matrix products, arithmetic and copies ran while one was open for 17% -> 17% of each run, Pallas kernels for 25% -> 25%
where the time goes in v5:
time: 849 us; the launch traced here: 838 us
  waiting for transfers between devices  262 us (31%)
  Pallas kernels  238 us (28%)
  starting transfers between devices  130 us (15%)
  local copies, waits for them, and re-layouts  106 us (12%)
  other arithmetic  85.5 us (10%)
  between operations  16.3 us (2%)
    pallas_call x22, Pallas kernels, call(): return lambda *operands: made(*operands, *gate)  229 us
    ppermute x61, waiting for transfers between devices, swap(): return lax.ppermute(value, 'fsdp', [(i, i ^ mask) for i in range(self.nf)])  138 us
    all_to_all x12, waiting for transfers between devices, exchange(): return lax.all_to_all(value, 'ctx', split_axis=0, concat_axis=0, tiled=True)  93.2 us
    all_to_all x12, starting transfers between devices, exchange(): return lax.all_to_all(value, 'ctx', split_axis=0, concat_axis=0, tiled=True)  64.4 us
    ppermute x61, starting transfers between devices, swap(): return lax.ppermute(value, 'fsdp', [(i, i ^ mask) for i in range(self.nf)])  49.7 us
    convert_element_type x20, other arithmetic, add_low(): return sum((t.astype(F32) for t in terms)).astype(BF)  44.7 us
    unnamed x212, local copies, waits for them, and re-layouts  33.5 us
    ppermute x5, waiting for transfers between devices, cswap(): return lax.ppermute(value, 'ctx', [(i, i ^ mask) for i in range(self.nc)])  26.2 us
  transfers between devices with their start and end apart: 80, of which 35 were waited for; matrix products, arithmetic and copies ran while one was open for 17% of the time, Pallas kernels for 25%

profile of v5, /device:TPU:0, one launch (start us, length us, event | category | flops | bytes accessed | tf_op | source)
XLA Modules:
  0.0 837.7 jit_solution(11157188974047141499)
XLA Ops:
  14.8 6.4 all-to-all-start
  21.4 43.9 %all-to-all-done = bf16[4,64,3712]{2,1,0:T(8,128)(2,1)S(1)} async-done(((bf16[4,64,3712]{2,1,0:T(8,128)(2,1)}), bf16[4,64,3712]{2,1,0:T(8,128)(2,1)S(1)}, u32[]{:S(2)}, u32[]{:S(2)}) %all-to-all-start) | async-done | bytes 1900576 | tf_op jit(solution)/shard_map/all_to_all | solution.py:78
  81.2 5.4 collective-permute-done.2.refs_1_
  94.9 7.5 collective-permute-done.5
  115.7 16.9 %collective-permute-done.9.refs_6_.refs_14_ = bf16[256,2048]{1,0:T(8,128)(2,1)} collective-permute-done((bf16[256,2048]{1,0:T(8,128)(2,1)}, bf16[256,2048]{1,0:T(8,128)(2,1)}, u32[]{:S(2)}, u32[]{:S(2)}) %collective-permute-start.9) | collective-permute-done | bytes 1048608 | tf_op jit(solution)/shard_map/ppermute | solution.py:72
  137.8 9.6 %shard_map.258 = (bf16[512,2048]{1,0:T(8,128)(2,1)}, f32[2,512,512]{2,1,0:T(8,128)}, bf16[512,512]{1,0:T(8,128)(2,1)}, f32[2,8,512]{2,1,0:T(8,128)}) custom-call(s32[8]{0:T(128)} %iota_xor_fusion.refs_0_, f32[1,2048]{1,0:T(1,128)} %copy.312.refs_1_, bf16[512,2048]{1,0:T(8,128)(2,1)} %bitcast.271, bf16[256,1664]{1,0:T(8,128)(2,1)} %pad_maximum_fusion.9.refs_3_.refs_7_, ...), custom_call_target="tpu_custom_call" | custom-call | flops 160000000 | bytes 650000 | tf_op jit(solution)/shard_map/pallas_call | solution.py:241
  164.4 7.0 shard_map.259
  171.4 5.1 all-to-all-start.3
  191.2 6.3 shard_map.261
  199.1 12.9 %collective-permute-done.16.refs_1_ = bf16[128,2048]{1,0:T(8,128)(2,1)S(1)} collective-permute-done((bf16[128,2048]{1,0:T(8,128)(2,1)}, bf16[128,2048]{1,0:T(8,128)(2,1)S(1)}, u32[]{:S(2)}, u32[]{:S(2)}) %collective-permute-start.16) | collective-permute-done | bytes 524320 | tf_op jit(solution)/shard_map/ppermute | solution.py:75
  214.8 5.0 all-to-all-start.4
  223.8 9.0 %shard_map.264.refs_2_.refs_6_ = bf16[2,384,2048]{2,1,0:T(8,128)(2,1)} custom-call(s32[8]{0:T(128)} %broadcast_xor_fusion.places, bf16[8,96,256]{2,1,0:T(8,128)(2,1)} %broadcast_multiply_fusion.1.refs_16_.slots, bf16[8,256,2048]{2,1,0:T(8,128)(2,1)} %bitcast.284), custom_call_target="tpu_custom_call" | custom-call | flops 40000000 | bytes 600000 | tf_op jit(solution)/shard_map/pallas_call | solution.py:708
  232.8 13.5 %collective-permute-done.18.refs_1_ = bf16[256,2048]{1,0:T(8,128)(2,1)S(1)} collective-permute-done((bf16[256,2048]{1,0:T(8,128)(2,1)}, bf16[256,2048]{1,0:T(8,128)(2,1)S(1)}, u32[]{:S(2)}, u32[]{:S(2)}) %collective-permute-start.18) | collective-permute-done | bytes 1048608 | tf_op jit(solution)/shard_map/ppermute | solution.py:72
  253.6 14.3 %all-to-all-done.4.refs_0_ = bf16[4,128,2048]{2,1,0:T(8,128)(2,1)S(1)} async-done(((bf16[4,128,2048]{2,1,0:T(8,128)(2,1)}), bf16[4,128,2048]{2,1,0:T(8,128)(2,1)S(1)}, u32[]{:S(2)}, u32[]{:S(2)}) %all-to-all-start.4) | async-done | bytes 2097184 | tf_op jit(solution)/shard_map/all_to_all | solution.py:78
  271.1 4.7 all-to-all-start.5
  277.0 4.3 shard_map.268
  286.1 32.1 %shard_map.269 = (bf16[2,192,2048]{2,1,0:T(8,128)(2,1)}, bf16[2,192,2048]{2,1,0:T(8,128)(2,1)}, bf16[4,384,1024]{2,1,0:T(8,128)(2,1)}, bf16[2,384,1024]{2,1,0:T(8,128)(2,1)}, f32[2,384,128]{2,1,0:T(8,128)}) custom-call(s32[1]{0:T(128)} %bitcast.69.refs_0_, bf16[2048,128]{1,0:T(8,128)(2,1)} %get-tuple-element.252.refs_1_.refs_6_, ...), custom_call_target="tpu_custom_call" | custom-call | flops 1700000000 | bytes 1500000 | tf_op jit(solution)/shard_map/pallas_call | solution.py:241
  333.5 27.5 %collective-permute-done.25.refs_4_ = bf16[128,2048]{1,0:T(8,128)(2,1)S(1)} collective-permute-done((bf16[128,2048]{1,0:T(8,128)(2,1)S(1)}, bf16[128,2048]{1,0:T(8,128)(2,1)S(1)}, u32[]{:S(2)}, u32[]{:S(2)}) %collective-permute-start.25) | collective-permute-done | bytes 524320 | tf_op jit(solution)/shard_map/ppermute | solution.py:72
  372.5 8.8 %collective-permute-done.31.refs_4_ = bf16[128,2048]{1,0:T(8,128)(2,1)S(1)} collective-permute-done((bf16[128,2048]{1,0:T(8,128)(2,1)S(1)}, bf16[128,2048]{1,0:T(8,128)(2,1)S(1)}, u32[]{:S(2)}, u32[]{:S(2)}) %collective-permute-start.31) | collective-permute-done | bytes 524320 | tf_op jit(solution)/shard_map/ppermute | solution.py:72
  383.4 4.5 shard_map.276
  393.7 32.1 %shard_map.277 = (bf16[2,192,2048]{2,1,0:T(8,128)(2,1)}, bf16[2,192,2048]{2,1,0:T(8,128)(2,1)}, bf16[4,384,1024]{2,1,0:T(8,128)(2,1)}, bf16[2,384,1024]{2,1,0:T(8,128)(2,1)}, f32[2,384,128]{2,1,0:T(8,128)}) custom-call(s32[1]{0:T(128)} %bitcast.69.refs_0_, bf16[2048,128]{1,0:T(8,128)(2,1)} %get-tuple-element.252.refs_1_.refs_6_, ...), custom_call_target="tpu_custom_call" | custom-call | flops 1700000000 | bytes 1500000 | tf_op jit(solution)/shard_map/pallas_call | solution.py:241
  442.1 7.1 shard_map.281
  452.8 6.0 all-to-all-start.6
  458.8 7.2 shard_map.282
  471.7 4.7 all-to-all-done.6.refs_0_
  478.5 4.3 shard_map.285
  494.9 4.3 shard_map.288
  514.8 15.6 %shard_map.290.refs_4_.refs_5_ = f32[2,1024,2048]{2,1,0:T(8,128)} custom-call(bf16[2,384,1024]{2,1,0:T(8,128)(2,1)} %get-tuple-element.142.refs_0_, bf16[2,384,1024]{2,1,0:T(8,128)(2,1)} %get-tuple-element.170.refs_0_.refs_1_, bf16[2,384,2048]{2,1,0:T(8,128)(2,1)} %shard_map.264.refs_2_.refs_6_, ...), custom_call_target="tpu_custom_call" | custom-call | flops 325000000 | bytes 1300000 | tf_op jit(solution)/shard_map/pallas_call | solution.py:241
  531.4 13.4 %collective-permute-done.48.refs_2_ = bf16[128,2048]{1,0:T(8,128)(2,1)S(1)} collective-permute-done((bf16[128,2048]{1,0:T(8,128)(2,1)}, bf16[128,2048]{1,0:T(8,128)(2,1)S(1)}, u32[]{:S(2)}, u32[]{:S(2)}) %collective-permute-start.48) | collective-permute-done | bytes 524320 | tf_op jit(solution)/shard_map/ppermute | solution.py:75
  545.6 10.1 %shard_map.292 = (f32[128,2048]{1,0:T(8,128)}, f32[2048,128]{1,0:T(8,128)}, f32[8,2048]{1,0:T(8,128)}, bf16[128,2048]{1,0:T(8,128)(2,1)}, bf16[4,128,512]{2,1,0:T(8,128)(2,1)}) custom-call(s32[8]{0:T(128)} %iota_xor_fusion.refs_0_, f32[128,2048]{1,0:T(8,128)} %get-tuple-element.136.refs_1_, f32[128,128]{1,0:T(8,128)} %get-tuple-element.187.refs_2_, ...), custom_call_target="tpu_custom_call" | custom-call | flops 65000000 | bytes 750000 | tf_op jit(solution)/shard_map/pallas_call | solution.py:241
  556.5 13.3 %all-to-all-start.7 = ((bf16[4,128,512]{2,1,0:T(8,128)(2,1)}), bf16[4,128,512]{2,1,0:T(8,128)(2,1)S(1)}, u32[]{:S(2)}, u32[]{:S(2)}) async-start(bf16[4,128,512]{2,1,0:T(8,128)(2,1)} %get-tuple-element.208), calls=%async_computation.7 | async-start | bytes 1048576 | tf_op jit(solution)/shard_map/all_to_all | solution.py:78
  578.3 16.6 %shard_map.296.refs_1_.refs_6_ = f32[4,2048,1024]{2,1,0:T(8,128)} custom-call(bf16[2,192,2048]{2,1,0:T(8,128)(2,1)} %get-tuple-element.140.refs_4_.refs_7_.refs_0_, bf16[2,192,2048]{2,1,0:T(8,128)(2,1)} %copy-done.10, bf16[2,192,2048]{2,1,0:T(8,128)(2,1)} %get-tuple-element.148.refs_2_.refs_4_, bf16[2,192,2048]{2,1,0:T(8,128)(2,1)} %copy-done.11, ...), custom_call_target="tpu_custom_call" | custom-call | flops 325000000 | bytes 1250000 | tf_op jit(solution)/shard_map/pallas_call | solution.py:241
  595.7 11.6 %shard_map.298 = (f32[2,512,512]{2,1,0:T(8,128)}, bf16[512,512]{1,0:T(8,128)(2,1)}, f32[2,8,512]{2,1,0:T(8,128)}, f32[2,8,512]{2,1,0:T(8,128)}) custom-call(f32[2,512,512]{2,1,0:T(8,128)} %get-tuple-element.132.refs_0_.refs_2_, bf16[2,512,512]{2,1,0:T(8,128)(2,1)} %get-tuple-element.207.refs_1_, bf16[512,512]{1,0:T(8,128)(2,1)} %get-tuple-element.133.refs_1_.refs_2_, ...), custom_call_target="tpu_custom_call" | custom-call | flops 70000000 | bytes 500000 | tf_op jit(solution)/shard_map/pallas_call | solution.py:241
  607.3 7.3 shard_map.299
  622.2 5.1 all-to-all-start.9
  638.1 4.4 collective-permute-done.54.refs_0_
  648.0 5.3 all-to-all-start.8
  655.3 11.0 %shard_map.303 = (bf16[512,1536]{1,0:T(8,128)(2,1)}, bf16[512,2048]{1,0:T(8,128)(2,1)}, f32[8,2048]{1,0:T(8,128)}) custom-call(s32[8]{0:T(128)} %iota_xor_fusion.refs_0_, f32[2,512,512]{2,1,0:T(8,128)} %get-tuple-element.229.refs_1_, f32[2,512,512]{2,1,0:T(8,128)} %get-tuple-element.132.refs_0_.refs_2_, f32[2,512,128]{2,1,0:T(8,128)} %broadcast_in_dim.100.refs_2_.refs_3_, ...), custom_call_target="tpu_custom_call" | custom-call | flops 165000000 | bytes 750000 | tf_op jit(solution)/shard_map/pallas_call | solution.py:241
  667.2 5.1 add_convert_fusion
  679.7 16.6 %shard_map.305.refs_2_ = f32[4,2048,1024]{2,1,0:T(8,128)} custom-call(bf16[2,192,2048]{2,1,0:T(8,128)(2,1)} %get-tuple-element.140.refs_4_.refs_7_.refs_0_, bf16[2,192,2048]{2,1,0:T(8,128)(2,1)} %copy-done.10, bf16[2,192,2048]{2,1,0:T(8,128)(2,1)} %get-tuple-element.148.refs_2_.refs_4_, ...), custom_call_target="tpu_custom_call", output_to_operand_aliasing={{}: (6, {})} | custom-call | flops 325000000 | bytes 1250000 | tf_op jit(solution)/shard_map/pallas_call | solution.py:241
  703.0 8.4 shard_map.308
  711.4 4.8 all-to-all-start.10
  729.6 8.5 %collective-permute-done.62.refs_0_ = bf16[128,2176]{1,0:T(8,128)(2,1)} collective-permute-done((bf16[128,2176]{1,0:T(8,128)(2,1)}, bf16[128,2176]{1,0:T(8,128)(2,1)}, u32[]{:S(2)}, u32[]{:S(2)}) %collective-permute-start.62) | collective-permute-done | bytes 557088 | tf_op jit(solution)/shard_map/ppermute | solution.py:72
  741.3 14.0 %collective-permute-done.61.refs_1_ = bf16[256,1664]{1,0:T(8,128)(2,1)} collective-permute-done((bf16[256,1664]{1,0:T(8,128)(2,1)}, bf16[256,1664]{1,0:T(8,128)(2,1)}, u32[]{:S(2)}, u32[]{:S(2)}) %collective-permute-start.61) | collective-permute-done | bytes 852000 | tf_op jit(solution)/shard_map/ppermute | solution.py:72
  755.3 9.8 %all-to-all-done.10.refs_0_ = bf16[4,128,2048]{2,1,0:T(8,128)(2,1)S(1)} async-done(((bf16[4,128,2048]{2,1,0:T(8,128)(2,1)}), bf16[4,128,2048]{2,1,0:T(8,128)(2,1)S(1)}, u32[]{:S(2)}, u32[]{:S(2)}) %all-to-all-start.10) | async-done | bytes 2097184 | tf_op jit(solution)/shard_map/all_to_all | solution.py:78
  774.1 8.1 collective-permute-done.65.refs_1_
  788.5 7.3 all-to-all-done.12
  804.1 16.1 %all-to-all-done.11 = bf16[4,64,1664]{2,1,0:T(8,128)(2,1)S(1)} async-done(((bf16[4,64,1664]{2,1,0:T(8,128)(2,1)}), bf16[4,64,1664]{2,1,0:T(8,128)(2,1)S(1)}, u32[]{:S(2)}, u32[]{:S(2)}) %all-to-all-start.11) | async-done | bytes 852000 | tf_op jit(solution)/shard_map/all_to_all | solution.py:78
  (593 shorter events, 299.0 us)
Async XLA Ops:
  14.8 50.4 %all-to-all-start = ((bf16[4,64,3712]{2,1,0:T(8,128)(2,1)}), bf16[4,64,3712]{2,1,0:T(8,128)(2,1)S(1)}, u32[]{:S(2)}, u32[]{:S(2)}) async-start(bf16[4,64,3712]{2,1,0:T(8,128)(2,1)} %pad_maximum_fusion), calls=%async_computation | async-start | bytes 3801088 | tf_op jit(solution)/shard_map/all_to_all | solution.py:78
  69.5 23.8 %collective-permute-start = (bf16[256,1664]{1,0:T(8,128)(2,1)}, bf16[256,1664]{1,0:T(8,128)(2,1)}, u32[]{:S(2)}, u32[]{:S(2)}) collective-permute-start(bf16[256,1664]{1,0:T(8,128)(2,1)} %pad_maximum_fusion.9.refs_3_.refs_7_), channel_id=1, source_target_pairs={{0,4},{4,0},{8,12},{12,8},{16,20},{20,16},{24,28},{28,24},{1,5},{5... | collective-permute-start | bytes 2555912 | tf_op jit(solution)/shard_map/ppermute | solution.py:72
  76.7 59.7 %all-to-all-start.1 = ((bf16[4,128,2048]{2,1,0:T(8,128)(2,1)}), bf16[4,128,2048]{2,1,0:T(8,128)(2,1)S(1)}, u32[]{:S(2)}, u32[]{:S(2)}) async-start(bf16[4,128,2048]{2,1,0:T(8,128)(2,1)} %shard_map.255.refs_2_), calls=%async_computation.1 | async-start | bytes 4194304 | tf_op jit(solution)/shard_map/all_to_all | solution.py:78
  80.3 143.5 %all-gather.3.cloned.1.call-start = ((), (), s32[]{:S(2)}) async-start(), calls=%async_computation.13 | async-start | bytes 9437184 | tf_op jit(solution)/shard_map/all_gather | solution.py:586
  107.1 25.5 %collective-permute-start.9 = (bf16[256,2048]{1,0:T(8,128)(2,1)}, bf16[256,2048]{1,0:T(8,128)(2,1)}, u32[]{:S(2)}, u32[]{:S(2)}) collective-permute-start(bf16[256,2048]{1,0:T(8,128)(2,1)} %shard_map.257.refs_4_.refs_12_), channel_id=1, source_target_pairs={{0,8},{4,12},{8,0},{12,4},{16,24},{20,28},{24,16},{28,20},{1,9},{5... | collective-permute-start | bytes 3145736 | tf_op jit(solution)/shard_map/ppermute | solution.py:72
  107.6 26.9 %collective-permute-start.8 = (bf16[256,2048]{1,0:T(8,128)(2,1)}, bf16[256,2048]{1,0:T(8,128)(2,1)}, u32[]{:S(2)}, u32[]{:S(2)}) collective-permute-start(bf16[256,2048]{1,0:T(8,128)(2,1)} %shard_map.257.refs_4_.refs_12_), channel_id=1, source_target_pairs={{0,16},{4,20},{8,24},{12,28},{16,0},{20,4},{24,8},{28,12},{1,17},{... | collective-permute-start | bytes 3145736 | tf_op jit(solution)/shard_map/ppermute | solution.py:72
  108.7 38.6 %collective-permute-start.19 = (bf16[128,2048]{1,0:T(8,128)(2,1)}, bf16[128,2048]{1,0:T(8,128)(2,1)}, u32[]{:S(2)}, u32[]{:S(2)}) collective-permute-start(bf16[128,2048]{1,0:T(8,128)(2,1)} %shard_map.262), channel_id=1, source_target_pairs={{0,1},{1,0},{2,3},{3,2},{4,5},{5,4},{6,7},{7,6},{8,9},{9,8},{10,11... | collective-permute-start | bytes 1572872 | tf_op jit(solution)/shard_map/ppermute | solution.py:75
  157.5 33.3 %collective-permute-start.10 = (bf16[256,2048]{1,0:T(8,128)(2,1)S(1)}, bf16[256,2048]{1,0:T(8,128)(2,1)}, u32[]{:S(2)}, u32[]{:S(2)}) collective-permute-start(bf16[256,2048]{1,0:T(8,128)(2,1)S(1)} %copy-done.6), channel_id=1, source_target_pairs={{0,4},{4,0},{8,12},{12,8},{16,20},{20,16},{24,28},{28,24},{1,5},{5... | collective-permute-start | bytes 3145736 | tf_op jit(solution)/shard_map/ppermute | solution.py:72
  162.8 28.4 %collective-permute-start.11 = (bf16[256,2048]{1,0:T(8,128)(2,1)}, bf16[256,2048]{1,0:T(8,128)(2,1)}, u32[]{:S(2)}, u32[]{:S(2)}) collective-permute-start(bf16[256,2048]{1,0:T(8,128)(2,1)} %collective-permute-done.9.refs_6_.refs_14_), channel_id=1, source_target_pairs={{0,4},{4,0},{8,12},{12,8},{16,20},{20,16},{24,28},{28,24},{1,5},{5... | collective-permute-start | bytes 3145736 | tf_op jit(solution)/shard_map/ppermute | solution.py:72
  162.8 28.4 %collective-permute-start.12 = (bf16[256,2048]{1,0:T(8,128)(2,1)}, bf16[256,2048]{1,0:T(8,128)(2,1)}, u32[]{:S(2)}, u32[]{:S(2)}) collective-permute-start(bf16[256,2048]{1,0:T(8,128)(2,1)} %collective-permute-done.8.refs_8_.refs_16_), channel_id=1, source_target_pairs={{0,4},{4,0},{8,12},{12,8},{16,20},{20,16},{24,28},{28,24},{1,5},{5... | collective-permute-start | bytes 3145736 | tf_op jit(solution)/shard_map/ppermute | solution.py:72
  214.8 53.1 %all-to-all-start.4 = ((bf16[4,128,2048]{2,1,0:T(8,128)(2,1)}), bf16[4,128,2048]{2,1,0:T(8,128)(2,1)S(1)}, u32[]{:S(2)}, u32[]{:S(2)}) async-start(bf16[4,128,2048]{2,1,0:T(8,128)(2,1)} %shard_map.266), calls=%async_computation.4 | async-start | bytes 4194304 | tf_op jit(solution)/shard_map/all_to_all | solution.py:78
  221.5 24.8 %collective-permute-start.18 = (bf16[256,2048]{1,0:T(8,128)(2,1)}, bf16[256,2048]{1,0:T(8,128)(2,1)S(1)}, u32[]{:S(2)}, u32[]{:S(2)}) collective-permute-start(bf16[256,2048]{1,0:T(8,128)(2,1)} %constant_dynamic-update-slice_fusion.4.refs_1_), channel_id=1, source_target_pairs={{0,16},{4,20},{8,24},{12,28},{16,0},{20,4},{24,8},{28,12},{1,17},{... | collective-permute-start | bytes 3145736 | tf_op jit(solution)/shard_map/ppermute | solution.py:72
  222.3 24.6 %collective-permute-start.17 = (bf16[256,2048]{1,0:T(8,128)(2,1)}, bf16[256,2048]{1,0:T(8,128)(2,1)}, u32[]{:S(2)}, u32[]{:S(2)}) collective-permute-start(bf16[256,2048]{1,0:T(8,128)(2,1)} %constant_dynamic-update-slice_fusion.4.refs_1_), channel_id=1, source_target_pairs={{0,8},{4,12},{8,0},{12,4},{16,24},{20,28},{24,16},{28,20},{1,9},{5... | collective-permute-start | bytes 3145736 | tf_op jit(solution)/shard_map/ppermute | solution.py:72
  271.1 52.5 %all-to-all-start.5 = ((bf16[4,128,2048]{2,1,0:T(8,128)(2,1)}), bf16[4,128,2048]{2,1,0:T(8,128)(2,1)}, u32[]{:S(2)}, u32[]{:S(2)}) async-start(bf16[4,128,2048]{2,1,0:T(8,128)(2,1)} %shard_map.271), calls=%async_computation.5 | async-start | bytes 4194304 | tf_op jit(solution)/shard_map/all_to_all | solution.py:78
  281.4 37.0 %collective-permute-start.24 = (bf16[256,2048]{1,0:T(8,128)(2,1)S(1)}, bf16[256,2048]{1,0:T(8,128)(2,1)}, u32[]{:S(2)}, u32[]{:S(2)}) collective-permute-start(bf16[256,2048]{1,0:T(8,128)(2,1)S(1)} %copy-done.14), channel_id=1, source_target_pairs={{0,16},{4,20},{8,24},{12,28},{16,0},{20,4},{24,8},{28,12},{1,17},{... | collective-permute-start | bytes 3145736 | tf_op jit(solution)/shard_map/ppermute | solution.py:72
  282.2 36.1 %collective-permute-start.23 = (bf16[256,2048]{1,0:T(8,128)(2,1)S(1)}, bf16[256,2048]{1,0:T(8,128)(2,1)}, u32[]{:S(2)}, u32[]{:S(2)}) collective-permute-start(bf16[256,2048]{1,0:T(8,128)(2,1)S(1)} %copy-done.14), channel_id=1, source_target_pairs={{0,8},{4,12},{8,0},{12,4},{16,24},{20,28},{24,16},{28,20},{1,9},{5... | collective-permute-start | bytes 3145736 | tf_op jit(solution)/shard_map/ppermute | solution.py:72
  325.1 40.9 %collective-permute-start.30 = (bf16[256,2048]{1,0:T(8,128)(2,1)S(1)}, bf16[256,2048]{1,0:T(8,128)(2,1)S(1)}, u32[]{:S(2)}, u32[]{:S(2)}) collective-permute-start(bf16[256,2048]{1,0:T(8,128)(2,1)S(1)} %pad_maximum_fusion.4.refs_3_.refs_1_), channel_id=1, source_target_pairs={{0,16},{4,20},{8,24},{12,28},{16,0},{20,4},{24,8},{28,12},{1,17},{... | collective-permute-start | bytes 3145736 | tf_op jit(solution)/shard_map/ppermute | solution.py:72
  325.9 40.1 %collective-permute-start.29 = (bf16[256,2048]{1,0:T(8,128)(2,1)S(1)}, bf16[256,2048]{1,0:T(8,128)(2,1)}, u32[]{:S(2)}, u32[]{:S(2)}) collective-permute-start(bf16[256,2048]{1,0:T(8,128)(2,1)S(1)} %pad_maximum_fusion.4.refs_3_.refs_1_), channel_id=1, source_target_pairs={{0,8},{4,12},{8,0},{12,4},{16,24},{20,28},{24,16},{28,20},{1,9},{5... | collective-permute-start | bytes 3145736 | tf_op jit(solution)/shard_map/ppermute | solution.py:72
  327.0 34.0 %collective-permute-start.25 = (bf16[128,2048]{1,0:T(8,128)(2,1)S(1)}, bf16[128,2048]{1,0:T(8,128)(2,1)S(1)}, u32[]{:S(2)}, u32[]{:S(2)}) collective-permute-start(bf16[128,2048]{1,0:T(8,128)(2,1)S(1)} %copy-done.67), channel_id=1, source_target_pairs={{0,8},{4,12},{8,0},{12,4},{16,24},{20,28},{24,16},{28,20},{1,9},{5... | collective-permute-start | bytes 1572872 | tf_op jit(solution)/shard_map/ppermute | solution.py:72
  328.0 33.0 %collective-permute-start.26 = (bf16[128,2048]{1,0:T(8,128)(2,1)S(1)}, bf16[128,2048]{1,0:T(8,128)(2,1)}, u32[]{:S(2)}, u32[]{:S(2)}) collective-permute-start(bf16[128,2048]{1,0:T(8,128)(2,1)S(1)} %copy-done.64), channel_id=1, source_target_pairs={{0,16},{4,20},{8,24},{12,28},{16,0},{20,4},{24,8},{28,12},{1,17},{... | collective-permute-start | bytes 1572872 | tf_op jit(solution)/shard_map/ppermute | solution.py:72
  389.5 39.0 %collective-permute-start.35 = (bf16[256,2048]{1,0:T(8,128)(2,1)}, bf16[256,2048]{1,0:T(8,128)(2,1)}, u32[]{:S(2)}, u32[]{:S(2)}) collective-permute-start(bf16[256,2048]{1,0:T(8,128)(2,1)} %get-tuple-element.161), channel_id=1, source_target_pairs={{0,8},{4,12},{8,0},{12,4},{16,24},{20,28},{24,16},{28,20},{1,9},{5... | collective-permute-start | bytes 3145736 | tf_op jit(solution)/shard_map/ppermute | solution.py:72
  390.6 37.8 %collective-permute-start.36 = (bf16[256,2048]{1,0:T(8,128)(2,1)}, bf16[256,2048]{1,0:T(8,128)(2,1)}, u32[]{:S(2)}, u32[]{:S(2)}) collective-permute-start(bf16[256,2048]{1,0:T(8,128)(2,1)} %get-tuple-element.162), channel_id=1, source_target_pairs={{0,16},{4,20},{8,24},{12,28},{16,0},{20,4},{24,8},{28,12},{1,17},{... | collective-permute-start | bytes 3145736 | tf_op jit(solution)/shard_map/ppermute | solution.py:72
  430.4 35.6 %collective-permute-start.39 = (bf16[128,2048]{1,0:T(8,128)(2,1)S(1)}, bf16[128,2048]{1,0:T(8,128)(2,1)}, u32[]{:S(2)}, u32[]{:S(2)}) collective-permute-start(bf16[128,2048]{1,0:T(8,128)(2,1)S(1)} %add_convert_fusion.27.refs_4_), channel_id=1, source_target_pairs={{0,8},{4,12},{8,0},{12,4},{16,24},{20,28},{24,16},{28,20},{1,9},{5... | collective-permute-start | bytes 1572872 | tf_op jit(solution)/shard_map/ppermute | solution.py:72
  432.6 33.6 %collective-permute-start.38 = (bf16[128,2048]{1,0:T(8,128)(2,1)S(1)}, bf16[128,2048]{1,0:T(8,128)(2,1)}, u32[]{:S(2)}, u32[]{:S(2)}) collective-permute-start(bf16[128,2048]{1,0:T(8,128)(2,1)S(1)} %add_convert_fusion.28.refs_3_), channel_id=1, source_target_pairs={{0,16},{4,20},{8,24},{12,28},{16,0},{20,4},{24,8},{28,12},{1,17},{... | collective-permute-start | bytes 1572872 | tf_op jit(solution)/shard_map/ppermute | solution.py:72
  449.3 29.2 %collective-permute-start.37 = (bf16[2,192,2048]{2,1,0:T(8,128)(2,1)}, bf16[2,192,2048]{2,1,0:T(8,128)(2,1)}, u32[]{:S(2)}, u32[]{:S(2)}) collective-permute-start(bf16[2,192,2048]{2,1,0:T(8,128)(2,1)} %get-tuple-element.168), channel_id=1, source_target_pairs={{0,4},{4,0},{8,12},{12,8},{16,20},{20,16},{24,28},{28,24},{1,5},{5... | collective-permute-start | bytes 4718600 | tf_op jit(solution)/shard_map/ppermute | solution.py:72
  449.5 33.3 %collective-permute-start.40 = (bf16[256,2048]{1,0:T(8,128)(2,1)}, bf16[256,2048]{1,0:T(8,128)(2,1)S(1)}, u32[]{:S(2)}, u32[]{:S(2)}) collective-permute-start(bf16[256,2048]{1,0:T(8,128)(2,1)} %get-tuple-element.166.refs_2_), channel_id=1, source_target_pairs={{0,8},{4,12},{8,0},{12,4},{16,24},{20,28},{24,16},{28,20},{1,9},{5... | collective-permute-start | bytes 3145736 | tf_op jit(solution)/shard_map/ppermute | solution.py:72
  450.6 32.2 %collective-permute-start.41 = (bf16[256,2048]{1,0:T(8,128)(2,1)}, bf16[256,2048]{1,0:T(8,128)(2,1)S(1)}, u32[]{:S(2)}, u32[]{:S(2)}) collective-permute-start(bf16[256,2048]{1,0:T(8,128)(2,1)} %get-tuple-element.182), channel_id=1, source_target_pairs={{0,16},{4,20},{8,24},{12,28},{16,0},{20,4},{24,8},{28,12},{1,17},{... | collective-permute-start | bytes 3145736 | tf_op jit(solution)/shard_map/ppermute | solution.py:72
  452.8 23.6 %all-to-all-start.6 = ((f32[32,2,128]{2,1,0:T(2,128)}), f32[32,2,128]{2,1,0:T(2,128)S(1)}, u32[]{:S(2)}, u32[]{:S(2)}) async-start(f32[32,2,128]{2,1,0:T(2,128)} %fusion.37), calls=%async_computation.6 | async-start | bytes 65536 | tf_op jit(solution)/shard_map/all_to_all | solution.py:860
  465.9 28.2 %collective-permute-start.47 = (bf16[2,192,2048]{2,1,0:T(8,128)(2,1)}, bf16[2,192,2048]{2,1,0:T(8,128)(2,1)}, u32[]{:S(2)}, u32[]{:S(2)}) collective-permute-start(bf16[2,192,2048]{2,1,0:T(8,128)(2,1)} %get-tuple-element.191), channel_id=1, source_target_pairs={{0,4},{4,0},{8,12},{12,8},{16,20},{20,16},{24,28},{28,24},{1,5},{5... | collective-permute-start | bytes 4718600 | tf_op jit(solution)/shard_map/ppermute | solution.py:72
  489.9 40.5 %collective-permute-start.44 = (bf16[128,2048]{1,0:T(8,128)(2,1)}, bf16[128,2048]{1,0:T(8,128)(2,1)S(1)}, u32[]{:S(2)}, u32[]{:S(2)}) collective-permute-start(bf16[128,2048]{1,0:T(8,128)(2,1)} %get-tuple-element.283), channel_id=1, source_target_pairs={{0,1},{1,0},{2,3},{3,2},{4,5},{5,4},{6,7},{7,6},{8,9},{9,8},{10,11... | collective-permute-start | bytes 1572872 | tf_op jit(solution)/shard_map/ppermute | solution.py:75
  493.1 76.7 %collective-permute-start.42 = (bf16[256,2048]{1,0:T(8,128)(2,1)}, bf16[256,2048]{1,0:T(8,128)(2,1)}, u32[]{:S(2)}, u32[]{:S(2)}) collective-permute-start(bf16[256,2048]{1,0:T(8,128)(2,1)} %get-tuple-element.185), channel_id=1, source_target_pairs={{0,8},{4,12},{8,0},{12,4},{16,24},{20,28},{24,16},{28,20},{1,9},{5... | collective-permute-start | bytes 3145736 | tf_op jit(solution)/shard_map/ppermute | solution.py:72
  494.2 75.6 %collective-permute-start.43 = (bf16[256,2048]{1,0:T(8,128)(2,1)}, bf16[256,2048]{1,0:T(8,128)(2,1)}, u32[]{:S(2)}, u32[]{:S(2)}) collective-permute-start(bf16[256,2048]{1,0:T(8,128)(2,1)} %get-tuple-element.186), channel_id=1, source_target_pairs={{0,16},{4,20},{8,24},{12,28},{16,0},{20,4},{24,8},{28,12},{1,17},{... | collective-permute-start | bytes 3145736 | tf_op jit(solution)/shard_map/ppermute | solution.py:72
  506.9 37.9 %collective-permute-start.48 = (bf16[128,2048]{1,0:T(8,128)(2,1)}, bf16[128,2048]{1,0:T(8,128)(2,1)S(1)}, u32[]{:S(2)}, u32[]{:S(2)}) collective-permute-start(bf16[128,2048]{1,0:T(8,128)(2,1)} %get-tuple-element.280), channel_id=1, source_target_pairs={{0,2},{1,3},{2,0},{3,1},{4,6},{5,7},{6,4},{7,5},{8,10},{9,11},{10,... | collective-permute-start | bytes 1572872 | tf_op jit(solution)/shard_map/ppermute | solution.py:75
  511.0 34.5 %collective-permute-start.49 = (bf16[128,2048]{1,0:T(8,128)(2,1)}, bf16[128,2048]{1,0:T(8,128)(2,1)}, u32[]{:S(2)}, u32[]{:S(2)}) collective-permute-start(bf16[128,2048]{1,0:T(8,128)(2,1)} %get-tuple-element.281), channel_id=1, source_target_pairs={{0,3},{1,2},{2,1},{3,0},{4,7},{5,6},{6,5},{7,4},{8,11},{9,10},{10,... | collective-permute-start | bytes 1572872 | tf_op jit(solution)/shard_map/ppermute | solution.py:75
  530.4 43.9 %collective-permute-start.52 = (bf16[256,2048]{1,0:T(8,128)(2,1)}, bf16[256,2048]{1,0:T(8,128)(2,1)S(1)}, u32[]{:S(2)}, u32[]{:S(2)}) collective-permute-start(bf16[256,2048]{1,0:T(8,128)(2,1)} %get-tuple-element.216), channel_id=1, source_target_pairs={{0,8},{4,12},{8,0},{12,4},{16,24},{20,28},{24,16},{28,20},{1,9},{5... | collective-permute-start | bytes 3145736 | tf_op jit(solution)/shard_map/ppermute | solution.py:72
  544.8 29.6 %collective-permute-start.53 = (bf16[256,2048]{1,0:T(8,128)(2,1)}, bf16[256,2048]{1,0:T(8,128)(2,1)S(1)}, u32[]{:S(2)}, u32[]{:S(2)}) collective-permute-start(bf16[256,2048]{1,0:T(8,128)(2,1)} %get-tuple-element.217), channel_id=1, source_target_pairs={{0,16},{4,20},{8,24},{12,28},{16,0},{20,4},{24,8},{28,12},{1,17},{... | collective-permute-start | bytes 3145736 | tf_op jit(solution)/shard_map/ppermute | solution.py:72
  556.5 38.4 %all-to-all-start.7 = ((bf16[4,128,512]{2,1,0:T(8,128)(2,1)}), bf16[4,128,512]{2,1,0:T(8,128)(2,1)S(1)}, u32[]{:S(2)}, u32[]{:S(2)}) async-start(bf16[4,128,512]{2,1,0:T(8,128)(2,1)} %get-tuple-element.208), calls=%async_computation.7 | async-start | bytes 1048576 | tf_op jit(solution)/shard_map/all_to_all | solution.py:78
  614.6 52.5 %collective-permute-start.56 = (bf16[1024,2176]{1,0:T(8,128)(2,1)}, bf16[1024,2176]{1,0:T(8,128)(2,1)}, u32[]{:S(2)}, u32[]{:S(2)}) collective-permute-start(bf16[1024,2176]{1,0:T(8,128)(2,1)} %get-tuple-element.232), channel_id=1, source_target_pairs={{0,4},{4,0},{8,12},{12,8},{16,20},{20,16},{24,28},{28,24},{1,5},{5... | collective-permute-start | bytes 13369352 | tf_op jit(solution)/shard_map/ppermute | solution.py:72
  618.3 24.4 %collective-permute-start.55 = (bf16[128,2048]{1,0:T(8,128)(2,1)S(1)}, bf16[128,2048]{1,0:T(8,128)(2,1)S(1)}, u32[]{:S(2)}, u32[]{:S(2)}) collective-permute-start(bf16[128,2048]{1,0:T(8,128)(2,1)S(1)} %copy-done.53), channel_id=1, source_target_pairs={{0,8},{4,12},{8,0},{12,4},{16,24},{20,28},{24,16},{28,20},{1,9},{5... | collective-permute-start | bytes 1572872 | tf_op jit(solution)/shard_map/ppermute | solution.py:72
  620.3 22.1 %collective-permute-start.54 = (bf16[128,2048]{1,0:T(8,128)(2,1)}, bf16[128,2048]{1,0:T(8,128)(2,1)}, u32[]{:S(2)}, u32[]{:S(2)}) collective-permute-start(bf16[128,2048]{1,0:T(8,128)(2,1)} %add_convert_fusion.15), channel_id=1, source_target_pairs={{0,16},{4,20},{8,24},{12,28},{16,0},{20,4},{24,8},{28,12},{1,17},{... | collective-permute-start | bytes 1572872 | tf_op jit(solution)/shard_map/ppermute | solution.py:72
  648.0 53.7 %all-to-all-start.8 = ((bf16[4,128,2048]{2,1,0:T(8,128)(2,1)}), bf16[4,128,2048]{2,1,0:T(8,128)(2,1)S(1)}, u32[]{:S(2)}, u32[]{:S(2)}) async-start(bf16[4,128,2048]{2,1,0:T(8,128)(2,1)} %maximum_select_fusion.1), calls=%async_computation.8 | async-start | bytes 4194304 | tf_op jit(solution)/shard_map/all_to_all | solution.py:78
  672.3 26.0 %collective-permute-start.58 = (bf16[256,2176]{1,0:T(8,128)(2,1)}, bf16[256,2176]{1,0:T(8,128)(2,1)S(1)}, u32[]{:S(2)}, u32[]{:S(2)}) collective-permute-start(bf16[256,2176]{1,0:T(8,128)(2,1)} %get-tuple-element.255), channel_id=1, source_target_pairs={{0,16},{4,20},{8,24},{12,28},{16,0},{20,4},{24,8},{28,12},{1,17},{... | collective-permute-start | bytes 3342344 | tf_op jit(solution)/shard_map/ppermute | solution.py:72
  673.5 25.7 %collective-permute-start.57 = (bf16[256,2176]{1,0:T(8,128)(2,1)}, bf16[256,2176]{1,0:T(8,128)(2,1)}, u32[]{:S(2)}, u32[]{:S(2)}) collective-permute-start(bf16[256,2176]{1,0:T(8,128)(2,1)} %get-tuple-element.256), channel_id=1, source_target_pairs={{0,8},{4,12},{8,0},{12,4},{16,24},{20,28},{24,16},{28,20},{1,9},{5... | collective-permute-start | bytes 3342344 | tf_op jit(solution)/shard_map/ppermute | solution.py:72
  711.4 53.7 %all-to-all-start.10 = ((bf16[4,128,2048]{2,1,0:T(8,128)(2,1)}), bf16[4,128,2048]{2,1,0:T(8,128)(2,1)S(1)}, u32[]{:S(2)}, u32[]{:S(2)}) async-start(bf16[4,128,2048]{2,1,0:T(8,128)(2,1)} %shard_map.307.refs_4_), calls=%async_computation.10 | async-start | bytes 4194304 | tf_op jit(solution)/shard_map/all_to_all | solution.py:78
  727.7 27.6 %collective-permute-start.61 = (bf16[256,1664]{1,0:T(8,128)(2,1)}, bf16[256,1664]{1,0:T(8,128)(2,1)}, u32[]{:S(2)}, u32[]{:S(2)}) collective-permute-start(bf16[256,1664]{1,0:T(8,128)(2,1)} %get-tuple-element.260), channel_id=1, source_target_pairs={{0,16},{4,20},{8,24},{12,28},{16,0},{20,4},{24,8},{28,12},{1,17},{... | collective-permute-start | bytes 2555912 | tf_op jit(solution)/shard_map/ppermute | solution.py:72
  728.6 26.8 %collective-permute-start.60 = (bf16[256,1664]{1,0:T(8,128)(2,1)}, bf16[256,1664]{1,0:T(8,128)(2,1)}, u32[]{:S(2)}, u32[]{:S(2)}) collective-permute-start(bf16[256,1664]{1,0:T(8,128)(2,1)} %get-tuple-element.261), channel_id=1, source_target_pairs={{0,8},{4,12},{8,0},{12,4},{16,24},{20,28},{24,16},{28,20},{1,9},{5... | collective-permute-start | bytes 2555912 | tf_op jit(solution)/shard_map/ppermute | solution.py:72
  765.1 30.7 %all-to-all-start.12 = ((bf16[4,64,2176]{2,1,0:T(8,128)(2,1)}), bf16[4,64,2176]{2,1,0:T(8,128)(2,1)S(1)}, u32[]{:S(2)}, u32[]{:S(2)}) async-start(bf16[4,64,2176]{2,1,0:T(8,128)(2,1)} %bitcast.127), calls=%async_computation.12 | async-start | bytes 2228224 | tf_op jit(solution)/shard_map/all_to_all | solution.py:78
  795.8 24.5 %all-to-all-start.11 = ((bf16[4,64,1664]{2,1,0:T(8,128)(2,1)}), bf16[4,64,1664]{2,1,0:T(8,128)(2,1)S(1)}, u32[]{:S(2)}, u32[]{:S(2)}) async-start(bf16[4,64,1664]{2,1,0:T(8,128)(2,1)} %bitcast.125), calls=%async_computation.11 | async-start | bytes 1703936 | tf_op jit(solution)/shard_map/all_to_all | solution.py:78
  (129 other events, 955.5 us)
Sparse Core Ops, SparseCore 0:
  149.7 57.2 all-gather.2
